TPU v7x, 256 devices: a whole 4x4x8 slice. The times are simulated.
256 devices in a mesh: row: 16 (over y, z_hi, core), col: 16 (over x, z_lo).
Axes of the slice: x: 4, y: 4, z: 8 (z_hi: 2, z_lo: 4; z = z_hi * 4 + z_lo), core: 2. Of those that a mesh axis runs over, the one named last changes fastest.
Arguments:
- pair: bfloat16 [1024, 1024, 128], P('row', 'col'), may hold values from -6 to 6
- norm_gain: float32 [128], replicated, may hold values from 0.1 to 1.9
- norm_shift: float32 [128], replicated, may hold values from -3 to 3
- w_query: bfloat16 [128, 128], replicated, may hold values from -1 to 1
- w_key: bfloat16 [128, 128], replicated, may hold values from -0.5 to 0.5
- w_value: bfloat16 [128, 128], replicated, may hold values from -0.5 to 0.5
- w_gate: bfloat16 [128, 128], replicated, may hold values from -0.5 to 0.5
- gate_shift: float32 [128], replicated, may hold values from -1 to 1
- w_bias: float32 [128, 4], replicated, may hold values from -30 to 30
- w_out: bfloat16 [128, 128], replicated, may hold values from -1 to 1
- out_shift: float32 [128], replicated, may hold values from -3 to 3
Outputs:
- update: bfloat16 [1024, 1024, 128], P('row', 'col')
All inputs are finite; a program needn't handle non-finite values.
Results may differ from a plain program's by a relative error of at most 0.0015.
The roundings to bfloat16 on the way count: a program that leaves them out, or rounds other values in their place, can miss the bound.
Values may be sent and summed in bfloat16 or wider, within the bound.
No kernel may reach another device: no remote copies, remote signals or barrier semaphores. Data moves between devices by JAX's collectives and lax.ppermute only.
A program may use at most 128 MiB of HBM per device.

v0:
```python
import math

import jax
import jax.numpy as jnp
from jax import lax
from jax.sharding import PartitionSpec as P


def normalize(values, gain, shift):
    values = values.astype(jnp.float32)
    mean = jnp.mean(values, axis=-1, keepdims=True)
    centred = values - mean
    spread = jnp.mean(centred * centred, axis=-1, keepdims=True)
    return (centred * lax.rsqrt(spread + 1e-05) * gain + shift).astype(jnp.bfloat16)


def attend_one(
    pair_row, query_rows, bias, w_query, w_key, w_value, w_gate, gate_shift, w_out, out_shift
):
    heads = bias.shape[0]
    inner = w_query.shape[1]
    depth = inner // heads
    seq_length = pair_row.shape[0]
    query_count = query_rows.shape[0]
    query = (
        jnp.dot(query_rows, w_query, preferred_element_type=jnp.float32) * (1.0 / math.sqrt(depth))
    ).astype(jnp.bfloat16)
    key = jnp.dot(pair_row, w_key, preferred_element_type=jnp.float32).astype(jnp.bfloat16)
    value = jnp.dot(pair_row, w_value, preferred_element_type=jnp.float32).astype(jnp.bfloat16)
    gate = jax.nn.sigmoid(
        jnp.dot(query_rows, w_gate, preferred_element_type=jnp.float32) + gate_shift
    )
    query = query.reshape(query_count, heads, depth)
    key = key.reshape(seq_length, heads, depth)
    value = value.reshape(seq_length, heads, depth)
    scores = jnp.einsum("jhd,khd->hjk", query, key, preferred_element_type=jnp.float32) + bias
    largest = jnp.max(scores, axis=2, keepdims=True)
    raised = jnp.exp(scores - largest)
    weights = (raised / jnp.sum(raised, axis=2, keepdims=True)).astype(jnp.bfloat16)
    attended = jnp.einsum(
        "hjk,khd->jhd", weights, value, preferred_element_type=jnp.float32
    ).reshape(query_count, inner)
    gated = (gate * attended).astype(jnp.bfloat16)
    return (jnp.dot(gated, w_out, preferred_element_type=jnp.float32) + out_shift).astype(
        jnp.bfloat16
    )


def on_device(
    pair,
    norm_gain,
    norm_shift,
    w_query,
    w_key,
    w_value,
    w_gate,
    gate_shift,
    w_bias,
    w_out,
    out_shift,
):
    params = (w_query, w_key, w_value, w_gate, gate_shift, w_out, out_shift)
    col_count = lax.axis_size("col")
    row_count = lax.axis_size("row")
    groups = 1
    while (
        groups * 2 * (groups * 2) <= col_count
        and row_count % (groups * 2) == 0
        and (col_count % (groups * 2) == 0)
    ):
        groups = groups * 2
    across = col_count // groups
    tile_rows, tile_cols, channels = pair.shape
    unit = tile_cols // row_count
    heads = w_bias.shape[1]
    tile_normed = normalize(pair, norm_gain, norm_shift)
    tile_bias = jnp.einsum(
        "jkc,ch->hjk", tile_normed.astype(jnp.float32), w_bias, precision=lax.Precision.HIGHEST
    )
    sorted_bias = tile_bias.reshape(heads, col_count // groups, groups, unit, tile_cols).transpose(
        0, 2, 1, 3, 4
    )
    send_bias = jnp.broadcast_to(
        sorted_bias[:, None], (heads, across, groups, col_count // groups, unit, tile_cols)
    )
    send_bias = send_bias.reshape(heads, col_count, col_count // groups, unit, tile_cols)
    got_bias = lax.all_to_all(send_bias, "col", split_axis=1, concat_axis=4, tiled=True)
    group_bias = lax.all_gather(got_bias, "row", axis=1, tiled=True)
    seq_length = group_bias.shape[4]
    query_bias = group_bias.reshape(heads, seq_length // groups, seq_length)
    part_rows = tile_normed.reshape(across, tile_rows // across, tile_cols, channels)
    send_rows = jnp.broadcast_to(
        part_rows[:, None], (across, groups, tile_rows // across, tile_cols, channels)
    )
    send_rows = send_rows.reshape(col_count, tile_rows // across, tile_cols, channels)
    my_rows = lax.all_to_all(send_rows, "col", split_axis=0, concat_axis=2, tiled=True)[0]
    slot = lax.axis_index("col") % groups

    def row_update(pair_row):
        split_rows = pair_row.reshape(seq_length // (groups * unit), groups, unit, channels)
        picked = lax.dynamic_slice_in_dim(split_rows, slot, 1, 1).reshape(
            seq_length // groups, channels
        )
        return attend_one(pair_row, picked, query_bias, *params)

    update_part = lax.map(row_update, my_rows)
    blocks = update_part.reshape(
        tile_rows // across, col_count, row_count // groups, unit, channels
    )
    back = lax.all_to_all(blocks, "col", split_axis=1, concat_axis=0, tiled=True)
    tile = back.reshape(across, groups, tile_rows // across, row_count // groups, unit, channels)
    return tile.transpose(0, 2, 3, 1, 4, 5).reshape(tile_rows, tile_cols, channels)


def solution(mesh):
    in_specs = (P("row", "col", None), P(), P(), P(), P(), P(), P(), P(), P(), P(), P())
    out_specs = P("row", "col", None)
    return jax.shard_map(
        on_device, mesh=mesh, in_specs=in_specs, out_specs=out_specs, check_vma=False
    )
```

profile of v0, /device:TPU:1, one launch (start us, length us, event | category | flops | bytes accessed | tf_op | source)
XLA Modules:
  0.0 441.6 jit_solution(9916702821150374395)
XLA Ops:
  8.4 2.3 fusion.20
  10.8 2.3 fusion.23
  13.1 2.5 fusion.24
  16.3 18.5 %all_to_all.48 = f32[16,1,4096]{2,1,0:T(1,128)S(1)} all-to-all(f32[16,1,4096]{2,1,0:T(1,128)S(1)} %reshape.82), channel_id=1, replica_groups=mesh['row'=16,'col'=16] {'col'}, dimensions={0} | all-to-all | bytes 524288 | tf_op jit(solution)/shard_map/all_to_all | solution.py:87
  34.8 3.0 broadcast_in_dim.15
  37.8 4.5 %all-to-all-start = ((bf16[16,16,64,128]{3,2,1,0:T(8,128)(2,1)}), bf16[16,16,64,128]{3,2,1,0:T(8,128)(2,1)}, u32[]{:S(2)}, u32[]{:S(2)}) async-start(bf16[16,16,64,128]{3,2,1,0:T(8,128)(2,1)} %bitcast.111), calls=%async_computation | async-start | bytes 8388608 | tf_op jit(solution)/shard_map/all_to_all | solution.py:96
  46.0 119.0 %all-to-all-done = bf16[16,16,64,128]{3,2,1,0:T(8,128)(2,1)} async-done(((bf16[16,16,64,128]{3,2,1,0:T(8,128)(2,1)}), bf16[16,16,64,128]{3,2,1,0:T(8,128)(2,1)}, u32[]{:S(2)}, u32[]{:S(2)}) %all-to-all-start) | async-done | bytes 4194336 | tf_op jit(solution)/shard_map/all_to_all | solution.py:96
  165.1 5.5 %copy.51 = bf16[16,16,64,128]{3,2,0,1:T(8,128)(2,1)} copy(bf16[16,16,64,128]{3,2,1,0:T(8,128)(2,1)} %all-to-all-done) | data formatting | bytes 8388608 | tf_op jit(solution)/shard_map/all_to_all | solution.py:96
  170.6 6.1 %copy.54 = f32[4,16,4,4,1024]{4,0,3,2,1:T(4,128)S(1)} copy(f32[4,16,4,4,1024]{4,3,2,0,1:T(4,128)} %all-gather.2.cloned.1.call-done) | data formatting | bytes 8388608 | tf_op jit(solution)/shard_map/all_gather | solution.py:88
  176.8 4.4 copy.55
  181.2 220.3 %while.12 = (s32[]{:T(128)}, bf16[16,256,128]{2,1,0:T(8,128)(2,1)S(1)}, bf16[16,1024,128]{2,1,0:T(8,128)(2,1)}, s32[]{:T(128)}, bf16[128,128]{1,0:T(8,128)(2,1)S...) while((s32[]{:T(128)}, ...), condition=%wide.region_5.6_spmd, body=%wide.region_2.5_spmd.sunk | while | flops 233376768 | bytes 36807844 | solution.py:106
  183.0 2.9 convolution_add_fusion.4
  185.9 2.0 copy-done.1
  189.2 5.6 %fusion.74 = f32[4,32,256]{2,1,0:T(8,128)S(1)} fusion(bf16[1024,4,32]{0,2,1:T(8,128)(2,1)S(1)} %bitcast.116, f32[4,256]{1,0:T(4,128)S(1)} %fusion.73, f32[4,256,1024]{2,1,0:T(8,128)} %copy-done.1), kind=kOutput, calls=%fused_computation.4.clone.1 | convolution fusion | flops 70256640 | bytes 4591616 | tf_op jit(solution)/shard_map/while/body/eval_jaxpr/hjk,khd->jhd/dot_general | solution.py:40
  196.7 2.9 convolution_add_fusion.4
  202.9 5.6 %fusion.74 = f32[4,32,256]{2,1,0:T(8,128)S(1)} fusion(bf16[1024,4,32]{0,2,1:T(8,128)(2,1)S(1)} %bitcast.116, f32[4,256]{1,0:T(4,128)S(1)} %fusion.73, f32[4,256,1024]{2,1,0:T(8,128)} %copy-done.1), kind=kOutput, calls=%fused_computation.4.clone.1 | convolution fusion | flops 70256640 | bytes 4591616 | tf_op jit(solution)/shard_map/while/body/eval_jaxpr/hjk,khd->jhd/dot_general | solution.py:40
  210.5 2.9 convolution_add_fusion.4
  216.7 5.6 %fusion.74 = f32[4,32,256]{2,1,0:T(8,128)S(1)} fusion(bf16[1024,4,32]{0,2,1:T(8,128)(2,1)S(1)} %bitcast.116, f32[4,256]{1,0:T(4,128)S(1)} %fusion.73, f32[4,256,1024]{2,1,0:T(8,128)} %copy-done.1), kind=kOutput, calls=%fused_computation.4.clone.1 | convolution fusion | flops 70256640 | bytes 4591616 | tf_op jit(solution)/shard_map/while/body/eval_jaxpr/hjk,khd->jhd/dot_general | solution.py:40
  224.2 2.9 convolution_add_fusion.4
  227.2 2.0 copy-done.1
  230.5 5.6 %fusion.74 = f32[4,32,256]{2,1,0:T(8,128)S(1)} fusion(bf16[1024,4,32]{0,2,1:T(8,128)(2,1)S(1)} %bitcast.116, f32[4,256]{1,0:T(4,128)S(1)} %fusion.73, f32[4,256,1024]{2,1,0:T(8,128)} %copy-done.1), kind=kOutput, calls=%fused_computation.4.clone.1 | convolution fusion | flops 70256640 | bytes 4591616 | tf_op jit(solution)/shard_map/while/body/eval_jaxpr/hjk,khd->jhd/dot_general | solution.py:40
  238.0 2.9 convolution_add_fusion.4
  240.9 2.0 copy-done.1
  244.2 5.6 %fusion.74 = f32[4,32,256]{2,1,0:T(8,128)S(1)} fusion(bf16[1024,4,32]{0,2,1:T(8,128)(2,1)S(1)} %bitcast.116, f32[4,256]{1,0:T(4,128)S(1)} %fusion.73, f32[4,256,1024]{2,1,0:T(8,128)} %copy-done.1), kind=kOutput, calls=%fused_computation.4.clone.1 | convolution fusion | flops 70256640 | bytes 4591616 | tf_op jit(solution)/shard_map/while/body/eval_jaxpr/hjk,khd->jhd/dot_general | solution.py:40
  251.8 2.9 convolution_add_fusion.4
  254.7 2.0 copy-done.1
  258.0 5.6 %fusion.74 = f32[4,32,256]{2,1,0:T(8,128)S(1)} fusion(bf16[1024,4,32]{0,2,1:T(8,128)(2,1)S(1)} %bitcast.116, f32[4,256]{1,0:T(4,128)S(1)} %fusion.73, f32[4,256,1024]{2,1,0:T(8,128)} %copy-done.1), kind=kOutput, calls=%fused_computation.4.clone.1 | convolution fusion | flops 70256640 | bytes 4591616 | tf_op jit(solution)/shard_map/while/body/eval_jaxpr/hjk,khd->jhd/dot_general | solution.py:40
  265.5 2.9 convolution_add_fusion.4
  271.7 5.6 %fusion.74 = f32[4,32,256]{2,1,0:T(8,128)S(1)} fusion(bf16[1024,4,32]{0,2,1:T(8,128)(2,1)S(1)} %bitcast.116, f32[4,256]{1,0:T(4,128)S(1)} %fusion.73, f32[4,256,1024]{2,1,0:T(8,128)} %copy-done.1), kind=kOutput, calls=%fused_computation.4.clone.1 | convolution fusion | flops 70256640 | bytes 4591616 | tf_op jit(solution)/shard_map/while/body/eval_jaxpr/hjk,khd->jhd/dot_general | solution.py:40
  279.3 2.9 convolution_add_fusion.4
  285.5 5.6 %fusion.74 = f32[4,32,256]{2,1,0:T(8,128)S(1)} fusion(bf16[1024,4,32]{0,2,1:T(8,128)(2,1)S(1)} %bitcast.116, f32[4,256]{1,0:T(4,128)S(1)} %fusion.73, f32[4,256,1024]{2,1,0:T(8,128)} %copy-done.1), kind=kOutput, calls=%fused_computation.4.clone.1 | convolution fusion | flops 70256640 | bytes 4591616 | tf_op jit(solution)/shard_map/while/body/eval_jaxpr/hjk,khd->jhd/dot_general | solution.py:40
  293.0 2.9 convolution_add_fusion.4
  299.2 5.6 %fusion.74 = f32[4,32,256]{2,1,0:T(8,128)S(1)} fusion(bf16[1024,4,32]{0,2,1:T(8,128)(2,1)S(1)} %bitcast.116, f32[4,256]{1,0:T(4,128)S(1)} %fusion.73, f32[4,256,1024]{2,1,0:T(8,128)} %copy-done.1), kind=kOutput, calls=%fused_computation.4.clone.1 | convolution fusion | flops 70256640 | bytes 4591616 | tf_op jit(solution)/shard_map/while/body/eval_jaxpr/hjk,khd->jhd/dot_general | solution.py:40
  306.8 2.9 convolution_add_fusion.4
  313.0 5.6 %fusion.74 = f32[4,32,256]{2,1,0:T(8,128)S(1)} fusion(bf16[1024,4,32]{0,2,1:T(8,128)(2,1)S(1)} %bitcast.116, f32[4,256]{1,0:T(4,128)S(1)} %fusion.73, f32[4,256,1024]{2,1,0:T(8,128)} %copy-done.1), kind=kOutput, calls=%fused_computation.4.clone.1 | convolution fusion | flops 70256640 | bytes 4591616 | tf_op jit(solution)/shard_map/while/body/eval_jaxpr/hjk,khd->jhd/dot_general | solution.py:40
  320.5 2.9 convolution_add_fusion.4
  326.8 5.6 %fusion.74 = f32[4,32,256]{2,1,0:T(8,128)S(1)} fusion(bf16[1024,4,32]{0,2,1:T(8,128)(2,1)S(1)} %bitcast.116, f32[4,256]{1,0:T(4,128)S(1)} %fusion.73, f32[4,256,1024]{2,1,0:T(8,128)} %copy-done.1), kind=kOutput, calls=%fused_computation.4.clone.1 | convolution fusion | flops 70256640 | bytes 4591616 | tf_op jit(solution)/shard_map/while/body/eval_jaxpr/hjk,khd->jhd/dot_general | solution.py:40
  334.3 2.9 convolution_add_fusion.4
  340.5 5.6 %fusion.74 = f32[4,32,256]{2,1,0:T(8,128)S(1)} fusion(bf16[1024,4,32]{0,2,1:T(8,128)(2,1)S(1)} %bitcast.116, f32[4,256]{1,0:T(4,128)S(1)} %fusion.73, f32[4,256,1024]{2,1,0:T(8,128)} %copy-done.1), kind=kOutput, calls=%fused_computation.4.clone.1 | convolution fusion | flops 70256640 | bytes 4591616 | tf_op jit(solution)/shard_map/while/body/eval_jaxpr/hjk,khd->jhd/dot_general | solution.py:40
  348.0 2.9 convolution_add_fusion.4
  354.3 5.6 %fusion.74 = f32[4,32,256]{2,1,0:T(8,128)S(1)} fusion(bf16[1024,4,32]{0,2,1:T(8,128)(2,1)S(1)} %bitcast.116, f32[4,256]{1,0:T(4,128)S(1)} %fusion.73, f32[4,256,1024]{2,1,0:T(8,128)} %copy-done.1), kind=kOutput, calls=%fused_computation.4.clone.1 | convolution fusion | flops 70256640 | bytes 4591616 | tf_op jit(solution)/shard_map/while/body/eval_jaxpr/hjk,khd->jhd/dot_general | solution.py:40
  361.8 2.9 convolution_add_fusion.4
  368.0 5.6 %fusion.74 = f32[4,32,256]{2,1,0:T(8,128)S(1)} fusion(bf16[1024,4,32]{0,2,1:T(8,128)(2,1)S(1)} %bitcast.116, f32[4,256]{1,0:T(4,128)S(1)} %fusion.73, f32[4,256,1024]{2,1,0:T(8,128)} %copy-done.1), kind=kOutput, calls=%fused_computation.4.clone.1 | convolution fusion | flops 70256640 | bytes 4591616 | tf_op jit(solution)/shard_map/while/body/eval_jaxpr/hjk,khd->jhd/dot_general | solution.py:40
  375.6 2.9 convolution_add_fusion.4
  381.8 5.6 %fusion.74 = f32[4,32,256]{2,1,0:T(8,128)S(1)} fusion(bf16[1024,4,32]{0,2,1:T(8,128)(2,1)S(1)} %bitcast.116, f32[4,256]{1,0:T(4,128)S(1)} %fusion.73, f32[4,256,1024]{2,1,0:T(8,128)} %copy-done.1), kind=kOutput, calls=%fused_computation.4.clone.1 | convolution fusion | flops 70256640 | bytes 4591616 | tf_op jit(solution)/shard_map/while/body/eval_jaxpr/hjk,khd->jhd/dot_general | solution.py:40
  389.3 2.9 convolution_add_fusion.4
  395.5 5.6 %fusion.74 = f32[4,32,256]{2,1,0:T(8,128)S(1)} fusion(bf16[1024,4,32]{0,2,1:T(8,128)(2,1)S(1)} %bitcast.116, f32[4,256]{1,0:T(4,128)S(1)} %fusion.73, f32[4,256,1024]{2,1,0:T(8,128)} %copy-done.1), kind=kOutput, calls=%fused_computation.4.clone.1 | convolution fusion | flops 70256640 | bytes 4591616 | tf_op jit(solution)/shard_map/while/body/eval_jaxpr/hjk,khd->jhd/dot_general | solution.py:40
  402.2 30.5 %all_to_all.49 = bf16[16,16,4,4,128]{4,0,3,2,1:T(8,128)(2,1)S(1)} all-to-all(bf16[16,16,4,4,128]{4,0,3,2,1:T(8,128)(2,1)S(1)} %bitcast.119), channel_id=1, replica_groups=mesh['row'=16,'col'=16] {'col'}, dimensions={1} | all-to-all | bytes 2097152 | tf_op jit(solution)/shard_map/all_to_all | solution.py:110
  (191 shorter events, 83.9 us)
Async XLA Ops:
  6.5 6.6 %copy-start = (f32[128,4]{0,1:T(4,128)S(1)}, f32[128,4]{0,1:T(4,128)}, u32[]{:S(2)}) copy-start(f32[128,4]{0,1:T(4,128)} %param.21) | copy-start | bytes 6148
  37.8 127.3 %all-to-all-start = ((bf16[16,16,64,128]{3,2,1,0:T(8,128)(2,1)}), bf16[16,16,64,128]{3,2,1,0:T(8,128)(2,1)}, u32[]{:S(2)}, u32[]{:S(2)}) async-start(bf16[16,16,64,128]{3,2,1,0:T(8,128)(2,1)} %bitcast.111), calls=%async_computation | async-start | bytes 8388608 | tf_op jit(solution)/shard_map/all_to_all | solution.py:96
  42.3 128.2 %all-gather.2.cloned.1.call-start = ((), (), s32[]{:S(2)}) async-start(), calls=%async_computation.3 | async-start | bytes 4456448 | tf_op jit(solution)/shard_map/all_gather | solution.py:88
  176.7 4.5 %copy-start.2 = (bf16[128,128]{1,0:T(8,128)(2,1)S(1)}, bf16[128,128]{1,0:T(8,128)(2,1)}, u32[]{:S(2)}) copy-start(bf16[128,128]{1,0:T(8,128)(2,1)} %param.18) | copy-start | bytes 98308
  176.7 4.5 %copy-start.3 = (bf16[128,128]{1,0:T(8,128)(2,1)S(1)}, bf16[128,128]{1,0:T(8,128)(2,1)}, u32[]{:S(2)}) copy-start(bf16[128,128]{1,0:T(8,128)(2,1)} %param.16) | copy-start | bytes 98308
  176.7 4.5 %copy-start.4 = (bf16[128,128]{1,0:T(8,128)(2,1)S(1)}, bf16[128,128]{1,0:T(8,128)(2,1)}, u32[]{:S(2)}) copy-start(bf16[128,128]{1,0:T(8,128)(2,1)} %param.17) | copy-start | bytes 98308
  176.7 4.5 %copy-start.5 = (bf16[128,128]{1,0:T(8,128)(2,1)S(1)}, bf16[128,128]{1,0:T(8,128)(2,1)}, u32[]{:S(2)}) copy-start(bf16[128,128]{1,0:T(8,128)(2,1)} %param.19) | copy-start | bytes 98308
  176.8 4.5 %copy-start.6 = (bf16[128,128]{1,0:T(8,128)(2,1)S(1)}, bf16[128,128]{1,0:T(8,128)(2,1)}, u32[]{:S(2)}) copy-start(bf16[128,128]{1,0:T(8,128)(2,1)} %param.22) | copy-start | bytes 98308
  176.8 4.5 %copy-start.7 = (f32[128]{0:T(128)S(1)}, f32[128]{0:T(128)}, u32[]{:S(2)}) copy-start(f32[128]{0:T(128)} %param.20) | copy-start | bytes 1540
  176.8 4.4 %copy-start.8 = (f32[128]{0:T(128)S(1)}, f32[128]{0:T(128)}, u32[]{:S(2)}) copy-start(f32[128]{0:T(128)} %param.23) | copy-start | bytes 1540
  185.9 2.0 copy-start.1
  199.7 2.0 copy-start.1
  213.4 2.0 copy-start.1
  227.2 2.0 copy-start.1
  240.9 2.0 copy-start.1
  254.7 2.0 copy-start.1
  268.4 2.0 copy-start.1
  282.2 2.0 copy-start.1
  296.0 2.0 copy-start.1
  309.7 2.0 copy-start.1
  323.5 2.0 copy-start.1
  337.2 2.0 copy-start.1
  351.0 2.0 copy-start.1
  364.7 2.0 copy-start.1
  378.5 2.0 copy-start.1
  392.2 2.0 copy-start.1
Sparse Core Ops, SparseCore 0:
  46.1 117.3 all-gather.1
where the time goes:
time: 443 us; the launch traced here: 442 us
  matrix products  155 us (35%)
  waiting for transfers between devices  119 us (27%)
  local copies, waits for them, and re-layouts  73.9 us (17%)
  blocking collectives  49.1 us (11%)
  other arithmetic  24.4 us (6%)
  between operations  13.6 us (3%)
  starting transfers between devices  4.75 us (1%)
    all_to_all x1, waiting for transfers between devices, on_device(): lax.all_to_all(send_rows, 'col', split_axis=0, concat_axis=2, tiled=True)[0]  119 us
    dot_general x16, matrix products, attend_one(): jnp.einsum('hjk,khd->jhd', weights, value, preferred_element_type=jnp.flo...  89.1 us
    dot_general x16, matrix products, attend_one(): jnp.einsum('jhd,khd->hjk', query, key, preferred_element_type=jnp.float32)  46.8 us
    while x32, local copies, waits for them, and re-layouts  31.5 us
    all_to_all x1, blocking collectives, on_device(): lax.all_to_all(blocks, 'col', split_axis=1, concat_axis=0, tiled=True)  30.5 us
    all_to_all x1, blocking collectives, on_device(): lax.all_to_all(send_bias, 'col', split_axis=1, concat_axis=4, tiled=True)  18.5 us
    sub x16, other arithmetic, attend_one(): raised = jnp.exp(scores - largest)  16.6 us
    dynamic_slice x16, local copies, waits for them, and re-layouts, on_device(): update_part = lax.map(row_update, my_rows)  15.5 us
  transfers between devices with their start and end apart: 2, of which 1 were waited for; matrix products, arithmetic and copies ran while one was open for 2% of the time, Pallas kernels for 0%

commit v1 on v0

v1 whole, which is shorter than its diff:
```python
import functools, math
import jax, jax.numpy as jnp
from jax import lax
from jax.sharding import PartitionSpec as P
from jax.experimental import pallas as pl
from jax.experimental.pallas import tpu as pltpu

F32 = jnp.float32
BF = jnp.bfloat16
CHUNKS = 2
def dot_t(a,b):
    return lax.dot_general(a,b,(((1,),(1,)),((),())),preferred_element_type=F32)

def attend_kernel(depth, at, x0,x1,x2,x3, b00,b01,b10,b11,b20,b21,b30,b31, wk,wvT,wqT,wgT,gsh,wo,osh, out, k_ref, v_ref, s_ref):
    xs=(x0,x1,x2,x3)
    bias=((b00,b01),(b10,b11),(b20,b21),(b30,b31))
    y=at[0]; z=at[1]; zl=at[2]; core=at[3]
    pieces=[]
    for b in range(2):
        half=lax.rem(core+b,2)
        for s in range(4):
            for t in range(4):
                pieces.append(xs[t][s,0,pl.ds(pl.multiple_of(half*32,32),32),:])
    xk=jnp.concatenate(pieces,axis=0)
    k_ref[...]=jnp.dot(xk,wk[...],preferred_element_type=F32).astype(BF)
    v_ref[...]=dot_t(wvT[...],xk).astype(BF)
    slot=[lax.rem(zl+4-qb,4) for qb in range(4)]
    xq=jnp.concatenate([x0[slot[qb],0] for qb in range(4)],axis=0)
    qT=(dot_t(wqT[...],xq)*(1.0/math.sqrt(depth))).astype(BF)
    gate=jax.nn.sigmoid(dot_t(wgT[...],xq)+gsh[...])
    rows=lax.broadcasted_iota(jnp.int32,qT.shape,0)//depth
    zslot=[[lax.rem(z+8-(zh*4+lax.rem(zl+4-s,4)),8) for s in range(4)] for zh in range(2)]
    parts=[]
    for a in range(4):
        h=lax.rem(y+4-a,4)
        qm=jnp.where(rows==h,qT,jnp.zeros_like(qT))
        top=None
        for b in range(2):
            for s in range(4):
                c=b*4+s
                sc=jnp.dot(k_ref[c*128:(c+1)*128,:],qm,preferred_element_type=F32)
                sc=sc+jnp.concatenate([bias[a][b][zslot[zh][s]] for zh in range(2)],axis=1)
                s_ref[a%2,c]=sc
                m=jnp.max(sc.reshape(16,8,256),axis=0)
                top=m if top is None else jnp.maximum(top,m)
        top=jnp.max(top,axis=0,keepdims=True)
        tot=None
        for c in range(8):
            e=jnp.exp(s_ref[a%2,c]-top)
            s_ref[a%2,c]=e
            m=jnp.sum(e.reshape(16,8,256),axis=0)
            tot=m if tot is None else tot+m
        inv=1.0/jnp.sum(tot,axis=0,keepdims=True)
        acc=None
        vh=v_ref[pl.ds(pl.multiple_of(h*depth,depth),depth),:]
        w=[(s_ref[a%2,c]*inv).astype(BF) for c in range(8)]
        acc=jnp.dot(vh,jnp.concatenate(w,axis=0),preferred_element_type=F32)
        parts.append((h,acc))
    for h,acc in parts:
        s_ref[0,0,pl.ds(pl.multiple_of(h*depth,depth),depth),:]=acc
    gated=(gate*s_ref[0,0]).astype(BF)
    upd=lax.dot_general(gated,wo[...],(((0,),(0,)),((),())),preferred_element_type=F32)+osh[...]
    upd=upd.astype(BF)
    for qb in range(4):
        out[slot[qb],0]=upd[qb*64:(qb+1)*64]

def attend(at, xs, biases, wk,wvT,wqT,wgT,gsh,wo,osh, kernel=attend_kernel, extra=()):
    R=xs[0].shape[1]
    xspec=pl.BlockSpec((4,1,64,128),lambda i,at:(0,i,0,0))
    bspec=pl.BlockSpec((8,128,128),lambda i,at:(0,0,0))
    full=lambda a: pl.BlockSpec(a.shape,lambda i,at:(0,)*a.ndim)
    ws=(wk,wvT,wqT,wgT,gsh,wo,osh)
    return pl.pallas_call(functools.partial(kernel,32),
        out_shape=jax.ShapeDtypeStruct((4,R,64,128),BF),
        grid_spec=pltpu.PrefetchScalarGridSpec(num_scalar_prefetch=1,grid=(R,),
            in_specs=[xspec]*4+[bspec]*8+[full(w) for w in ws],
            out_specs=xspec,
            scratch_shapes=[pltpu.VMEM((1024,128),BF),pltpu.VMEM((128,1024),BF),pltpu.VMEM((2,8,128,256),F32),*extra]),
        compiler_params=pltpu.CompilerParams(vmem_limit_bytes=48<<20,dimension_semantics=("arbitrary",)),
        cost_estimate=pl.CostEstimate(flops=R*300_000_000,bytes_accessed=R*(1<<20),transcendentals=R*(1<<20)),
    )(at,*xs,*[b for p in biases for b in p],*ws)


def normalize(values, gain, shift):
    values = values.astype(F32)
    mean = jnp.mean(values, axis=-1, keepdims=True)
    centred = values - mean
    spread = jnp.mean(centred * centred, axis=-1, keepdims=True)
    return (centred * lax.rsqrt(spread + 1e-05) * gain + shift).astype(BF)


AXES = ("row", "col")


def move(array, to):
    pairs = []
    for source in range(256):
        row, col = divmod(source, 16)
        y, zh, core = row // 4, row // 2 % 2, row % 2
        x, zl = divmod(col, 4)
        y, z, core, x = to(y, zh * 4 + zl, core, x)
        y, z, x = y % 4, z % 8, x % 4
        target = ((y * 2 + z // 4) * 2 + core) * 16 + x * 4 + z % 4
        pairs.append((source, target))
    return lax.ppermute(array, AXES, pairs)


def turn(z, step):
    return z // 4 * 4 + (z + step) % 4


def on_device(
    pair,
    norm_gain,
    norm_shift,
    w_query,
    w_key,
    w_value,
    w_gate,
    gate_shift,
    w_bias,
    w_out,
    out_shift,
):
    row, col = lax.axis_index("row"), lax.axis_index("col")
    y, zh, core = row // 4, row // 2 % 2, row % 2
    x, zl = col // 4, col % 4
    z = zh * 4 + zl
    place = jnp.stack([y, z, zl, core]).astype(jnp.int32)
    normed = normalize(pair, norm_gain, norm_shift)
    with jax.named_scope("bias"):
        tile = jnp.einsum(
            "jkc,ch->hkj", normed.astype(F32), w_bias, precision=lax.Precision.HIGHEST
        )
        kept = lax.dynamic_slice_in_dim(tile, core * 32, 32, 1)
        sent = lax.dynamic_slice_in_dim(tile, (1 - core) * 32, 32, 1)
        got = move(sent, lambda y, z, core, x: (y, z, 1 - core, x))
        tile = jnp.where(
            core == 0, jnp.concatenate([kept, got], 2), jnp.concatenate([got, kept], 2)
        )
        rounds = []
        for step in range(4):
            part = lax.dynamic_index_in_dim(tile, (x + step) % 4, 0, keepdims=False)
            rounds.append(move(part, lambda y, z, core, x: (x + step, z, core, y)))
        rounds = jnp.stack(rounds + rounds[:3])
        block = lax.dynamic_slice_in_dim(rounds, (y - x) % 4, 4, 0).reshape(128, 128)
        along_z = [block]
        for step in range(1, 8):
            along_z.append(move(block, lambda y, z, core, x: (y, z + step, core, x)))
        along_z = jnp.stack(along_z)
        biases = []
        for step in range(4):
            here = (
                along_z
                if step == 0
                else move(along_z, lambda y, z, core, x: (y + step, z, core, x))
            )
            biases.append((here, move(here, lambda y, z, core, x: (y, z, 1 - core, x))))
    count = 16 // CHUNKS
    result = jnp.zeros(pair.shape, BF)
    for chunk in range(CHUNKS):
        with jax.named_scope("rows"):
            pieces = []
            for step in range(4):
                part = lax.dynamic_slice_in_dim(
                    normed, (zl + step) % 4 * 16 + chunk * count, count, 0
                )
                if step:
                    part = move(part, lambda y, z, core, x: (y, turn(z, step), core, x))
                pieces.append(part)
            held = jnp.stack(pieces)
            rows = [held]
            for step in range(1, 4):
                rows.append(move(held, lambda y, z, core, x: (y, z, core, x + step)))
        with jax.named_scope("attention"):
            part = attend(
                place,
                rows,
                biases,
                w_key,
                w_value.T,
                w_query.T,
                w_gate.T,
                gate_shift[:, None],
                w_out,
                out_shift[None],
            )
        with jax.named_scope("update"):
            for step in range(4):
                back = part[step]
                if step:
                    back = move(back, lambda y, z, core, x: (y, turn(z, -step), core, x))
                result = lax.dynamic_update_slice_in_dim(
                    result, back, (zl + step) % 4 * 16 + chunk * count, 0
                )
    return result


def solution(mesh):
    in_specs = (P("row", "col", None), P(), P(), P(), P(), P(), P(), P(), P(), P(), P())
    out_specs = P("row", "col", None)
    return jax.shard_map(
        on_device, mesh=mesh, in_specs=in_specs, out_specs=out_specs, check_vma=False
    )
```

time: 443 us -> 211 us (0.48)
  matrix products: 155 us -> 2.53 us
  starting transfers between devices: 4.75 us -> 75 us
  local copies, waits for them, and re-layouts: 73.9 us -> 6.2 us
  Pallas kernels: 0 us -> 51.3 us
  waiting for transfers between devices: 119 us -> 69.5 us
  blocking collectives: 49.1 us -> 0 us
  other arithmetic: 24.4 us -> 5.93 us
  between operations: 13.6 us -> 0.47 us
    dot_general x97 -> x1, matrix products: 155 us -> 2.53 us  [on_device(): jnp.einsum('jkc,ch->hkj', normed.astype(F32), w_bias, precision=lax.Preci...]
    all_to_all x1 -> x0, waiting for transfers between devices: 119 us -> none  [on_device(): lax.all_to_all(send_rows, 'col', split_axis=0, concat_axis=2, tiled=True)[0]]
    ppermute x0 -> x37, starting transfers between devices: none -> 75 us  [move(): return lax.ppermute(array, AXES, pairs)]
    ppermute x0 -> x37, waiting for transfers between devices: none -> 69.5 us  [move(): return lax.ppermute(array, AXES, pairs)]
    pallas_call x0 -> x2, Pallas kernels: none -> 51.3 us  [attend(): pl.pallas_call(functools.partial(kernel, 32), out_shape=jax.ShapeDtypeStr...]
    all_to_all x2 -> x0, blocking collectives: 49.1 us -> none  [the longest x1 30.5 us: on_device(): lax.all_to_all(blocks, 'col', split_axis=1, concat_axis=0, tiled=True)]
    while x34 -> x0, local copies, waits for them, and re-layouts: 36.6 us -> none
    sub x16 -> x0, other arithmetic: 16.6 us -> none  [attend_one(): raised = jnp.exp(scores - largest)]
  transfers between devices with their start and end apart: 2 -> 37, of which waited for: 1 -> 15; matrix products, arithmetic and copies ran while one was open for 2% -> 2% of each run, Pallas kernels for 0% -> 24%
where the time goes in v1:
time: 211 us
  starting transfers between devices  75 us (36%)
  waiting for transfers between devices  69.5 us (33%)
  Pallas kernels  51.3 us (24%)
  local copies, waits for them, and re-layouts  6.2 us (3%)
  other arithmetic  5.93 us (3%)
  matrix products  2.53 us (1%)
    ppermute x37, starting transfers between devices, move(): return lax.ppermute(array, AXES, pairs)  75 us
    ppermute x37, waiting for transfers between devices, move(): return lax.ppermute(array, AXES, pairs)  69.5 us
    pallas_call x2, Pallas kernels, attend(): pl.pallas_call(functools.partial(kernel, 32), out_shape=jax.ShapeDtypeStr...  51.3 us
    unnamed x42, local copies, waits for them, and re-layouts  4.45 us
  transfers between devices with their start and end apart: 37, of which 15 were waited for; matrix products, arithmetic and copies ran while one was open for 2% of the time, Pallas kernels for 24%

profile of v1, /device:TPU:1, one launch (start us, length us, event | category | flops | bytes accessed | tf_op | source)
XLA Modules:
  0.0 210.9 jit_solution(2295049175268562335)
XLA Ops:
  0.0 1.9 convert_reduce_fusion
  2.0 1.3 fusion.2
  3.3 1.3 fusion.5
  4.6 2.5 %fusion.8 = f32[64,64,4]{1,2,0:T(4,128)S(1)} fusion(bf16[64,64,128]{2,1,0:T(8,128)(2,1)S(1)} %fusion.5, f32[128,4]{0,1:T(4,128)S(1)} %copy-done), kind=kOutput, calls=%fused_computation.59 | convolution fusion | flops 25165824 | bytes 1116160 | tf_op jit(solution)/shard_map/bias/jkc,ch->hkj/dot_general | solution.py:132
  7.4 3.3 %collective-permute-start.6 = (f32[4,32,64]{1,0,2:T(4,128)S(1)}, f32[4,32,64]{1,0,2:T(4,128)S(1)}, u32[]{:S(2)}, u32[]{:S(2)}) collective-permute-start(f32[4,32,64]{1,0,2:T(4,128)S(1)} %get-tuple-element.20), channel_id=1, source_target_pairs={{0,16},{1,17},{2,18},{3,19},{4,20},{5,21},{6,22},{7,23},{8,24},{9,... | collective-permute-start | bytes 98312 | tf_op jit(solution)/shard_map/bias/ppermute | solution.py:105
  10.8 0.9 collective-permute-done.6
  12.8 2.9 %collective-permute-start.29 = (bf16[8,64,128]{2,1,0:T(8,128)(2,1)S(1)}, bf16[8,64,128]{2,1,0:T(8,128)(2,1)}, u32[]{:S(2)}, u32[]{:S(2)}) collective-permute-start(bf16[8,64,128]{2,1,0:T(8,128)(2,1)S(1)} %get-tuple-element.7), channel_id=1, source_target_pairs={{0,2},{1,3},{2,0},{3,1},{4,6},{5,7},{6,4},{7,5},{8,10},{9,11},{10,... | collective-permute-start | bytes 393224 | tf_op jit(solution)/shard_map/rows/ppermute | solution.py:105
  15.7 0.7 collective-permute-start.30
  16.4 0.7 collective-permute-start
  17.1 3.6 %collective-permute-start.8 = (f32[32,128]{1,0:T(8,128)S(1)}, f32[32,128]{1,0:T(8,128)S(1)}, u32[]{:S(2)}, u32[]{:S(2)}) collective-permute-start(f32[32,128]{1,0:T(8,128)S(1)} %get-tuple-element.23), channel_id=1, source_target_pairs={{0,64},{1,65},{2,66},{3,67},{4,128},{5,129},{6,130},{7,131},{8,192... | collective-permute-start | bytes 49160 | tf_op jit(solution)/shard_map/bias/ppermute | solution.py:105
  20.8 4.1 %collective-permute-done.8 = f32[32,128]{1,0:T(8,128)S(1)} collective-permute-done((f32[32,128]{1,0:T(8,128)S(1)}, f32[32,128]{1,0:T(8,128)S(1)}, u32[]{:S(2)}, u32[]{:S(2)}) %collective-permute-start.8) | collective-permute-done | bytes 16416 | tf_op jit(solution)/shard_map/bias/ppermute | solution.py:105
  24.9 3.9 %collective-permute-start.9 = (f32[32,128]{1,0:T(8,128)S(1)}, f32[32,128]{1,0:T(8,128)S(1)}, u32[]{:S(2)}, u32[]{:S(2)}) collective-permute-start(f32[32,128]{1,0:T(8,128)S(1)} %get-tuple-element.22), channel_id=1, source_target_pairs={{0,128},{1,129},{2,130},{3,131},{4,192},{5,193},{6,194},{7,195},{8... | collective-permute-start | bytes 49160 | tf_op jit(solution)/shard_map/bias/ppermute | solution.py:105
  28.8 1.3 collective-permute-done.9
  30.1 4.1 %collective-permute-start.10 = (f32[32,128]{1,0:T(8,128)S(1)}, f32[32,128]{1,0:T(8,128)S(1)}, u32[]{:S(2)}, u32[]{:S(2)}) collective-permute-start(f32[32,128]{1,0:T(8,128)S(1)} %get-tuple-element.21), channel_id=1, source_target_pairs={{0,192},{1,193},{2,194},{3,195},{4,0},{5,1},{6,2},{7,3},{8,64},{9,... | collective-permute-start | bytes 49160 | tf_op jit(solution)/shard_map/bias/ppermute | solution.py:105
  34.2 0.9 collective-permute-done.10
  35.3 6.2 %collective-permute-done.11 = f32[128,128]{1,0:T(8,128)S(1)} collective-permute-done((f32[128,128]{1,0:T(8,128)S(1)}, f32[128,128]{1,0:T(8,128)S(1)}, u32[]{:S(2)}, u32[]{:S(2)}) %collective-permute-start.11) | collective-permute-done | bytes 65568 | tf_op jit(solution)/shard_map/bias/ppermute | solution.py:105
  41.5 5.8 %collective-permute-done.12 = f32[128,128]{1,0:T(8,128)S(1)} collective-permute-done((f32[128,128]{1,0:T(8,128)S(1)}, f32[128,128]{1,0:T(8,128)S(1)}, u32[]{:S(2)}, u32[]{:S(2)}) %collective-permute-start.12) | collective-permute-done | bytes 65568 | tf_op jit(solution)/shard_map/bias/ppermute | solution.py:105
  47.3 7.9 %collective-permute-done.13 = f32[128,128]{1,0:T(8,128)S(1)} collective-permute-done((f32[128,128]{1,0:T(8,128)S(1)}, f32[128,128]{1,0:T(8,128)S(1)}, u32[]{:S(2)}, u32[]{:S(2)}) %collective-permute-start.13) | collective-permute-done | bytes 65568 | tf_op jit(solution)/shard_map/bias/ppermute | solution.py:105
  55.2 0.9 collective-permute-start.14
  56.1 6.5 %collective-permute-done.14 = f32[128,128]{1,0:T(8,128)S(1)} collective-permute-done((f32[128,128]{1,0:T(8,128)S(1)}, f32[128,128]{1,0:T(8,128)S(1)}, u32[]{:S(2)}, u32[]{:S(2)}) %collective-permute-start.14) | collective-permute-done | bytes 65568 | tf_op jit(solution)/shard_map/bias/ppermute | solution.py:105
  62.6 5.0 %collective-permute-done.15 = f32[128,128]{1,0:T(8,128)S(1)} collective-permute-done((f32[128,128]{1,0:T(8,128)S(1)}, f32[128,128]{1,0:T(8,128)S(1)}, u32[]{:S(2)}, u32[]{:S(2)}) %collective-permute-start.15) | collective-permute-done | bytes 65568 | tf_op jit(solution)/shard_map/bias/ppermute | solution.py:105
  67.7 4.0 %collective-permute-done.16 = f32[128,128]{1,0:T(8,128)S(1)} collective-permute-done((f32[128,128]{1,0:T(8,128)S(1)}, f32[128,128]{1,0:T(8,128)S(1)}, u32[]{:S(2)}, u32[]{:S(2)}) %collective-permute-start.16) | collective-permute-done | bytes 65568 | tf_op jit(solution)/shard_map/bias/ppermute | solution.py:105
  71.7 1.3 collective-permute-start.17
  73.0 1.8 collective-permute-done.17
  74.8 0.7 collective-permute-start.1
  75.5 3.6 %collective-permute-start.2 = (bf16[8,64,128]{2,1,0:T(8,128)(2,1)S(1)}, bf16[8,64,128]{2,1,0:T(8,128)(2,1)S(1)}, u32[]{:S(2)}, u32[]{:S(2)}) collective-permute-start(bf16[8,64,128]{2,1,0:T(8,128)(2,1)S(1)} %get-tuple-element.9), channel_id=1, source_target_pairs={{0,3},{1,0},{2,1},{3,2},{4,7},{5,4},{6,5},{7,6},{8,11},{9,8},{10,9... | collective-permute-start | bytes 393224 | tf_op jit(solution)/shard_map/rows/ppermute | solution.py:105
  79.6 3.8 %collective-permute-start.19 = (f32[8,128,128]{2,1,0:T(8,128)S(1)}, f32[8,128,128]{2,1,0:T(8,128)S(1)}, u32[]{:S(2)}, u32[]{:S(2)}) collective-permute-start(f32[8,128,128]{2,1,0:T(8,128)S(1)} %bitcast_dynamic-update-slice_fusion.b00), channel_id=1, source_target_pairs={{0,64},{1,65},{2,66},{3,67},{4,68},{5,69},{6,70},{7,71},{8,72},{9,... | collective-permute-start | bytes 1572872 | tf_op jit(solution)/shard_map/bias/ppermute | solution.py:105
  83.4 5.7 %collective-permute-start.21 = (f32[8,128,128]{2,1,0:T(8,128)S(1)}, f32[8,128,128]{2,1,0:T(8,128)S(1)}, u32[]{:S(2)}, u32[]{:S(2)}) collective-permute-start(f32[8,128,128]{2,1,0:T(8,128)S(1)} %bitcast_dynamic-update-slice_fusion.b00), channel_id=1, source_target_pairs={{0,128},{1,129},{2,130},{3,131},{4,132},{5,133},{6,134},{7,135},{8... | collective-permute-start | bytes 1572872 | tf_op jit(solution)/shard_map/bias/ppermute | solution.py:105
  89.2 0.7 collective-permute-start.23
  90.0 15.3 %collective-permute-start.18 = (f32[8,128,128]{2,1,0:T(8,128)S(1)}, f32[8,128,128]{2,1,0:T(8,128)S(1)}, u32[]{:S(2)}, u32[]{:S(2)}) collective-permute-start(f32[8,128,128]{2,1,0:T(8,128)S(1)} %bitcast_dynamic-update-slice_fusion.b00), channel_id=1, source_target_pairs={{0,16},{1,17},{2,18},{3,19},{4,20},{5,21},{6,22},{7,23},{8,24},{9,... | collective-permute-start | bytes 1572872 | tf_op jit(solution)/shard_map/bias/ppermute | solution.py:105
  105.3 1.6 collective-permute-start.4
  106.9 1.2 collective-permute-start.5
  108.1 8.9 %collective-permute-start.20 = (f32[8,128,128]{2,1,0:T(8,128)S(1)}, f32[8,128,128]{2,1,0:T(8,128)S(1)}, u32[]{:S(2)}, u32[]{:S(2)}) collective-permute-start(f32[8,128,128]{2,1,0:T(8,128)S(1)} %collective-permute-done.19.b10), channel_id=1, source_target_pairs={{0,16},{1,17},{2,18},{3,19},{4,20},{5,21},{6,22},{7,23},{8,24},{9,... | collective-permute-start | bytes 1572872 | tf_op jit(solution)/shard_map/bias/ppermute | solution.py:105
  117.1 14.1 %collective-permute-done.3.x1 = bf16[4,8,64,128]{3,2,1,0:T(8,128)(2,1)S(1)} collective-permute-done((bf16[4,8,64,128]{3,2,1,0:T(8,128)(2,1)S(1)}, bf16[4,8,64,128]{3,2,1,0:T(8,128)(2,1)S(1)}, u32[]{:S(2)}, u32[]{:S(2)}) %collective-permute-start.3) | collective-permute-done | bytes 524320 | tf_op jit(solution)/shard_map/rows/ppermute | solution.py:105
  131.2 0.8 copy-done.1
  132.0 0.9 collective-permute-start.24
  133.0 0.9 copy.30
  133.9 0.9 copy.31
  134.7 0.9 copy.32
  135.7 1.1 pad_maximum_fusion.1.x0
  137.4 2.5 %collective-permute-start.33 = (bf16[4,8,64,128]{3,2,1,0:T(8,128)(2,1)S(1)}, bf16[4,8,64,128]{3,2,1,0:T(8,128)(2,1)S(1)}, u32[]{:S(2)}, u32[]{:S(2)}) collective-permute-start(bf16[4,8,64,128]{3,2,1,0:T(8,128)(2,1)S(1)} %pad_maximum_fusion.1.x0), channel_id=1, source_target_pairs={{0,12},{1,13},{2,14},{3,15},{4,0},{5,1},{6,2},{7,3},{8,4},{9,5},{1... | collective-permute-start | bytes 1572872 | tf_op jit(solution)/shard_map/rows/ppermute | solution.py:105
  140.0 25.7 %attention.2 = bf16[4,8,64,128]{3,2,1,0:T(8,128)(2,1)S(1)} custom-call(s32[4]{0:T(128)S(1)} %pad_add_fusion.at, bf16[4,8,64,128]{3,2,1,0:T(8,128)(2,1)S(1)} %pad_maximum_fusion.x0, bf16[4,8,64,128]{3,2,1,0:T(8,128)(2,1)S(1)} %copy-done.2, bf16[4,8,64,128]{3,2,1,0:T(8,128)(2,1)} %collective-permute-done.4.x2, ...), custom_call_target="tpu_custom_call" | custom-call | flops 2400000000 | bytes 8388608 | tf_op jit(solution)/shard_map/attention/pallas_call | solution.py:73
  165.7 2.9 %collective-permute-start.25 = (bf16[8,64,128]{2,1,0:T(8,128)(2,1)S(1)}, bf16[8,64,128]{2,1,0:T(8,128)(2,1)S(1)}, u32[]{:S(2)}, u32[]{:S(2)}) collective-permute-start(bf16[8,64,128]{2,1,0:T(8,128)(2,1)S(1)} %get-tuple-element.18), channel_id=1, source_target_pairs={{0,3},{1,0},{2,1},{3,2},{4,7},{5,4},{6,5},{7,6},{8,11},{9,8},{10,9... | collective-permute-start | bytes 393224 | tf_op jit(solution)/shard_map/update/ppermute | solution.py:105
  169.4 25.6 %attention.3 = bf16[4,8,64,128]{3,2,1,0:T(8,128)(2,1)S(1)} custom-call(s32[4]{0:T(128)S(1)} %pad_add_fusion.at, bf16[4,8,64,128]{3,2,1,0:T(8,128)(2,1)S(1)} %pad_maximum_fusion.1.x0, bf16[4,8,64,128]{3,2,1,0:T(8,128)(2,1)S(1)} %collective-permute-done.31.x1, bf16[4,8,64,128]{3,2,1,0:T(8,128)(2,1)S(1)} %collective-permute-done.32.x2, ...), custom_call_target="tpu_custom_call" | custom-call | flops 2400000000 | bytes 8388608 | tf_op jit(solution)/shard_map/attention/pallas_call | solution.py:73
  195.1 3.0 %collective-permute-start.34 = (bf16[8,64,128]{2,1,0:T(8,128)(2,1)S(1)}, bf16[8,64,128]{2,1,0:T(8,128)(2,1)S(1)}, u32[]{:S(2)}, u32[]{:S(2)}) collective-permute-start(bf16[8,64,128]{2,1,0:T(8,128)(2,1)S(1)} %get-tuple-element.15), channel_id=1, source_target_pairs={{0,3},{1,0},{2,1},{3,2},{4,7},{5,4},{6,5},{7,6},{8,11},{9,8},{10,9... | collective-permute-start | bytes 393224 | tf_op jit(solution)/shard_map/update/ppermute | solution.py:105
  198.8 1.2 collective-permute-done.34
  200.0 9.3 %collective-permute-done.35 = bf16[8,64,128]{2,1,0:T(8,128)(2,1)S(1)} collective-permute-done((bf16[8,64,128]{2,1,0:T(8,128)(2,1)S(1)}, bf16[8,64,128]{2,1,0:T(8,128)(2,1)S(1)}, u32[]{:S(2)}, u32[]{:S(2)}) %collective-permute-start.35) | collective-permute-done | bytes 131104 | tf_op jit(solution)/shard_map/update/ppermute | solution.py:105
  209.3 0.9 copy-done.7
  (100 shorter events, 5.3 us)
Async XLA Ops:
  0.0 4.6 %copy-start = (f32[128,4]{0,1:T(4,128)S(1)}, f32[128,4]{0,1:T(4,128)}, u32[]{:S(2)}) copy-start(f32[128,4]{0,1:T(4,128)} %param.19) | copy-start | bytes 6148
  0.0 2.0 copy-start.6
  0.0 3.3 %copy-start.11 = (f32[128]{0:T(128)S(1)}, f32[128]{0:T(128)}, u32[]{:S(2)}) copy-start(f32[128]{0:T(128)} %param.13) | copy-start | bytes 1540
  0.0 3.3 %copy-start.12 = (f32[128]{0:T(128)S(1)}, f32[128]{0:T(128)}, u32[]{:S(2)}) copy-start(f32[128]{0:T(128)} %param.12) | copy-start | bytes 1540
  7.4 4.3 %collective-permute-start.6 = (f32[4,32,64]{1,0,2:T(4,128)S(1)}, f32[4,32,64]{1,0,2:T(4,128)S(1)}, u32[]{:S(2)}, u32[]{:S(2)}) collective-permute-start(f32[4,32,64]{1,0,2:T(4,128)S(1)} %get-tuple-element.20), channel_id=1, source_target_pairs={{0,16},{1,17},{2,18},{3,19},{4,20},{5,21},{6,22},{7,23},{8,24},{9,... | collective-permute-start | bytes 98312 | tf_op jit(solution)/shard_map/bias/ppermute | solution.py:105
  11.9 5.2 %collective-permute-start.7 = (f32[32,128]{1,0:T(8,128)S(1)}, f32[32,128]{1,0:T(8,128)S(1)}, u32[]{:S(2)}, u32[]{:S(2)}) collective-permute-start(f32[32,128]{1,0:T(8,128)S(1)} %get-tuple-element.24), channel_id=1, source_target_pairs={{0,0},{1,1},{2,2},{3,3},{4,64},{5,65},{6,66},{7,67},{8,128},{9,129... | collective-permute-start | bytes 49160 | tf_op jit(solution)/shard_map/bias/ppermute | solution.py:105
  12.7 76.5 %collective-permute-start.28 = (bf16[8,64,128]{2,1,0:T(8,128)(2,1)S(1)}, bf16[8,64,128]{2,1,0:T(8,128)(2,1)S(1)}, u32[]{:S(2)}, u32[]{:S(2)}) collective-permute-start(bf16[8,64,128]{2,1,0:T(8,128)(2,1)S(1)} %get-tuple-element.8), channel_id=1, source_target_pairs={{0,1},{1,2},{2,3},{3,0},{4,5},{5,6},{6,7},{7,4},{8,9},{9,10},{10,1... | collective-permute-start | bytes 393224 | tf_op jit(solution)/shard_map/rows/ppermute | solution.py:105
  12.8 77.2 %collective-permute-start.29 = (bf16[8,64,128]{2,1,0:T(8,128)(2,1)S(1)}, bf16[8,64,128]{2,1,0:T(8,128)(2,1)}, u32[]{:S(2)}, u32[]{:S(2)}) collective-permute-start(bf16[8,64,128]{2,1,0:T(8,128)(2,1)S(1)} %get-tuple-element.7), channel_id=1, source_target_pairs={{0,2},{1,3},{2,0},{3,1},{4,6},{5,7},{6,4},{7,5},{8,10},{9,11},{10,... | collective-permute-start | bytes 393224 | tf_op jit(solution)/shard_map/rows/ppermute | solution.py:105
  15.7 89.6 %collective-permute-start.30 = (bf16[8,64,128]{2,1,0:T(8,128)(2,1)S(1)}, bf16[8,64,128]{2,1,0:T(8,128)(2,1)S(1)}, u32[]{:S(2)}, u32[]{:S(2)}) collective-permute-start(bf16[8,64,128]{2,1,0:T(8,128)(2,1)S(1)} %get-tuple-element.6), channel_id=1, source_target_pairs={{0,3},{1,0},{2,1},{3,2},{4,7},{5,4},{6,5},{7,6},{8,11},{9,8},{10,9... | collective-permute-start | bytes 393224 | tf_op jit(solution)/shard_map/rows/ppermute | solution.py:105
  16.4 59.1 %collective-permute-start = (bf16[8,64,128]{2,1,0:T(8,128)(2,1)S(1)}, bf16[8,64,128]{2,1,0:T(8,128)(2,1)S(1)}, u32[]{:S(2)}, u32[]{:S(2)}) collective-permute-start(bf16[8,64,128]{2,1,0:T(8,128)(2,1)S(1)} %get-tuple-element.11), channel_id=1, source_target_pairs={{0,1},{1,2},{2,3},{3,0},{4,5},{5,6},{6,7},{7,4},{8,9},{9,10},{10,1... | collective-permute-start | bytes 393224 | tf_op jit(solution)/shard_map/rows/ppermute | solution.py:105
  17.1 7.7 %collective-permute-start.8 = (f32[32,128]{1,0:T(8,128)S(1)}, f32[32,128]{1,0:T(8,128)S(1)}, u32[]{:S(2)}, u32[]{:S(2)}) collective-permute-start(f32[32,128]{1,0:T(8,128)S(1)} %get-tuple-element.23), channel_id=1, source_target_pairs={{0,64},{1,65},{2,66},{3,67},{4,128},{5,129},{6,130},{7,131},{8,192... | collective-permute-start | bytes 49160 | tf_op jit(solution)/shard_map/bias/ppermute | solution.py:105
  24.9 5.2 %collective-permute-start.9 = (f32[32,128]{1,0:T(8,128)S(1)}, f32[32,128]{1,0:T(8,128)S(1)}, u32[]{:S(2)}, u32[]{:S(2)}) collective-permute-start(f32[32,128]{1,0:T(8,128)S(1)} %get-tuple-element.22), channel_id=1, source_target_pairs={{0,128},{1,129},{2,130},{3,131},{4,192},{5,193},{6,194},{7,195},{8... | collective-permute-start | bytes 49160 | tf_op jit(solution)/shard_map/bias/ppermute | solution.py:105
  30.1 4.9 %collective-permute-start.10 = (f32[32,128]{1,0:T(8,128)S(1)}, f32[32,128]{1,0:T(8,128)S(1)}, u32[]{:S(2)}, u32[]{:S(2)}) collective-permute-start(f32[32,128]{1,0:T(8,128)S(1)} %get-tuple-element.21), channel_id=1, source_target_pairs={{0,192},{1,193},{2,194},{3,195},{4,0},{5,1},{6,2},{7,3},{8,64},{9,... | collective-permute-start | bytes 49160 | tf_op jit(solution)/shard_map/bias/ppermute | solution.py:105
  35.1 6.4 %collective-permute-start.11 = (f32[128,128]{1,0:T(8,128)S(1)}, f32[128,128]{1,0:T(8,128)S(1)}, u32[]{:S(2)}, u32[]{:S(2)}) collective-permute-start(f32[128,128]{1,0:T(8,128)S(1)} %bitcast.92), channel_id=1, source_target_pairs={{0,1},{1,2},{2,3},{3,32},{4,5},{5,6},{6,7},{7,36},{8,9},{9,10},{10... | collective-permute-start | bytes 196616 | tf_op jit(solution)/shard_map/bias/ppermute | solution.py:105
  35.2 97.6 %copy-start.10 = (f32[128]{0:T(128)S(1)}, f32[128]{0:T(128)}, u32[]{:S(2)}) copy-start(f32[128]{0:T(128)} %param.18) | copy-start | bytes 1540
  41.5 5.9 %collective-permute-start.12 = (f32[128,128]{1,0:T(8,128)S(1)}, f32[128,128]{1,0:T(8,128)S(1)}, u32[]{:S(2)}, u32[]{:S(2)}) collective-permute-start(f32[128,128]{1,0:T(8,128)S(1)} %bitcast.94), channel_id=1, source_target_pairs={{0,2},{1,3},{2,32},{3,33},{4,6},{5,7},{6,36},{7,37},{8,10},{9,11},... | collective-permute-start | bytes 196616 | tf_op jit(solution)/shard_map/bias/ppermute | solution.py:105
  47.3 7.9 %collective-permute-start.13 = (f32[128,128]{1,0:T(8,128)S(1)}, f32[128,128]{1,0:T(8,128)S(1)}, u32[]{:S(2)}, u32[]{:S(2)}) collective-permute-start(f32[128,128]{1,0:T(8,128)S(1)} %bitcast.95), channel_id=1, source_target_pairs={{0,3},{1,32},{2,33},{3,34},{4,7},{5,36},{6,37},{7,38},{8,11},{9,40... | collective-permute-start | bytes 196616 | tf_op jit(solution)/shard_map/bias/ppermute | solution.py:105
  55.2 7.4 %collective-permute-start.14 = (f32[128,128]{1,0:T(8,128)S(1)}, f32[128,128]{1,0:T(8,128)S(1)}, u32[]{:S(2)}, u32[]{:S(2)}) collective-permute-start(f32[128,128]{1,0:T(8,128)S(1)} %bitcast.96), channel_id=1, source_target_pairs={{0,32},{1,33},{2,34},{3,35},{4,36},{5,37},{6,38},{7,39},{8,40},{9,... | collective-permute-start | bytes 196616 | tf_op jit(solution)/shard_map/bias/ppermute | solution.py:105
  62.6 5.0 %collective-permute-start.15 = (f32[128,128]{1,0:T(8,128)S(1)}, f32[128,128]{1,0:T(8,128)S(1)}, u32[]{:S(2)}, u32[]{:S(2)}) collective-permute-start(f32[128,128]{1,0:T(8,128)S(1)} %bitcast.97), channel_id=1, source_target_pairs={{0,33},{1,34},{2,35},{3,0},{4,37},{5,38},{6,39},{7,4},{8,41},{9,42... | collective-permute-start | bytes 196616 | tf_op jit(solution)/shard_map/bias/ppermute | solution.py:105
  67.7 4.1 %collective-permute-start.16 = (f32[128,128]{1,0:T(8,128)S(1)}, f32[128,128]{1,0:T(8,128)S(1)}, u32[]{:S(2)}, u32[]{:S(2)}) collective-permute-start(f32[128,128]{1,0:T(8,128)S(1)} %bitcast.98), channel_id=1, source_target_pairs={{0,34},{1,35},{2,0},{3,1},{4,38},{5,39},{6,4},{7,5},{8,42},{9,43},... | collective-permute-start | bytes 196616 | tf_op jit(solution)/shard_map/bias/ppermute | solution.py:105
  71.7 3.1 %collective-permute-start.17 = (f32[128,128]{1,0:T(8,128)S(1)}, f32[128,128]{1,0:T(8,128)S(1)}, u32[]{:S(2)}, u32[]{:S(2)}) collective-permute-start(f32[128,128]{1,0:T(8,128)S(1)} %bitcast.99), channel_id=1, source_target_pairs={{0,35},{1,0},{2,1},{3,2},{4,39},{5,4},{6,5},{7,6},{8,43},{9,8},{10... | collective-permute-start | bytes 196616 | tf_op jit(solution)/shard_map/bias/ppermute | solution.py:105
  74.8 4.8 %collective-permute-start.1 = (bf16[8,64,128]{2,1,0:T(8,128)(2,1)S(1)}, bf16[8,64,128]{2,1,0:T(8,128)(2,1)S(1)}, u32[]{:S(2)}, u32[]{:S(2)}) collective-permute-start(bf16[8,64,128]{2,1,0:T(8,128)(2,1)S(1)} %get-tuple-element.10), channel_id=1, source_target_pairs={{0,2},{1,3},{2,0},{3,1},{4,6},{5,7},{6,4},{7,5},{8,10},{9,11},{10,... | collective-permute-start | bytes 393224 | tf_op jit(solution)/shard_map/rows/ppermute | solution.py:105
  75.5 7.9 %collective-permute-start.2 = (bf16[8,64,128]{2,1,0:T(8,128)(2,1)S(1)}, bf16[8,64,128]{2,1,0:T(8,128)(2,1)S(1)}, u32[]{:S(2)}, u32[]{:S(2)}) collective-permute-start(bf16[8,64,128]{2,1,0:T(8,128)(2,1)S(1)} %get-tuple-element.9), channel_id=1, source_target_pairs={{0,3},{1,0},{2,1},{3,2},{4,7},{5,4},{6,5},{7,6},{8,11},{9,8},{10,9... | collective-permute-start | bytes 393224 | tf_op jit(solution)/shard_map/rows/ppermute | solution.py:105
  79.6 25.7 %collective-permute-start.19 = (f32[8,128,128]{2,1,0:T(8,128)S(1)}, f32[8,128,128]{2,1,0:T(8,128)S(1)}, u32[]{:S(2)}, u32[]{:S(2)}) collective-permute-start(f32[8,128,128]{2,1,0:T(8,128)S(1)} %bitcast_dynamic-update-slice_fusion.b00), channel_id=1, source_target_pairs={{0,64},{1,65},{2,66},{3,67},{4,68},{5,69},{6,70},{7,71},{8,72},{9,... | collective-permute-start | bytes 1572872 | tf_op jit(solution)/shard_map/bias/ppermute | solution.py:105
  83.4 23.5 %collective-permute-start.21 = (f32[8,128,128]{2,1,0:T(8,128)S(1)}, f32[8,128,128]{2,1,0:T(8,128)S(1)}, u32[]{:S(2)}, u32[]{:S(2)}) collective-permute-start(f32[8,128,128]{2,1,0:T(8,128)S(1)} %bitcast_dynamic-update-slice_fusion.b00), channel_id=1, source_target_pairs={{0,128},{1,129},{2,130},{3,131},{4,132},{5,133},{6,134},{7,135},{8... | collective-permute-start | bytes 1572872 | tf_op jit(solution)/shard_map/bias/ppermute | solution.py:105
  89.1 50.8 %copy-start.3 = (bf16[128,128]{1,0:T(8,128)(2,1)S(1)}, bf16[128,128]{1,0:T(8,128)(2,1)}, u32[]{:S(2)}) copy-start(bf16[128,128]{1,0:T(8,128)(2,1)} %wk.3) | copy-start | bytes 98308
  89.1 50.8 %copy-start.4 = (bf16[128,128]{1,0:T(8,128)(2,1)S(1)}, bf16[128,128]{1,0:T(8,128)(2,1)}, u32[]{:S(2)}) copy-start(bf16[128,128]{1,0:T(8,128)(2,1)} %wo.3) | copy-start | bytes 98308
  89.1 50.8 %copy-start.5 = (f32[128]{0:T(128)S(1)}, f32[128]{0:T(128)}, u32[]{:S(2)}) copy-start(f32[128]{0:T(128)} %param.21) | copy-start | bytes 1540
  89.2 18.8 %collective-permute-start.23 = (f32[8,128,128]{2,1,0:T(8,128)S(1)}, f32[8,128,128]{2,1,0:T(8,128)}, u32[]{:S(2)}, u32[]{:S(2)}) collective-permute-start(f32[8,128,128]{2,1,0:T(8,128)S(1)} %bitcast_dynamic-update-slice_fusion.b00), channel_id=1, source_target_pairs={{0,192},{1,193},{2,194},{3,195},{4,196},{5,197},{6,198},{7,199},{8... | collective-permute-start | bytes 1572872 | tf_op jit(solution)/shard_map/bias/ppermute | solution.py:105
  90.0 27.0 %collective-permute-start.18 = (f32[8,128,128]{2,1,0:T(8,128)S(1)}, f32[8,128,128]{2,1,0:T(8,128)S(1)}, u32[]{:S(2)}, u32[]{:S(2)}) collective-permute-start(f32[8,128,128]{2,1,0:T(8,128)S(1)} %bitcast_dynamic-update-slice_fusion.b00), channel_id=1, source_target_pairs={{0,16},{1,17},{2,18},{3,19},{4,20},{5,21},{6,22},{7,23},{8,24},{9,... | collective-permute-start | bytes 1572872 | tf_op jit(solution)/shard_map/bias/ppermute | solution.py:105
  105.3 27.6 %copy-start.9 = (bf16[8,64,128]{2,1,0:T(8,128)(2,1)}, bf16[8,64,128]{2,1,0:T(8,128)(2,1)S(1)}, u32[]{:S(2)}) copy-start(bf16[8,64,128]{2,1,0:T(8,128)(2,1)S(1)} %collective-permute-done.30) | copy-start | bytes 393220
  105.3 25.9 %collective-permute-start.3 = (bf16[4,8,64,128]{3,2,1,0:T(8,128)(2,1)S(1)}, bf16[4,8,64,128]{3,2,1,0:T(8,128)(2,1)S(1)}, u32[]{:S(2)}, u32[]{:S(2)}) collective-permute-start(bf16[4,8,64,128]{3,2,1,0:T(8,128)(2,1)S(1)} %pad_maximum_fusion.x0), channel_id=1, source_target_pairs={{0,4},{1,5},{2,6},{3,7},{4,8},{5,9},{6,10},{7,11},{8,12},{9,13},{1... | collective-permute-start | bytes 1572872 | tf_op jit(solution)/shard_map/rows/ppermute | solution.py:105
  105.3 31.6 %collective-permute-start.4 = (bf16[4,8,64,128]{3,2,1,0:T(8,128)(2,1)S(1)}, bf16[4,8,64,128]{3,2,1,0:T(8,128)(2,1)}, u32[]{:S(2)}, u32[]{:S(2)}) collective-permute-start(bf16[4,8,64,128]{3,2,1,0:T(8,128)(2,1)S(1)} %pad_maximum_fusion.x0), channel_id=1, source_target_pairs={{0,8},{1,9},{2,10},{3,11},{4,12},{5,13},{6,14},{7,15},{8,0},{9,1},... | collective-permute-start | bytes 1572872 | tf_op jit(solution)/shard_map/rows/ppermute | solution.py:105
  106.9 30.1 %collective-permute-start.5 = (bf16[4,8,64,128]{3,2,1,0:T(8,128)(2,1)S(1)}, bf16[4,8,64,128]{3,2,1,0:T(8,128)(2,1)}, u32[]{:S(2)}, u32[]{:S(2)}) collective-permute-start(bf16[4,8,64,128]{3,2,1,0:T(8,128)(2,1)S(1)} %pad_maximum_fusion.x0), channel_id=1, source_target_pairs={{0,12},{1,13},{2,14},{3,15},{4,0},{5,1},{6,2},{7,3},{8,4},{9,5},{1... | collective-permute-start | bytes 1572872 | tf_op jit(solution)/shard_map/rows/ppermute | solution.py:105
  108.1 29.4 %collective-permute-start.20 = (f32[8,128,128]{2,1,0:T(8,128)S(1)}, f32[8,128,128]{2,1,0:T(8,128)S(1)}, u32[]{:S(2)}, u32[]{:S(2)}) collective-permute-start(f32[8,128,128]{2,1,0:T(8,128)S(1)} %collective-permute-done.19.b10), channel_id=1, source_target_pairs={{0,16},{1,17},{2,18},{3,19},{4,20},{5,21},{6,22},{7,23},{8,24},{9,... | collective-permute-start | bytes 1572872 | tf_op jit(solution)/shard_map/bias/ppermute | solution.py:105
  117.0 22.9 %collective-permute-start.22 = (f32[8,128,128]{2,1,0:T(8,128)S(1)}, f32[8,128,128]{2,1,0:T(8,128)}, u32[]{:S(2)}, u32[]{:S(2)}) collective-permute-start(f32[8,128,128]{2,1,0:T(8,128)S(1)} %collective-permute-done.21.b20), channel_id=1, source_target_pairs={{0,16},{1,17},{2,18},{3,19},{4,20},{5,21},{6,22},{7,23},{8,24},{9,... | collective-permute-start | bytes 1572872 | tf_op jit(solution)/shard_map/bias/ppermute | solution.py:105
  132.0 7.9 %collective-permute-start.24 = (f32[8,128,128]{2,1,0:T(8,128)}, f32[8,128,128]{2,1,0:T(8,128)}, u32[]{:S(2)}, u32[]{:S(2)}) collective-permute-start(f32[8,128,128]{2,1,0:T(8,128)} %collective-permute-done.23.b30), channel_id=1, source_target_pairs={{0,16},{1,17},{2,18},{3,19},{4,20},{5,21},{6,22},{7,23},{8,24},{9,... | collective-permute-start | bytes 1572872 | tf_op jit(solution)/shard_map/bias/ppermute | solution.py:105
  135.6 4.3 %copy-start.2 = (bf16[4,8,64,128]{3,2,1,0:T(8,128)(2,1)S(1)}, bf16[4,8,64,128]{3,2,1,0:T(8,128)(2,1)}, u32[]{:S(2)}) copy-start(bf16[4,8,64,128]{3,2,1,0:T(8,128)(2,1)} %copy-done.1) | copy-start | bytes 1572868
  136.9 32.1 %collective-permute-start.31 = (bf16[4,8,64,128]{3,2,1,0:T(8,128)(2,1)S(1)}, bf16[4,8,64,128]{3,2,1,0:T(8,128)(2,1)S(1)}, u32[]{:S(2)}, u32[]{:S(2)}) collective-permute-start(bf16[4,8,64,128]{3,2,1,0:T(8,128)(2,1)S(1)} %pad_maximum_fusion.1.x0), channel_id=1, source_target_pairs={{0,4},{1,5},{2,6},{3,7},{4,8},{5,9},{6,10},{7,11},{8,12},{9,13},{1... | collective-permute-start | bytes 1572872 | tf_op jit(solution)/shard_map/rows/ppermute | solution.py:105
  137.0 32.4 %collective-permute-start.32 = (bf16[4,8,64,128]{3,2,1,0:T(8,128)(2,1)S(1)}, bf16[4,8,64,128]{3,2,1,0:T(8,128)(2,1)S(1)}, u32[]{:S(2)}, u32[]{:S(2)}) collective-permute-start(bf16[4,8,64,128]{3,2,1,0:T(8,128)(2,1)S(1)} %pad_maximum_fusion.1.x0), channel_id=1, source_target_pairs={{0,8},{1,9},{2,10},{3,11},{4,12},{5,13},{6,14},{7,15},{8,0},{9,1},... | collective-permute-start | bytes 1572872 | tf_op jit(solution)/shard_map/rows/ppermute | solution.py:105
  137.4 32.0 %collective-permute-start.33 = (bf16[4,8,64,128]{3,2,1,0:T(8,128)(2,1)S(1)}, bf16[4,8,64,128]{3,2,1,0:T(8,128)(2,1)S(1)}, u32[]{:S(2)}, u32[]{:S(2)}) collective-permute-start(bf16[4,8,64,128]{3,2,1,0:T(8,128)(2,1)S(1)} %pad_maximum_fusion.1.x0), channel_id=1, source_target_pairs={{0,12},{1,13},{2,14},{3,15},{4,0},{5,1},{6,2},{7,3},{8,4},{9,5},{1... | collective-permute-start | bytes 1572872 | tf_op jit(solution)/shard_map/rows/ppermute | solution.py:105
  165.7 32.9 %collective-permute-start.25 = (bf16[8,64,128]{2,1,0:T(8,128)(2,1)S(1)}, bf16[8,64,128]{2,1,0:T(8,128)(2,1)S(1)}, u32[]{:S(2)}, u32[]{:S(2)}) collective-permute-start(bf16[8,64,128]{2,1,0:T(8,128)(2,1)S(1)} %get-tuple-element.18), channel_id=1, source_target_pairs={{0,3},{1,0},{2,1},{3,2},{4,7},{5,4},{6,5},{7,6},{8,11},{9,8},{10,9... | collective-permute-start | bytes 393224 | tf_op jit(solution)/shard_map/update/ppermute | solution.py:105
  168.6 30.0 %collective-permute-start.26 = (bf16[8,64,128]{2,1,0:T(8,128)(2,1)S(1)}, bf16[8,64,128]{2,1,0:T(8,128)(2,1)S(1)}, u32[]{:S(2)}, u32[]{:S(2)}) collective-permute-start(bf16[8,64,128]{2,1,0:T(8,128)(2,1)S(1)} %get-tuple-element.17), channel_id=1, source_target_pairs={{0,2},{1,3},{2,0},{3,1},{4,6},{5,7},{6,4},{7,5},{8,10},{9,11},{10,... | collective-permute-start | bytes 393224 | tf_op jit(solution)/shard_map/update/ppermute | solution.py:105
  168.9 29.8 %collective-permute-start.27 = (bf16[8,64,128]{2,1,0:T(8,128)(2,1)S(1)}, bf16[8,64,128]{2,1,0:T(8,128)(2,1)S(1)}, u32[]{:S(2)}, u32[]{:S(2)}) collective-permute-start(bf16[8,64,128]{2,1,0:T(8,128)(2,1)S(1)} %get-tuple-element.16), channel_id=1, source_target_pairs={{0,1},{1,2},{2,3},{3,0},{4,5},{5,6},{6,7},{7,4},{8,9},{9,10},{10,1... | collective-permute-start | bytes 393224 | tf_op jit(solution)/shard_map/update/ppermute | solution.py:105
  195.1 4.9 %collective-permute-start.34 = (bf16[8,64,128]{2,1,0:T(8,128)(2,1)S(1)}, bf16[8,64,128]{2,1,0:T(8,128)(2,1)S(1)}, u32[]{:S(2)}, u32[]{:S(2)}) collective-permute-start(bf16[8,64,128]{2,1,0:T(8,128)(2,1)S(1)} %get-tuple-element.15), channel_id=1, source_target_pairs={{0,3},{1,0},{2,1},{3,2},{4,7},{5,4},{6,5},{7,6},{8,11},{9,8},{10,9... | collective-permute-start | bytes 393224 | tf_op jit(solution)/shard_map/update/ppermute | solution.py:105
  198.0 11.3 %collective-permute-start.35 = (bf16[8,64,128]{2,1,0:T(8,128)(2,1)S(1)}, bf16[8,64,128]{2,1,0:T(8,128)(2,1)S(1)}, u32[]{:S(2)}, u32[]{:S(2)}) collective-permute-start(bf16[8,64,128]{2,1,0:T(8,128)(2,1)S(1)} %get-tuple-element.14), channel_id=1, source_target_pairs={{0,2},{1,3},{2,0},{3,1},{4,6},{5,7},{6,4},{7,5},{8,10},{9,11},{10,... | collective-permute-start | bytes 393224 | tf_op jit(solution)/shard_map/update/ppermute | solution.py:105
  198.6 10.7 %collective-permute-start.36 = (bf16[8,64,128]{2,1,0:T(8,128)(2,1)S(1)}, bf16[8,64,128]{2,1,0:T(8,128)(2,1)S(1)}, u32[]{:S(2)}, u32[]{:S(2)}) collective-permute-start(bf16[8,64,128]{2,1,0:T(8,128)(2,1)S(1)} %get-tuple-element.13), channel_id=1, source_target_pairs={{0,1},{1,2},{2,3},{3,0},{4,5},{5,6},{6,7},{7,4},{8,9},{9,10},{10,1... | collective-permute-start | bytes 393224 | tf_op jit(solution)/shard_map/update/ppermute | solution.py:105
  209.3 1.0 copy-start.7
  (2 other events, 1.5 us)

commit v2 on v1

v2 whole, which is shorter than its diff:
```python
import functools
import math

import jax
import jax.numpy as jnp
from jax import lax
from jax.experimental import pallas as pl
from jax.experimental.pallas import tpu as pltpu
from jax.sharding import Mesh
from jax.sharding import PartitionSpec as P

F32 = jnp.float32
BF = jnp.bfloat16
CHUNKS = 2
TOGETHER = 2
DEPTH = 32


def dot(a, b):
    return jnp.dot(a, b, preferred_element_type=F32)


def dot_t(a, b):
    return lax.dot_general(a, b, (((1,), (1,)), ((), ())), preferred_element_type=F32)


def fold(function, so_far, value):
    return value if so_far is None else function(so_far, value)


def attend_kernel(
    at,
    rows,
    b00,
    b01,
    b10,
    b11,
    b20,
    b21,
    b30,
    b31,
    w_key,
    w_value_t,
    w_query_t,
    w_gate_t,
    gate_shift,
    w_out,
    out_shift,
    out,
    key_ref,
    value_ref,
    score_ref,
    attended_ref,
):
    bias = ((b00, b01), (b10, b11), (b20, b21), (b30, b31))
    y, x, zl, core = at[0], at[1], at[2], at[3]
    slot = [lax.rem(zl + 4 - part, 4) for part in range(4)]
    heads = [lax.rem(y + 4 - step, 4) for step in range(4)]
    halves = [pl.multiple_of(lax.rem(core + half, 2) * 32, 32) for half in range(2)]
    xs = [lax.rem(x + 4 - step, 4) for step in range(4)]
    kept = [{} for _ in range(TOGETHER)]

    def project_query(r):
        tokens = jnp.concatenate([rows[x, slot[part], r] for part in range(4)], axis=0)
        query = (dot_t(w_query_t[...], tokens) * (1.0 / math.sqrt(DEPTH))).astype(BF)
        gate = jax.nn.sigmoid(dot_t(w_gate_t[...], tokens) + gate_shift[...])
        of_head = lax.broadcasted_iota(jnp.int32, query.shape, 0) // DEPTH
        zero = jnp.zeros_like(query)
        return [jnp.where(of_head == head, query, zero) for head in heads], gate

    def project(r):
        tokens = jnp.concatenate(
            [
                rows[xs[t], s, r, pl.ds(halves[half], 32), :]
                for half in range(2)
                for s in range(4)
                for t in range(4)
            ],
            axis=0,
        )
        key_ref[r] = dot(tokens, w_key[...]).astype(BF)
        value_ref[r] = dot_t(w_value_t[...], tokens).astype(BF)
        kept[r]["query"], kept[r]["gate"] = project_query(r)

    def score(r, a, c, query):
        half, s = divmod(c, 4)
        z_of = [zh * 4 + lax.rem(zl + 4 - s, 4) for zh in range(2)]
        added = jnp.concatenate([bias[a][half][z] for z in z_of], axis=1)
        return dot(key_ref[r, c * 128 : (c + 1) * 128, :], query[a]) + added

    def raise_plain(r, a):
        total = None
        for c in range(8):
            raised = jnp.exp(score(r, a, c, kept[r]["query"]))
            score_ref[r, a, c] = raised
            total = fold(jnp.add, total, jnp.sum(raised.reshape(16, 8, 256), axis=0))
        return jnp.sum(total, axis=0, keepdims=True)

    def raise_shifted(r, a, query):
        largest = None
        for c in range(8):
            scores = score(r, a, c, query)
            score_ref[r, a, c] = scores
            largest = fold(
                jnp.maximum, largest, jnp.max(scores.reshape(16, 8, 256), axis=0)
            )
        largest = jnp.max(largest, axis=0, keepdims=True)
        total = None
        for c in range(8):
            raised = jnp.exp(score_ref[r, a, c] - largest)
            score_ref[r, a, c] = raised
            total = fold(jnp.add, total, jnp.sum(raised.reshape(16, 8, 256), axis=0))
        return jnp.sum(total, axis=0, keepdims=True)

    def weigh(r, a, total):
        scale = 1.0 / total
        weights = jnp.concatenate(
            [(score_ref[r, a, c] * scale).astype(BF) for c in range(8)], axis=0
        )
        own = pl.ds(pl.multiple_of(heads[a] * DEPTH, DEPTH), DEPTH)
        attended_ref[r, own, :] = dot(value_ref[r, own, :], weights)

    def finish(r, gate):
        gated = (gate * attended_ref[r]).astype(BF)
        update = lax.dot_general(
            gated, w_out[...], (((0,), (0,)), ((), ())), preferred_element_type=F32
        )
        update = (update + out_shift[...]).astype(BF)
        for part in range(4):
            out[slot[part], r] = update[part * 64 : (part + 1) * 64]

    for r in range(TOGETHER):
        project(r)
    totals = {}
    for r in range(TOGETHER):
        for a in range(4):
            totals[r, a] = raise_plain(r, a)
    for r in range(TOGETHER):
        for a in range(4):
            weigh(r, a, totals[r, a])
    for r in range(TOGETHER):
        finish(r, kept[r]["gate"])

    safe = None
    for total in totals.values():
        inside = jnp.logical_and(total > 2.0**-60, total < 2.0**120)
        safe = fold(jnp.minimum, safe, jnp.where(inside, 1.0, 0.0))

    @pl.when(jnp.min(safe) < 0.5)
    def _():
        for r in range(TOGETHER):
            query, gate = project_query(r)
            for a in range(4):
                weigh(r, a, raise_shifted(r, a, query))
            finish(r, gate)


def attend(at, rows, biases, *weights):
    count = rows.shape[2]
    whole = lambda a: pl.BlockSpec(a.shape, lambda i, at: (0,) * a.ndim)
    biases = [b for pair in biases for b in pair]
    return pl.pallas_call(
        attend_kernel,
        out_shape=jax.ShapeDtypeStruct((4, count, 64, 128), BF),
        grid_spec=pltpu.PrefetchScalarGridSpec(
            num_scalar_prefetch=1,
            grid=(count // TOGETHER,),
            in_specs=[
                pl.BlockSpec((4, 4, TOGETHER, 64, 128), lambda i, at: (0, 0, i, 0, 0))
            ]
            + [whole(a) for a in biases]
            + [whole(a) for a in weights],
            out_specs=pl.BlockSpec((4, TOGETHER, 64, 128), lambda i, at: (0, i, 0, 0)),
            scratch_shapes=[
                pltpu.VMEM((TOGETHER, 1024, 128), BF),
                pltpu.VMEM((TOGETHER, 128, 1024), BF),
                pltpu.VMEM((TOGETHER, 4, 8, 128, 256), F32),
                pltpu.VMEM((TOGETHER, 128, 256), F32),
            ],
        ),
        compiler_params=pltpu.CompilerParams(
            vmem_limit_bytes=48 << 20, dimension_semantics=("arbitrary",)
        ),
        cost_estimate=pl.CostEstimate(
            flops=count * 300_000_000,
            bytes_accessed=count << 20,
            transcendentals=count << 20,
        ),
    )(at, rows, *biases, *weights)


def normalize(values, gain, shift):
    values = values.astype(F32)
    mean = jnp.mean(values, axis=-1, keepdims=True)
    centred = values - mean
    spread = jnp.mean(centred * centred, axis=-1, keepdims=True)
    return (centred * lax.rsqrt(spread + 1e-05) * gain + shift).astype(BF)


def stack_kernel(*refs):
    *pieces, _, out = refs
    for at, piece in enumerate(pieces):
        out[at] = piece[...]


def stack_after(pieces, after):
    return pl.pallas_call(
        stack_kernel,
        out_shape=jax.ShapeDtypeStruct((len(pieces), *pieces[0].shape), BF),
        in_specs=[pl.BlockSpec(memory_space=pltpu.VMEM)] * len(pieces)
        + [pl.BlockSpec(memory_space=pl.ANY)],
        out_specs=pl.BlockSpec(memory_space=pltpu.VMEM),
        name="stack_rows",
    )(*pieces, after)


AXES = ("y", "zh", "core", "x", "zl")


def move(array, to):
    pairs = []
    for source in range(256):
        row, col = divmod(source, 16)
        y, zh, core = row // 4, row // 2 % 2, row % 2
        x, zl = divmod(col, 4)
        y, z, core, x = to(y, zh * 4 + zl, core, x)
        y, z, x = y % 4, z % 8, x % 4
        target = ((y * 2 + z // 4) * 2 + core) * 16 + x * 4 + z % 4
        pairs.append((source, target))
    return lax.ppermute(array, AXES, pairs)


def swap_cores(array):
    return move(array, lambda y, z, core, x: (y, z, 1 - core, x))


def turn(z, step):
    return z // 4 * 4 + (z + step) % 4


def on_device(
    pair,
    norm_gain,
    norm_shift,
    w_query,
    w_key,
    w_value,
    w_gate,
    gate_shift,
    w_bias,
    w_out,
    out_shift,
):
    y, core, x, zl = (lax.axis_index(name) for name in ("y", "core", "x", "zl"))
    place = jnp.stack([y, x, zl, core]).astype(jnp.int32)
    normed = normalize(pair, norm_gain, norm_shift)
    count = 16 // CHUNKS

    def exchange(normed, chunk, after):
        with jax.named_scope("rows"):
            pieces = []
            for step in range(4):
                part = lax.dynamic_slice_in_dim(
                    normed, (zl + step) % 4 * 16 + chunk * count, count, 0
                )
                if step:
                    part = move(part, lambda y, z, core, x: (y, turn(z, step), core, x))
                pieces.append(part)
            held = stack_after(pieces, after)
            return lax.all_gather(held, "x", axis=0, tiled=False)

    with jax.named_scope("bias"):
        tile = jnp.einsum(
            "jkc,ch->hkj", normed.astype(F32), w_bias, precision=lax.Precision.HIGHEST
        )
        kept = lax.dynamic_slice_in_dim(tile, core * 32, 32, 1)
        sent = lax.dynamic_slice_in_dim(tile, (1 - core) * 32, 32, 1)
        kept, sent, normed = lax.optimization_barrier((kept, sent, normed))
        got = swap_cores(sent)
        normed0 = normed
        tile = jnp.where(
            core == 0, jnp.concatenate([kept, got], 2), jnp.concatenate([got, kept], 2)
        )
        rounds = []
        for step in range(4):
            part = lax.dynamic_index_in_dim(tile, (x + step) % 4, 0, keepdims=False)
            rounds.append(move(part, lambda y, z, core, x: (x + step, z, core, y)))
        rounds = jnp.stack(rounds + rounds[:3])
        block = lax.dynamic_slice_in_dim(rounds, (y - x) % 4, 4, 0).reshape(128, 128)
        block, normed = lax.optimization_barrier((block, normed))
        along_z = lax.all_to_all(
            jnp.broadcast_to(block[None], (8, 128, 128)),
            ("zh", "zl"),
            split_axis=0,
            concat_axis=0,
            tiled=True,
        )
    rows = [exchange(normed0, 0, block)]
    with jax.named_scope("bias"):
        biases = []
        for step in range(4):
            here = along_z
            if step:
                here = move(along_z, lambda y, z, core, x: (y + step, z, core, x))
            biases.append((here, swap_cores(here)))
    for chunk in range(1, CHUNKS):
        rows.append(exchange(normed, chunk, along_z))
    result = jnp.zeros(pair.shape, BF)
    for chunk in range(CHUNKS):
        with jax.named_scope("attention"):
            part = attend(
                place,
                rows[chunk],
                biases,
                w_key,
                w_value.T,
                w_query.T,
                w_gate.T,
                gate_shift[:, None],
                w_out,
                out_shift[None],
            )
        with jax.named_scope("update"):
            for step in range(4):
                back = part[step]
                if step:
                    back = move(back, lambda y, z, core, x: (y, turn(z, -step), core, x))
                result = lax.dynamic_update_slice_in_dim(
                    result, back, (zl + step) % 4 * 16 + chunk * count, 0
                )
    return result


def solution(mesh):
    parts = Mesh(mesh.devices.reshape(4, 2, 2, 4, 4), AXES)
    tiles = P(("y", "zh", "core"), ("x", "zl"), None)
    return jax.shard_map(
        on_device,
        mesh=parts,
        in_specs=(tiles,) + (P(),) * 10,
        out_specs=tiles,
        check_vma=False,
    )
```

time: 211 us -> 215 us (1.019)
  waiting for transfers between devices: 69.5 us -> 34 us
  Pallas kernels: 51.3 us -> 72.9 us
  between operations: 0.47 us -> 13.8 us
  local copies, waits for them, and re-layouts: 6.2 us -> 15.7 us
  starting transfers between devices: 75 us -> 70.2 us
    ppermute x37 -> x24, waiting for transfers between devices: 69.5 us -> 34 us  [move(): return lax.ppermute(array, AXES, pairs)]
    pallas_call x2 -> x4, Pallas kernels: 51.3 us -> 72.9 us  [the longest x2 69.1 us: attend(): pl.pallas_call(attend_kernel, out_shape=jax.ShapeDtypeStruct((4, count, 6...]
    ppermute x37 -> x24, starting transfers between devices: 75 us -> 63.6 us  [move(): return lax.ppermute(array, AXES, pairs)]
    all_to_all x0 -> x1, starting transfers between devices: none -> 6.53 us  [on_device(): lax.all_to_all(jnp.broadcast_to(block[None], (8, 128, 128)), ('zh', 'zl')...]
    dynamic_update_slice x8, local copies, waits for them, and re-layouts: 0.81 us -> 5.32 us  [on_device(): lax.dynamic_update_slice_in_dim(result, back, (zl + step) % 4 * 16 + chun...]
    unnamed x42 -> x53, local copies, waits for them, and re-layouts: 4.45 us -> 4.85 us
  transfers between devices with their start and end apart: 37 -> 27, of which waited for: 15 -> 10; matrix products, arithmetic and copies ran while one was open for 2% -> 5% of each run, Pallas kernels for 24% -> 17%
where the time goes in v2:
time: 215 us
  Pallas kernels  72.9 us (34%)
  starting transfers between devices  70.2 us (33%)
  waiting for transfers between devices  34 us (16%)
  local copies, waits for them, and re-layouts  15.7 us (7%)
  between operations  13.8 us (6%)
  other arithmetic  5.74 us (3%)
  matrix products  2.53 us (1%)
    pallas_call x2, Pallas kernels, attend(): pl.pallas_call(attend_kernel, out_shape=jax.ShapeDtypeStruct((4, count, 6...  69.1 us
    ppermute x24, starting transfers between devices, move(): return lax.ppermute(array, AXES, pairs)  63.6 us
    ppermute x24, waiting for transfers between devices, move(): return lax.ppermute(array, AXES, pairs)  34 us
    all_to_all x1, starting transfers between devices, on_device(): lax.all_to_all(jnp.broadcast_to(block[None], (8, 128, 128)), ('zh', 'zl')...  6.53 us
    dynamic_update_slice x8, local copies, waits for them, and re-layouts, on_device(): lax.dynamic_update_slice_in_dim(result, back, (zl + step) % 4 * 16 + chun...  5.32 us
    unnamed x53, local copies, waits for them, and re-layouts  4.85 us
  transfers between devices with their start and end apart: 27, of which 10 were waited for; matrix products, arithmetic and copies ran while one was open for 5% of the time, Pallas kernels for 17%

profile of v2, /device:TPU:1, one launch (start us, length us, event | category | flops | bytes accessed | tf_op | source)
XLA Modules:
  0.0 214.9 jit_solution(5038893675208710511)
XLA Ops:
  6.6 1.9 convert_reduce_fusion
  8.5 2.3 %fusion.2 = f32[64,64]{1,0:T(8,128)S(1)} fusion(bf16[64,64,128]{2,1,0:T(8,128)(2,1)} %param.11, f32[64,64]{1,0:T(8,128)S(1)} %broadcast_multiply_fusion), kind=kLoop, calls=%fused_computation.4 | loop fusion | flops 2093056 | bytes 1081344 | tf_op jit(solution)/shard_map/reduce_sum | solution.py:196
  10.9 1.3 fusion.5
  12.2 2.5 %fusion.8 = f32[64,64,4]{1,2,0:T(4,128)S(1)} fusion(bf16[64,64,128]{2,1,0:T(8,128)(2,1)S(1)} %fusion.5, f32[128,4]{0,1:T(4,128)S(1)} %copy-done), kind=kOutput, calls=%fused_computation.49 | convolution fusion | flops 25165824 | bytes 1116160 | tf_op jit(solution)/shard_map/bias/jkc,ch->hkj/dot_general | solution.py:273
  15.0 3.3 %collective-permute-start.3 = (f32[4,32,64]{1,0,2:T(4,128)S(1)}, f32[4,32,64]{1,0,2:T(4,128)S(1)}, u32[]{:S(2)}, u32[]{:S(2)}) collective-permute-start(f32[4,32,64]{1,0,2:T(4,128)S(1)} %get-tuple-element.12), channel_id=1, source_target_pairs={{0,16},{1,17},{2,18},{3,19},{4,20},{5,21},{6,22},{7,23},{8,24},{9,... | collective-permute-start | bytes 98312 | tf_op jit(solution)/shard_map/bias/ppermute | solution.py:230
  18.4 0.9 collective-permute-done.3
  20.2 0.7 constant_dynamic-slice_fusion.5
  20.9 2.9 %collective-permute-start.1 = (bf16[8,64,128]{2,1,0:T(8,128)(2,1)S(1)}, bf16[8,64,128]{2,1,0:T(8,128)(2,1)S(1)}, u32[]{:S(2)}, u32[]{:S(2)}) collective-permute-start(bf16[8,64,128]{2,1,0:T(8,128)(2,1)S(1)} %get-tuple-element.20), channel_id=1, source_target_pairs={{0,2},{1,3},{2,0},{3,1},{4,6},{5,7},{6,4},{7,5},{8,10},{9,11},{10,... | collective-permute-start | bytes 393224 | tf_op jit(solution)/shard_map/rows/ppermute | solution.py:230
  23.8 0.7 collective-permute-start.2
  24.5 3.6 %collective-permute-start.5 = (f32[32,128]{1,0:T(8,128)S(1)}, f32[32,128]{1,0:T(8,128)S(1)}, u32[]{:S(2)}, u32[]{:S(2)}) collective-permute-start(f32[32,128]{1,0:T(8,128)S(1)} %get-tuple-element.33), channel_id=1, source_target_pairs={{0,64},{1,65},{2,66},{3,67},{4,128},{5,129},{6,130},{7,131},{8,192... | collective-permute-start | bytes 49160 | tf_op jit(solution)/shard_map/bias/ppermute | solution.py:230
  28.1 4.4 %collective-permute-start.6 = (f32[32,128]{1,0:T(8,128)S(1)}, f32[32,128]{1,0:T(8,128)S(1)}, u32[]{:S(2)}, u32[]{:S(2)}) collective-permute-start(f32[32,128]{1,0:T(8,128)S(1)} %get-tuple-element.32), channel_id=1, source_target_pairs={{0,128},{1,129},{2,130},{3,131},{4,192},{5,193},{6,194},{7,195},{8... | collective-permute-start | bytes 49160 | tf_op jit(solution)/shard_map/bias/ppermute | solution.py:230
  32.6 4.3 %collective-permute-start.7 = (f32[32,128]{1,0:T(8,128)S(1)}, f32[32,128]{1,0:T(8,128)S(1)}, u32[]{:S(2)}, u32[]{:S(2)}) collective-permute-start(f32[32,128]{1,0:T(8,128)S(1)} %get-tuple-element.31), channel_id=1, source_target_pairs={{0,192},{1,193},{2,194},{3,195},{4,0},{5,1},{6,2},{7,3},{8,64},{9,... | collective-permute-start | bytes 49160 | tf_op jit(solution)/shard_map/bias/ppermute | solution.py:230
  36.8 0.9 collective-permute-done.7
  39.1 1.9 stack_rows.2
  41.0 1.7 broadcast_in_dim.9
  42.8 6.5 %all-to-all-start = ((f32[8,128,128]{2,1,0:T(8,128)}), f32[8,128,128]{2,1,0:T(8,128)S(1)}, u32[]{:S(2)}, u32[]{:S(2)}) async-start(f32[8,128,128]{2,1,0:T(8,128)} %broadcast_in_dim.9), calls=%async_computation | async-start | bytes 1048576 | tf_op jit(solution)/shard_map/bias/all_to_all | solution.py:291
  49.4 0.7 constant_dynamic-slice_fusion
  50.1 1.4 collective-permute-start.18
  51.5 2.1 collective-permute-start.19
  53.5 1.2 collective-permute-start.20
  54.7 6.6 %collective-permute-done.18.refs_1_ = bf16[8,64,128]{2,1,0:T(8,128)(2,1)S(1)} collective-permute-done((bf16[8,64,128]{2,1,0:T(8,128)(2,1)S(1)}, bf16[8,64,128]{2,1,0:T(8,128)(2,1)S(1)}, u32[]{:S(2)}, u32[]{:S(2)}) %collective-permute-start.18) | collective-permute-done | bytes 131104 | tf_op jit(solution)/shard_map/rows/ppermute | solution.py:230
  61.4 5.8 %collective-permute-done.19.refs_2_ = bf16[8,64,128]{2,1,0:T(8,128)(2,1)S(1)} collective-permute-done((bf16[8,64,128]{2,1,0:T(8,128)(2,1)S(1)}, bf16[8,64,128]{2,1,0:T(8,128)(2,1)S(1)}, u32[]{:S(2)}, u32[]{:S(2)}) %collective-permute-start.19) | collective-permute-done | bytes 131104 | tf_op jit(solution)/shard_map/rows/ppermute | solution.py:230
  68.1 1.9 stack_rows.3
  70.1 1.0 collective-permute-start.9
  71.1 4.0 %collective-permute-start.11 = (f32[8,128,128]{2,1,0:T(8,128)}, f32[8,128,128]{2,1,0:T(8,128)S(1)}, u32[]{:S(2)}, u32[]{:S(2)}) collective-permute-start(f32[8,128,128]{2,1,0:T(8,128)} %copy-done.1), channel_id=1, source_target_pairs={{0,128},{1,129},{2,130},{3,131},{4,132},{5,133},{6,134},{7,135},{8... | collective-permute-start | bytes 1572872 | tf_op jit(solution)/shard_map/bias/ppermute | solution.py:230
  75.0 1.8 collective-permute-start.13
  76.8 8.3 %collective-permute-start.8 = (f32[8,128,128]{2,1,0:T(8,128)}, f32[8,128,128]{2,1,0:T(8,128)S(1)}, u32[]{:S(2)}, u32[]{:S(2)}) collective-permute-start(f32[8,128,128]{2,1,0:T(8,128)} %copy-done.1), channel_id=1, source_target_pairs={{0,16},{1,17},{2,18},{3,19},{4,20},{5,21},{6,22},{7,23},{8,24},{9,... | collective-permute-start | bytes 1572872 | tf_op jit(solution)/shard_map/bias/ppermute | solution.py:230
  85.1 8.3 %collective-permute-start.10 = (f32[8,128,128]{2,1,0:T(8,128)S(1)}, f32[8,128,128]{2,1,0:T(8,128)S(1)}, u32[]{:S(2)}, u32[]{:S(2)}) collective-permute-start(f32[8,128,128]{2,1,0:T(8,128)S(1)} %collective-permute-done.9.b10), channel_id=1, source_target_pairs={{0,16},{1,17},{2,18},{3,19},{4,20},{5,21},{6,22},{7,23},{8,24},{9,... | collective-permute-start | bytes 1572872 | tf_op jit(solution)/shard_map/bias/ppermute | solution.py:230
  93.5 5.6 %collective-permute-start.12 = (f32[8,128,128]{2,1,0:T(8,128)S(1)}, f32[8,128,128]{2,1,0:T(8,128)S(1)}, u32[]{:S(2)}, u32[]{:S(2)}) collective-permute-start(f32[8,128,128]{2,1,0:T(8,128)S(1)} %collective-permute-done.11.b20), channel_id=1, source_target_pairs={{0,16},{1,17},{2,18},{3,19},{4,20},{5,21},{6,22},{7,23},{8,24},{9,... | collective-permute-start | bytes 1572872 | tf_op jit(solution)/shard_map/bias/ppermute | solution.py:230
  99.7 1.6 collective-permute-done.12.b21
  101.5 1.0 copy-done.2
  102.6 34.5 %attention.2 = bf16[4,8,64,128]{3,2,1,0:T(8,128)(2,1)S(1)} custom-call(s32[4]{0:T(128)S(1)} %pad_add_fusion.at, bf16[4,4,8,64,128]{4,3,2,1,0:T(8,128)(2,1)} %bitcast.70, f32[8,128,128]{2,1,0:T(8,128)S(1)} %copy-done.2, f32[8,128,128]{2,1,0:T(8,128)S(1)} %collective-permute-done.8.b01, f32[8,128,128]{2,1,0:T(8,128)S(1)} %collective-permute-done.9.b10, ...), custom_call_target="tpu_custom_call" | custom-call | flops 2400000000 | bytes 8388608 | tf_op jit(solution)/shard_map/attention/pallas_call | solution.py:162
  137.1 0.8 copy-done.4
  138.0 7.6 %collective-permute-start.15 = (bf16[8,64,128]{2,1,0:T(8,128)(2,1)S(1)}, bf16[8,64,128]{2,1,0:T(8,128)(2,1)S(1)}, u32[]{:S(2)}, u32[]{:S(2)}) collective-permute-start(bf16[8,64,128]{2,1,0:T(8,128)(2,1)S(1)} %get-tuple-element.28), channel_id=1, source_target_pairs={{0,3},{1,0},{2,1},{3,2},{4,7},{5,4},{6,5},{7,6},{8,11},{9,8},{10,9... | collective-permute-start | bytes 393224 | tf_op jit(solution)/shard_map/update/ppermute | solution.py:230
  145.6 1.2 broadcast_in_dim.8
  146.9 0.7 fusion.7
  148.1 0.7 constant_dynamic-update-slice_fusion.12
  148.8 8.8 %collective-permute-done.16 = bf16[8,64,128]{2,1,0:T(8,128)(2,1)S(1)} collective-permute-done((bf16[8,64,128]{2,1,0:T(8,128)(2,1)S(1)}, bf16[8,64,128]{2,1,0:T(8,128)(2,1)S(1)}, u32[]{:S(2)}, u32[]{:S(2)}) %collective-permute-start.16) | collective-permute-done | bytes 131104 | tf_op jit(solution)/shard_map/update/ppermute | solution.py:230
  157.6 0.7 constant_dynamic-update-slice_fusion.11
  158.3 0.7 constant_dynamic-update-slice_fusion.10
  159.0 1.0 copy-done.5
  160.0 34.5 %attention.3 = bf16[4,8,64,128]{3,2,1,0:T(8,128)(2,1)S(1)} custom-call(s32[4]{0:T(128)S(1)} %pad_add_fusion.at, bf16[4,4,8,64,128]{4,3,2,1,0:T(8,128)(2,1)} %bitcast.71, f32[8,128,128]{2,1,0:T(8,128)S(1)} %copy-done.3, f32[8,128,128]{2,1,0:T(8,128)S(1)} %collective-permute-done.8.b01, f32[8,128,128]{2,1,0:T(8,128)S(1)} %collective-permute-done.9.b10, ...), custom_call_target="tpu_custom_call" | custom-call | flops 2400000000 | bytes 8388608 | tf_op jit(solution)/shard_map/attention/pallas_call | solution.py:162
  195.9 1.4 collective-permute-start.23
  197.3 2.3 %collective-permute-done.21 = bf16[8,64,128]{2,1,0:T(8,128)(2,1)S(1)} collective-permute-done((bf16[8,64,128]{2,1,0:T(8,128)(2,1)S(1)}, bf16[8,64,128]{2,1,0:T(8,128)(2,1)S(1)}, u32[]{:S(2)}, u32[]{:S(2)}) %collective-permute-start.21) | collective-permute-done | bytes 131104 | tf_op jit(solution)/shard_map/update/ppermute | solution.py:230
  199.6 0.7 constant_dynamic-update-slice_fusion.9
  200.2 6.5 %collective-permute-done.22 = bf16[8,64,128]{2,1,0:T(8,128)(2,1)S(1)} collective-permute-done((bf16[8,64,128]{2,1,0:T(8,128)(2,1)S(1)}, bf16[8,64,128]{2,1,0:T(8,128)(2,1)S(1)}, u32[]{:S(2)}, u32[]{:S(2)}) %collective-permute-start.22) | collective-permute-done | bytes 131104 | tf_op jit(solution)/shard_map/update/ppermute | solution.py:230
  206.7 0.7 constant_dynamic-update-slice_fusion.8
  207.4 0.7 constant_dynamic-update-slice_fusion.7
  (94 shorter events, 6.5 us)
Async XLA Ops:
  6.5 5.7 %copy-start = (f32[128,4]{0,1:T(4,128)S(1)}, f32[128,4]{0,1:T(4,128)}, u32[]{:S(2)}) copy-start(f32[128,4]{0,1:T(4,128)} %param.19) | copy-start | bytes 6148
  6.5 4.4 %copy-start.9 = (bf16[64,64,128]{2,1,0:T(8,128)(2,1)S(1)}, bf16[64,64,128]{2,1,0:T(8,128)(2,1)}, u32[]{:S(2)}) copy-start(bf16[64,64,128]{2,1,0:T(8,128)(2,1)} %param.11) | copy-start | bytes 3145732
  6.5 4.4 %copy-start.21 = (f32[128]{0:T(128)S(1)}, f32[128]{0:T(128)}, u32[]{:S(2)}) copy-start(f32[128]{0:T(128)} %param.12) | copy-start | bytes 1540
  6.5 4.4 %copy-start.20 = (f32[128]{0:T(128)S(1)}, f32[128]{0:T(128)}, u32[]{:S(2)}) copy-start(f32[128]{0:T(128)} %param.13) | copy-start | bytes 1540
  6.5 95.0 %all-gather.5.cloned.1.call-start = ((), (), s32[]{:S(2)}) async-start(), calls=%async_computation.1 | async-start | bytes 2621440 | tf_op jit(solution)/shard_map/rows/all_gather | solution.py:270
  15.0 4.3 %collective-permute-start.3 = (f32[4,32,64]{1,0,2:T(4,128)S(1)}, f32[4,32,64]{1,0,2:T(4,128)S(1)}, u32[]{:S(2)}, u32[]{:S(2)}) collective-permute-start(f32[4,32,64]{1,0,2:T(4,128)S(1)} %get-tuple-element.12), channel_id=1, source_target_pairs={{0,16},{1,17},{2,18},{3,19},{4,20},{5,21},{6,22},{7,23},{8,24},{9,... | collective-permute-start | bytes 98312 | tf_op jit(solution)/shard_map/bias/ppermute | solution.py:230
  19.5 8.6 %collective-permute-start.4 = (f32[32,128]{1,0:T(8,128)S(1)}, f32[32,128]{1,0:T(8,128)S(1)}, u32[]{:S(2)}, u32[]{:S(2)}) collective-permute-start(f32[32,128]{1,0:T(8,128)S(1)} %get-tuple-element.34), channel_id=1, source_target_pairs={{0,0},{1,1},{2,2},{3,3},{4,64},{5,65},{6,66},{7,67},{8,128},{9,129... | collective-permute-start | bytes 49160 | tf_op jit(solution)/shard_map/bias/ppermute | solution.py:230
  20.9 17.5 %collective-permute-start = (bf16[8,64,128]{2,1,0:T(8,128)(2,1)S(1)}, bf16[8,64,128]{2,1,0:T(8,128)(2,1)S(1)}, u32[]{:S(2)}, u32[]{:S(2)}) collective-permute-start(bf16[8,64,128]{2,1,0:T(8,128)(2,1)S(1)} %get-tuple-element.21), channel_id=1, source_target_pairs={{0,1},{1,2},{2,3},{3,0},{4,5},{5,6},{6,7},{7,4},{8,9},{9,10},{10,1... | collective-permute-start | bytes 393224 | tf_op jit(solution)/shard_map/rows/ppermute | solution.py:230
  20.9 17.5 %collective-permute-start.1 = (bf16[8,64,128]{2,1,0:T(8,128)(2,1)S(1)}, bf16[8,64,128]{2,1,0:T(8,128)(2,1)S(1)}, u32[]{:S(2)}, u32[]{:S(2)}) collective-permute-start(bf16[8,64,128]{2,1,0:T(8,128)(2,1)S(1)} %get-tuple-element.20), channel_id=1, source_target_pairs={{0,2},{1,3},{2,0},{3,1},{4,6},{5,7},{6,4},{7,5},{8,10},{9,11},{10,... | collective-permute-start | bytes 393224 | tf_op jit(solution)/shard_map/rows/ppermute | solution.py:230
  23.8 14.6 %collective-permute-start.2 = (bf16[8,64,128]{2,1,0:T(8,128)(2,1)S(1)}, bf16[8,64,128]{2,1,0:T(8,128)(2,1)S(1)}, u32[]{:S(2)}, u32[]{:S(2)}) collective-permute-start(bf16[8,64,128]{2,1,0:T(8,128)(2,1)S(1)} %get-tuple-element.19), channel_id=1, source_target_pairs={{0,3},{1,0},{2,1},{3,2},{4,7},{5,4},{6,5},{7,6},{8,11},{9,8},{10,9... | collective-permute-start | bytes 393224 | tf_op jit(solution)/shard_map/rows/ppermute | solution.py:230
  24.5 8.1 %collective-permute-start.5 = (f32[32,128]{1,0:T(8,128)S(1)}, f32[32,128]{1,0:T(8,128)S(1)}, u32[]{:S(2)}, u32[]{:S(2)}) collective-permute-start(f32[32,128]{1,0:T(8,128)S(1)} %get-tuple-element.33), channel_id=1, source_target_pairs={{0,64},{1,65},{2,66},{3,67},{4,128},{5,129},{6,130},{7,131},{8,192... | collective-permute-start | bytes 49160 | tf_op jit(solution)/shard_map/bias/ppermute | solution.py:230
  28.1 8.7 %collective-permute-start.6 = (f32[32,128]{1,0:T(8,128)S(1)}, f32[32,128]{1,0:T(8,128)S(1)}, u32[]{:S(2)}, u32[]{:S(2)}) collective-permute-start(f32[32,128]{1,0:T(8,128)S(1)} %get-tuple-element.32), channel_id=1, source_target_pairs={{0,128},{1,129},{2,130},{3,131},{4,192},{5,193},{6,194},{7,195},{8... | collective-permute-start | bytes 49160 | tf_op jit(solution)/shard_map/bias/ppermute | solution.py:230
  32.6 5.1 %collective-permute-start.7 = (f32[32,128]{1,0:T(8,128)S(1)}, f32[32,128]{1,0:T(8,128)S(1)}, u32[]{:S(2)}, u32[]{:S(2)}) collective-permute-start(f32[32,128]{1,0:T(8,128)S(1)} %get-tuple-element.31), channel_id=1, source_target_pairs={{0,192},{1,193},{2,194},{3,195},{4,0},{5,1},{6,2},{7,3},{8,64},{9,... | collective-permute-start | bytes 49160 | tf_op jit(solution)/shard_map/bias/ppermute | solution.py:230
  38.3 0.6 copy-start.10
  38.4 0.7 copy-start.11
  38.4 0.7 copy-start.12
  42.7 56.4 %copy-start.19 = (f32[128]{0:T(128)S(1)}, f32[128]{0:T(128)}, u32[]{:S(2)}) copy-start(f32[128]{0:T(128)} %param.18) | copy-start | bytes 1540
  42.7 56.5 %copy-start.16 = (bf16[128,128]{1,0:T(8,128)(2,1)S(1)}, bf16[128,128]{1,0:T(8,128)(2,1)}, u32[]{:S(2)}) copy-start(bf16[128,128]{1,0:T(8,128)(2,1)} %param.16) | copy-start | bytes 98308
  42.7 56.6 %copy-start.17 = (bf16[128,128]{1,0:T(8,128)(2,1)S(1)}, bf16[128,128]{1,0:T(8,128)(2,1)}, u32[]{:S(2)}) copy-start(bf16[128,128]{1,0:T(8,128)(2,1)} %param.14) | copy-start | bytes 98308
  42.7 56.8 %copy-start.18 = (bf16[128,128]{1,0:T(8,128)(2,1)S(1)}, bf16[128,128]{1,0:T(8,128)(2,1)}, u32[]{:S(2)}) copy-start(bf16[128,128]{1,0:T(8,128)(2,1)} %param.17) | copy-start | bytes 98308
  42.7 58.8 %copy-start.6 = (bf16[128,128]{1,0:T(8,128)(2,1)S(1)}, bf16[128,128]{1,0:T(8,128)(2,1)}, u32[]{:S(2)}) copy-start(bf16[128,128]{1,0:T(8,128)(2,1)} %w_key.3) | copy-start | bytes 98308
  42.7 58.8 %copy-start.7 = (bf16[128,128]{1,0:T(8,128)(2,1)S(1)}, bf16[128,128]{1,0:T(8,128)(2,1)}, u32[]{:S(2)}) copy-start(bf16[128,128]{1,0:T(8,128)(2,1)} %w_out.3) | copy-start | bytes 98308
  42.8 58.8 %copy-start.8 = (f32[128]{0:T(128)S(1)}, f32[128]{0:T(128)}, u32[]{:S(2)}) copy-start(f32[128]{0:T(128)} %param.21) | copy-start | bytes 1540
  42.8 24.5 %all-to-all-start = ((f32[8,128,128]{2,1,0:T(8,128)}), f32[8,128,128]{2,1,0:T(8,128)S(1)}, u32[]{:S(2)}, u32[]{:S(2)}) async-start(f32[8,128,128]{2,1,0:T(8,128)} %broadcast_in_dim.9), calls=%async_computation | async-start | bytes 1048576 | tf_op jit(solution)/shard_map/bias/all_to_all | solution.py:291
  49.3 109.7 %all-gather.7.cloned.1.call-start = ((), (), s32[]{:S(2)}) async-start(), calls=%async_computation.2 | async-start | bytes 2621440 | tf_op jit(solution)/shard_map/rows/all_gather | solution.py:270
  50.1 11.3 %collective-permute-start.18 = (bf16[8,64,128]{2,1,0:T(8,128)(2,1)S(1)}, bf16[8,64,128]{2,1,0:T(8,128)(2,1)S(1)}, u32[]{:S(2)}, u32[]{:S(2)}) collective-permute-start(bf16[8,64,128]{2,1,0:T(8,128)(2,1)S(1)} %get-tuple-element.17), channel_id=1, source_target_pairs={{0,1},{1,2},{2,3},{3,0},{4,5},{5,6},{6,7},{7,4},{8,9},{9,10},{10,1... | collective-permute-start | bytes 393224 | tf_op jit(solution)/shard_map/rows/ppermute | solution.py:230
  51.5 15.8 %collective-permute-start.19 = (bf16[8,64,128]{2,1,0:T(8,128)(2,1)S(1)}, bf16[8,64,128]{2,1,0:T(8,128)(2,1)S(1)}, u32[]{:S(2)}, u32[]{:S(2)}) collective-permute-start(bf16[8,64,128]{2,1,0:T(8,128)(2,1)S(1)} %get-tuple-element.16), channel_id=1, source_target_pairs={{0,2},{1,3},{2,0},{3,1},{4,6},{5,7},{6,4},{7,5},{8,10},{9,11},{10,... | collective-permute-start | bytes 393224 | tf_op jit(solution)/shard_map/rows/ppermute | solution.py:230
  53.5 13.7 %collective-permute-start.20 = (bf16[8,64,128]{2,1,0:T(8,128)(2,1)S(1)}, bf16[8,64,128]{2,1,0:T(8,128)(2,1)S(1)}, u32[]{:S(2)}, u32[]{:S(2)}) collective-permute-start(bf16[8,64,128]{2,1,0:T(8,128)(2,1)S(1)} %get-tuple-element.15), channel_id=1, source_target_pairs={{0,3},{1,0},{2,1},{3,2},{4,7},{5,4},{6,5},{7,6},{8,11},{9,8},{10,9... | collective-permute-start | bytes 393224 | tf_op jit(solution)/shard_map/rows/ppermute | solution.py:230
  61.4 5.9 %copy-start.13 = (bf16[8,64,128]{2,1,0:T(8,128)(2,1)}, bf16[8,64,128]{2,1,0:T(8,128)(2,1)S(1)}, u32[]{:S(2)}) copy-start(bf16[8,64,128]{2,1,0:T(8,128)(2,1)S(1)} %collective-permute-done.18.refs_1_) | copy-start | bytes 393220
  67.2 0.7 copy-start.15
  67.2 0.9 copy-start.1
  70.1 15.1 %collective-permute-start.9 = (f32[8,128,128]{2,1,0:T(8,128)}, f32[8,128,128]{2,1,0:T(8,128)S(1)}, u32[]{:S(2)}, u32[]{:S(2)}) collective-permute-start(f32[8,128,128]{2,1,0:T(8,128)} %copy-done.1), channel_id=1, source_target_pairs={{0,64},{1,65},{2,66},{3,67},{4,68},{5,69},{6,70},{7,71},{8,72},{9,... | collective-permute-start | bytes 1572872 | tf_op jit(solution)/shard_map/bias/ppermute | solution.py:230
  71.1 22.4 %collective-permute-start.11 = (f32[8,128,128]{2,1,0:T(8,128)}, f32[8,128,128]{2,1,0:T(8,128)S(1)}, u32[]{:S(2)}, u32[]{:S(2)}) collective-permute-start(f32[8,128,128]{2,1,0:T(8,128)} %copy-done.1), channel_id=1, source_target_pairs={{0,128},{1,129},{2,130},{3,131},{4,132},{5,133},{6,134},{7,135},{8... | collective-permute-start | bytes 1572872 | tf_op jit(solution)/shard_map/bias/ppermute | solution.py:230
  75.0 24.1 %collective-permute-start.13 = (f32[8,128,128]{2,1,0:T(8,128)}, f32[8,128,128]{2,1,0:T(8,128)S(1)}, u32[]{:S(2)}, u32[]{:S(2)}) collective-permute-start(f32[8,128,128]{2,1,0:T(8,128)} %copy-done.1), channel_id=1, source_target_pairs={{0,192},{1,193},{2,194},{3,195},{4,196},{5,197},{6,198},{7,199},{8... | collective-permute-start | bytes 1572872 | tf_op jit(solution)/shard_map/bias/ppermute | solution.py:230
  76.8 22.9 %collective-permute-start.8 = (f32[8,128,128]{2,1,0:T(8,128)}, f32[8,128,128]{2,1,0:T(8,128)S(1)}, u32[]{:S(2)}, u32[]{:S(2)}) collective-permute-start(f32[8,128,128]{2,1,0:T(8,128)} %copy-done.1), channel_id=1, source_target_pairs={{0,16},{1,17},{2,18},{3,19},{4,20},{5,21},{6,22},{7,23},{8,24},{9,... | collective-permute-start | bytes 1572872 | tf_op jit(solution)/shard_map/bias/ppermute | solution.py:230
  85.1 14.6 %collective-permute-start.10 = (f32[8,128,128]{2,1,0:T(8,128)S(1)}, f32[8,128,128]{2,1,0:T(8,128)S(1)}, u32[]{:S(2)}, u32[]{:S(2)}) collective-permute-start(f32[8,128,128]{2,1,0:T(8,128)S(1)} %collective-permute-done.9.b10), channel_id=1, source_target_pairs={{0,16},{1,17},{2,18},{3,19},{4,20},{5,21},{6,22},{7,23},{8,24},{9,... | collective-permute-start | bytes 1572872 | tf_op jit(solution)/shard_map/bias/ppermute | solution.py:230
  93.5 7.9 %collective-permute-start.12 = (f32[8,128,128]{2,1,0:T(8,128)S(1)}, f32[8,128,128]{2,1,0:T(8,128)S(1)}, u32[]{:S(2)}, u32[]{:S(2)}) collective-permute-start(f32[8,128,128]{2,1,0:T(8,128)S(1)} %collective-permute-done.11.b20), channel_id=1, source_target_pairs={{0,16},{1,17},{2,18},{3,19},{4,20},{5,21},{6,22},{7,23},{8,24},{9,... | collective-permute-start | bytes 1572872 | tf_op jit(solution)/shard_map/bias/ppermute | solution.py:230
  99.1 2.4 %collective-permute-start.14 = (f32[8,128,128]{2,1,0:T(8,128)S(1)}, f32[8,128,128]{2,1,0:T(8,128)}, u32[]{:S(2)}, u32[]{:S(2)}) collective-permute-start(f32[8,128,128]{2,1,0:T(8,128)S(1)} %collective-permute-done.13.b30), channel_id=1, source_target_pairs={{0,16},{1,17},{2,18},{3,19},{4,20},{5,21},{6,22},{7,23},{8,24},{9,... | collective-permute-start | bytes 1572872 | tf_op jit(solution)/shard_map/bias/ppermute | solution.py:230
  101.5 1.0 copy-start.2
  137.1 0.8 copy-start.4
  137.9 21.0 %copy-start.3 = (f32[8,128,128]{2,1,0:T(8,128)S(1)}, f32[8,128,128]{2,1,0:T(8,128)}, u32[]{:S(2)}) copy-start(f32[8,128,128]{2,1,0:T(8,128)} %copy-done.1) | copy-start | bytes 1572868
  138.0 10.2 %collective-permute-start.15 = (bf16[8,64,128]{2,1,0:T(8,128)(2,1)S(1)}, bf16[8,64,128]{2,1,0:T(8,128)(2,1)S(1)}, u32[]{:S(2)}, u32[]{:S(2)}) collective-permute-start(bf16[8,64,128]{2,1,0:T(8,128)(2,1)S(1)} %get-tuple-element.28), channel_id=1, source_target_pairs={{0,3},{1,0},{2,1},{3,2},{4,7},{5,4},{6,5},{7,6},{8,11},{9,8},{10,9... | collective-permute-start | bytes 393224 | tf_op jit(solution)/shard_map/update/ppermute | solution.py:230
  145.5 12.1 %collective-permute-start.16 = (bf16[8,64,128]{2,1,0:T(8,128)(2,1)S(1)}, bf16[8,64,128]{2,1,0:T(8,128)(2,1)S(1)}, u32[]{:S(2)}, u32[]{:S(2)}) collective-permute-start(bf16[8,64,128]{2,1,0:T(8,128)(2,1)S(1)} %get-tuple-element.27), channel_id=1, source_target_pairs={{0,2},{1,3},{2,0},{3,1},{4,6},{5,7},{6,4},{7,5},{8,10},{9,11},{10,... | collective-permute-start | bytes 393224 | tf_op jit(solution)/shard_map/update/ppermute | solution.py:230
  147.5 10.8 %collective-permute-start.17 = (bf16[8,64,128]{2,1,0:T(8,128)(2,1)S(1)}, bf16[8,64,128]{2,1,0:T(8,128)(2,1)S(1)}, u32[]{:S(2)}, u32[]{:S(2)}) collective-permute-start(bf16[8,64,128]{2,1,0:T(8,128)(2,1)S(1)} %get-tuple-element.26), channel_id=1, source_target_pairs={{0,1},{1,2},{2,3},{3,0},{4,5},{5,6},{6,7},{7,4},{8,9},{9,10},{10,1... | collective-permute-start | bytes 393224 | tf_op jit(solution)/shard_map/update/ppermute | solution.py:230
  159.0 1.0 copy-start.5
  194.6 5.0 %collective-permute-start.21 = (bf16[8,64,128]{2,1,0:T(8,128)(2,1)S(1)}, bf16[8,64,128]{2,1,0:T(8,128)(2,1)S(1)}, u32[]{:S(2)}, u32[]{:S(2)}) collective-permute-start(bf16[8,64,128]{2,1,0:T(8,128)(2,1)S(1)} %get-tuple-element.25), channel_id=1, source_target_pairs={{0,3},{1,0},{2,1},{3,2},{4,7},{5,4},{6,5},{7,6},{8,11},{9,8},{10,9... | collective-permute-start | bytes 393224 | tf_op jit(solution)/shard_map/update/ppermute | solution.py:230
  194.7 12.1 %collective-permute-start.22 = (bf16[8,64,128]{2,1,0:T(8,128)(2,1)S(1)}, bf16[8,64,128]{2,1,0:T(8,128)(2,1)S(1)}, u32[]{:S(2)}, u32[]{:S(2)}) collective-permute-start(bf16[8,64,128]{2,1,0:T(8,128)(2,1)S(1)} %get-tuple-element.24), channel_id=1, source_target_pairs={{0,2},{1,3},{2,0},{3,1},{4,6},{5,7},{6,4},{7,5},{8,10},{9,11},{10,... | collective-permute-start | bytes 393224 | tf_op jit(solution)/shard_map/update/ppermute | solution.py:230
  195.9 11.4 %collective-permute-start.23 = (bf16[8,64,128]{2,1,0:T(8,128)(2,1)S(1)}, bf16[8,64,128]{2,1,0:T(8,128)(2,1)S(1)}, u32[]{:S(2)}, u32[]{:S(2)}) collective-permute-start(bf16[8,64,128]{2,1,0:T(8,128)(2,1)S(1)} %get-tuple-element.23), channel_id=1, source_target_pairs={{0,1},{1,2},{2,3},{3,0},{4,5},{5,6},{6,7},{7,4},{8,9},{9,10},{10,1... | collective-permute-start | bytes 393224 | tf_op jit(solution)/shard_map/update/ppermute | solution.py:230
  (1 other events, 0.6 us)
Sparse Core Ops, SparseCore 0:
  41.2 37.8 all-gather.4
  80.9 33.4 all-gather.6

commit v3 on v2

--- a/solution.py
+++ b/solution.py
@@ -11,7 +11,7 @@
 
 F32 = jnp.float32
 BF = jnp.bfloat16
-CHUNKS = 2
+CHUNKS = ((0, 12), (12, 4))
 TOGETHER = 2
 DEPTH = 32
 
@@ -214,6 +214,25 @@
     )(*pieces, after)
 
 
+def assemble_kernel(at, *refs):
+    *blocks, out = refs
+    for i, block in enumerate(blocks):
+        chunk, step = divmod(i, 4)
+        start = lax.rem(at[2] + step, 4) * 16 + CHUNKS[chunk][0]
+        out[pl.ds(start, CHUNKS[chunk][1])] = block[...]
+
+
+def assemble(at, blocks):
+    return pl.pallas_call(
+        assemble_kernel,
+        out_shape=jax.ShapeDtypeStruct((64, 64, 128), BF),
+        in_specs=[pl.BlockSpec(memory_space=pltpu.SMEM)]
+        + [pl.BlockSpec(memory_space=pltpu.VMEM)] * len(blocks),
+        out_specs=pl.BlockSpec(memory_space=pltpu.VMEM),
+        name="assemble_update",
+    )(at, *blocks)
+
+
 AXES = ("y", "zh", "core", "x", "zl")
 
 
@@ -254,14 +273,12 @@
     y, core, x, zl = (lax.axis_index(name) for name in ("y", "core", "x", "zl"))
     place = jnp.stack([y, x, zl, core]).astype(jnp.int32)
     normed = normalize(pair, norm_gain, norm_shift)
-    count = 16 // CHUNKS
-
     def exchange(normed, chunk, after):
         with jax.named_scope("rows"):
             pieces = []
             for step in range(4):
                 part = lax.dynamic_slice_in_dim(
-                    normed, (zl + step) % 4 * 16 + chunk * count, count, 0
+                    normed, (zl + step) % 4 * 16 + CHUNKS[chunk][0], CHUNKS[chunk][1], 0
                 )
                 if step:
                     part = move(part, lambda y, z, core, x: (y, turn(z, step), core, x))
@@ -275,9 +292,7 @@
         )
         kept = lax.dynamic_slice_in_dim(tile, core * 32, 32, 1)
         sent = lax.dynamic_slice_in_dim(tile, (1 - core) * 32, 32, 1)
-        kept, sent, normed = lax.optimization_barrier((kept, sent, normed))
         got = swap_cores(sent)
-        normed0 = normed
         tile = jnp.where(
             core == 0, jnp.concatenate([kept, got], 2), jnp.concatenate([got, kept], 2)
         )
@@ -287,7 +302,6 @@
             rounds.append(move(part, lambda y, z, core, x: (x + step, z, core, y)))
         rounds = jnp.stack(rounds + rounds[:3])
         block = lax.dynamic_slice_in_dim(rounds, (y - x) % 4, 4, 0).reshape(128, 128)
-        block, normed = lax.optimization_barrier((block, normed))
         along_z = lax.all_to_all(
             jnp.broadcast_to(block[None], (8, 128, 128)),
             ("zh", "zl"),
@@ -295,7 +309,7 @@
             concat_axis=0,
             tiled=True,
         )
-    rows = [exchange(normed0, 0, block)]
+    rows = [exchange(normed, 0, block)]
     with jax.named_scope("bias"):
         biases = []
         for step in range(4):
@@ -303,10 +317,10 @@
             if step:
                 here = move(along_z, lambda y, z, core, x: (y + step, z, core, x))
             biases.append((here, swap_cores(here)))
-    for chunk in range(1, CHUNKS):
+    for chunk in range(1, len(CHUNKS)):
         rows.append(exchange(normed, chunk, along_z))
-    result = jnp.zeros(pair.shape, BF)
-    for chunk in range(CHUNKS):
+    blocks = []
+    for chunk in range(len(CHUNKS)):
         with jax.named_scope("attention"):
             part = attend(
                 place,
@@ -325,10 +339,8 @@
                 back = part[step]
                 if step:
                     back = move(back, lambda y, z, core, x: (y, turn(z, -step), core, x))
-                result = lax.dynamic_update_slice_in_dim(
-                    result, back, (zl + step) % 4 * 16 + chunk * count, 0
-                )
-    return result
+                blocks.append(back)
+    return assemble(place, blocks)
 
 
 def solution(mesh):

time: 215 us -> 223 us (1.037)
  waiting for transfers between devices: 34 us -> 55.1 us
  starting transfers between devices: 70.2 us -> 60 us
  local copies, waits for them, and re-layouts: 15.7 us -> 8.16 us
  Pallas kernels: 72.9 us -> 75.3 us
    ppermute x24, waiting for transfers between devices: 34 us -> 52.8 us  [move(): return lax.ppermute(array, AXES, pairs)]
    ppermute x24, starting transfers between devices: 63.6 us -> 51.7 us  [move(): return lax.ppermute(array, AXES, pairs)]
    dynamic_update_slice x8 -> x0, local copies, waits for them, and re-layouts: 5.32 us -> none  [on_device(): lax.dynamic_update_slice_in_dim(result, back, (zl + step) % 4 * 16 + chun...]
    pallas_call x0 -> x1, Pallas kernels: none -> 2.31 us  [assemble(): pl.pallas_call(assemble_kernel, out_shape=jax.ShapeDtypeStruct((64, 64, 1...]
    all_to_all x1, waiting for transfers between devices: 0.01 us -> 2.27 us  [on_device(): lax.all_to_all(jnp.broadcast_to(block[None], (8, 128, 128)), ('zh', 'zl')...]
    unnamed x53 -> x65, local copies, waits for them, and re-layouts: 4.85 us -> 4.02 us
  transfers between devices with their start and end apart: 27 -> 27, of which waited for: 10 -> 16; matrix products, arithmetic and copies ran while one was open for 5% -> 1% of each run, Pallas kernels for 17% -> 9%
where the time goes in v3:
time: 223 us; the launch traced here: 221 us
  Pallas kernels  75.3 us (34%)
  starting transfers between devices  60 us (27%)
  waiting for transfers between devices  55.1 us (25%)
  between operations  13.9 us (6%)
  local copies, waits for them, and re-layouts  8.16 us (4%)
  other arithmetic  5.75 us (3%)
  matrix products  2.53 us (1%)
    pallas_call x2, Pallas kernels, attend(): pl.pallas_call(attend_kernel, out_shape=jax.ShapeDtypeStruct((4, count, 6...  69.2 us
    ppermute x24, waiting for transfers between devices, move(): return lax.ppermute(array, AXES, pairs)  52.8 us
    ppermute x24, starting transfers between devices, move(): return lax.ppermute(array, AXES, pairs)  51.7 us
    all_to_all x1, starting transfers between devices, on_device(): lax.all_to_all(jnp.broadcast_to(block[None], (8, 128, 128)), ('zh', 'zl')...  8.19 us
  transfers between devices with their start and end apart: 27, of which 16 were waited for; matrix products, arithmetic and copies ran while one was open for 1% of the time, Pallas kernels for 9%

profile of v3, /device:TPU:1, one launch (start us, length us, event | category | flops | bytes accessed | tf_op | source)
XLA Modules:
  0.0 220.7 jit_solution(17097772508715159068)
XLA Ops:
  6.5 1.9 convert_reduce_fusion
  8.5 2.3 %fusion.2 = f32[64,64]{1,0:T(8,128)S(1)} fusion(bf16[64,64,128]{2,1,0:T(8,128)(2,1)} %param.11, f32[64,64]{1,0:T(8,128)S(1)} %broadcast_multiply_fusion), kind=kLoop, calls=%fused_computation.4 | loop fusion | flops 2093056 | bytes 1081344 | tf_op jit(solution)/shard_map/reduce_sum | solution.py:196
  10.9 1.3 fusion.5
  12.2 2.5 %fusion.6 = f32[64,64,4]{1,2,0:T(4,128)S(1)} fusion(bf16[64,64,128]{2,1,0:T(8,128)(2,1)S(1)} %fusion.5, f32[128,4]{0,1:T(4,128)S(1)} %copy-done), kind=kOutput, calls=%fused_computation.41 | convolution fusion | flops 25165824 | bytes 1116160 | tf_op jit(solution)/shard_map/bias/jkc,ch->hkj/dot_general | solution.py:290
  14.9 3.3 %collective-permute-start.3 = (f32[4,32,64]{1,0,2:T(4,128)S(1)}, f32[4,32,64]{1,0,2:T(4,128)S(1)}, u32[]{:S(2)}, u32[]{:S(2)}) collective-permute-start(f32[4,32,64]{1,0,2:T(4,128)S(1)} %get-tuple-element.22), channel_id=1, source_target_pairs={{0,16},{1,17},{2,18},{3,19},{4,20},{5,21},{6,22},{7,23},{8,24},{9,... | collective-permute-start | bytes 98312 | tf_op jit(solution)/shard_map/bias/ppermute | solution.py:249
  18.3 0.9 collective-permute-done.3
  20.2 2.0 collective-permute-start.5
  22.1 4.4 %collective-permute-start.6 = (f32[32,128]{1,0:T(8,128)S(1)}, f32[32,128]{1,0:T(8,128)S(1)}, u32[]{:S(2)}, u32[]{:S(2)}) collective-permute-start(f32[32,128]{1,0:T(8,128)S(1)} %get-tuple-element.24), channel_id=1, source_target_pairs={{0,128},{1,129},{2,130},{3,131},{4,192},{5,193},{6,194},{7,195},{8... | collective-permute-start | bytes 49160 | tf_op jit(solution)/shard_map/bias/ppermute | solution.py:249
  26.6 1.9 collective-permute-start.7
  28.6 2.4 %collective-permute-done.7 = f32[32,128]{1,0:T(8,128)S(1)} collective-permute-done((f32[32,128]{1,0:T(8,128)S(1)}, f32[32,128]{1,0:T(8,128)S(1)}, u32[]{:S(2)}, u32[]{:S(2)}) %collective-permute-start.7) | collective-permute-done | bytes 16416 | tf_op jit(solution)/shard_map/bias/ppermute | solution.py:249
  31.0 0.8 broadcast_in_dim.6
  31.9 8.2 %all-to-all-start = ((f32[8,128,128]{2,1,0:T(8,128)}), f32[8,128,128]{2,1,0:T(8,128)S(1)}, u32[]{:S(2)}, u32[]{:S(2)}) async-start(f32[8,128,128]{2,1,0:T(8,128)} %broadcast_in_dim.6), calls=%async_computation | async-start | bytes 1048576 | tf_op jit(solution)/shard_map/bias/all_to_all | solution.py:305
  40.8 1.3 collective-permute-start.18
  42.1 2.1 collective-permute-start.19
  44.2 1.2 collective-permute-start.20
  45.4 5.2 %collective-permute-done.18.refs_1_ = bf16[4,64,128]{2,1,0:T(8,128)(2,1)S(1)} collective-permute-done((bf16[4,64,128]{2,1,0:T(8,128)(2,1)S(1)}, bf16[4,64,128]{2,1,0:T(8,128)(2,1)S(1)}, u32[]{:S(2)}, u32[]{:S(2)}) %collective-permute-start.18) | collective-permute-done | bytes 65568 | tf_op jit(solution)/shard_map/rows/ppermute | solution.py:249
  50.6 1.6 collective-permute-done.19.refs_2_
  52.2 0.7 collective-permute-done.20.refs_3_
  52.9 2.3 %all-to-all-done.b00.refs_4_ = f32[8,128,128]{2,1,0:T(8,128)S(1)} async-done(((f32[8,128,128]{2,1,0:T(8,128)}), f32[8,128,128]{2,1,0:T(8,128)S(1)}, u32[]{:S(2)}, u32[]{:S(2)}) %all-to-all-start) | async-done | bytes 524320 | tf_op jit(solution)/shard_map/bias/all_to_all | solution.py:305
  55.2 0.8 copy-done.1
  56.0 1.6 stack_rows.3
  57.8 0.8 constant_dynamic-slice_fusion.5
  58.6 2.7 %collective-permute-start = (bf16[12,64,128]{2,1,0:T(8,128)(2,1)S(1)}, bf16[12,64,128]{2,1,0:T(8,128)(2,1)S(1)}, u32[]{:S(2)}, u32[]{:S(2)}) collective-permute-start(bf16[12,64,128]{2,1,0:T(8,128)(2,1)S(1)} %get-tuple-element.11), channel_id=1, source_target_pairs={{0,1},{1,2},{2,3},{3,0},{4,5},{5,6},{6,7},{7,4},{8,9},{9,10},{10,1... | collective-permute-start | bytes 589832 | tf_op jit(solution)/shard_map/rows/ppermute | solution.py:249
  61.3 3.2 %collective-permute-start.1 = (bf16[12,64,128]{2,1,0:T(8,128)(2,1)S(1)}, bf16[12,64,128]{2,1,0:T(8,128)(2,1)S(1)}, u32[]{:S(2)}, u32[]{:S(2)}) collective-permute-start(bf16[12,64,128]{2,1,0:T(8,128)(2,1)S(1)} %get-tuple-element.10), channel_id=1, source_target_pairs={{0,2},{1,3},{2,0},{3,1},{4,6},{5,7},{6,4},{7,5},{8,10},{9,11},{10,... | collective-permute-start | bytes 589832 | tf_op jit(solution)/shard_map/rows/ppermute | solution.py:249
  64.5 2.9 %collective-permute-done.refs_1_ = bf16[12,64,128]{2,1,0:T(8,128)(2,1)S(1)} collective-permute-done((bf16[12,64,128]{2,1,0:T(8,128)(2,1)S(1)}, bf16[12,64,128]{2,1,0:T(8,128)(2,1)S(1)}, u32[]{:S(2)}, u32[]{:S(2)}) %collective-permute-start) | collective-permute-done | bytes 196640 | tf_op jit(solution)/shard_map/rows/ppermute | solution.py:249
  67.4 10.7 %collective-permute-done.1.refs_2_ = bf16[12,64,128]{2,1,0:T(8,128)(2,1)S(1)} collective-permute-done((bf16[12,64,128]{2,1,0:T(8,128)(2,1)S(1)}, bf16[12,64,128]{2,1,0:T(8,128)(2,1)S(1)}, u32[]{:S(2)}, u32[]{:S(2)}) %collective-permute-start.1) | collective-permute-done | bytes 196640 | tf_op jit(solution)/shard_map/rows/ppermute | solution.py:249
  78.2 0.7 copy-done.14
  78.9 2.2 stack_rows.2
  81.2 3.4 %collective-permute-start.11 = (f32[8,128,128]{2,1,0:T(8,128)S(1)}, f32[8,128,128]{2,1,0:T(8,128)S(1)}, u32[]{:S(2)}, u32[]{:S(2)}) collective-permute-start(f32[8,128,128]{2,1,0:T(8,128)S(1)} %copy-done.2), channel_id=1, source_target_pairs={{0,128},{1,129},{2,130},{3,131},{4,132},{5,133},{6,134},{7,135},{8... | collective-permute-start | bytes 1572872 | tf_op jit(solution)/shard_map/bias/ppermute | solution.py:249
  84.6 1.3 collective-permute-start.13
  85.9 1.3 collective-permute-start.8
  87.2 8.2 %collective-permute-done.9.b10 = f32[8,128,128]{2,1,0:T(8,128)S(1)} collective-permute-done((f32[8,128,128]{2,1,0:T(8,128)S(1)}, f32[8,128,128]{2,1,0:T(8,128)S(1)}, u32[]{:S(2)}, u32[]{:S(2)}) %collective-permute-start.9) | collective-permute-done | bytes 524320 | tf_op jit(solution)/shard_map/bias/ppermute | solution.py:249
  95.4 1.5 collective-permute-start.10
  96.9 10.5 %collective-permute-done.11.b20 = f32[8,128,128]{2,1,0:T(8,128)S(1)} collective-permute-done((f32[8,128,128]{2,1,0:T(8,128)S(1)}, f32[8,128,128]{2,1,0:T(8,128)S(1)}, u32[]{:S(2)}, u32[]{:S(2)}) %collective-permute-start.11) | collective-permute-done | bytes 524320 | tf_op jit(solution)/shard_map/bias/ppermute | solution.py:249
  107.4 1.3 collective-permute-start.12
  109.3 1.1 collective-permute-done.12.b21
  110.4 0.7 collective-permute-done.14.b31
  111.2 1.2 copy-done.4
  112.4 18.2 %attention.3 = bf16[4,4,64,128]{3,2,1,0:T(8,128)(2,1)S(1)} custom-call(s32[4]{0:T(128)S(1)} %pad_add_fusion.at, bf16[4,4,4,64,128]{4,3,2,1,0:T(8,128)(2,1)S(1)} %bitcast.61, f32[8,128,128]{2,1,0:T(8,128)S(1)} %copy-done.2, f32[8,128,128]{2,1,0:T(8,128)S(1)} %collective-permute-done.8.b01, f32[8,128,128]{2,1,0:T(8,128)S(1)} %collective-permute-done.9.b10, ...), custom_call_target="tpu_custom_call" | custom-call | flops 1200000000 | bytes 4194304 | tf_op jit(solution)/shard_map/attention/pallas_call | solution.py:162
  130.6 51.0 %attention.2 = bf16[4,12,64,128]{3,2,1,0:T(8,128)(2,1)S(1)} custom-call(s32[4]{0:T(128)S(1)} %pad_add_fusion.at, bf16[4,4,12,64,128]{4,3,2,1,0:T(8,128)(2,1)} %bitcast.67, f32[8,128,128]{2,1,0:T(8,128)S(1)} %copy-done.2, f32[8,128,128]{2,1,0:T(8,128)S(1)} %collective-permute-done.8.b01, f32[8,128,128]{2,1,0:T(8,128)S(1)} %collective-permute-done.9.b10, ...), custom_call_target="tpu_custom_call" | custom-call | flops 3600000000 | bytes 12582912 | tf_op jit(solution)/shard_map/attention/pallas_call | solution.py:162
  181.6 0.7 slice_bitcast_fusion
  182.3 2.5 %collective-permute-start.15 = (bf16[12,64,128]{2,1,0:T(8,128)(2,1)S(1)}, bf16[12,64,128]{2,1,0:T(8,128)(2,1)S(1)}, u32[]{:S(2)}, u32[]{:S(2)}) collective-permute-start(bf16[12,64,128]{2,1,0:T(8,128)(2,1)S(1)} %get-tuple-element.15), channel_id=1, source_target_pairs={{0,3},{1,0},{2,1},{3,2},{4,7},{5,4},{6,5},{7,6},{8,11},{9,8},{10,9... | collective-permute-start | bytes 589832 | tf_op jit(solution)/shard_map/update/ppermute | solution.py:249
  184.8 3.1 %collective-permute-start.16 = (bf16[12,64,128]{2,1,0:T(8,128)(2,1)S(1)}, bf16[12,64,128]{2,1,0:T(8,128)(2,1)S(1)}, u32[]{:S(2)}, u32[]{:S(2)}) collective-permute-start(bf16[12,64,128]{2,1,0:T(8,128)(2,1)S(1)} %get-tuple-element.14), channel_id=1, source_target_pairs={{0,2},{1,3},{2,0},{3,1},{4,6},{5,7},{6,4},{7,5},{8,10},{9,11},{10,... | collective-permute-start | bytes 589832 | tf_op jit(solution)/shard_map/update/ppermute | solution.py:249
  188.5 3.3 %collective-permute-start.21 = (bf16[4,64,128]{2,1,0:T(8,128)(2,1)S(1)}, bf16[4,64,128]{2,1,0:T(8,128)(2,1)S(1)}, u32[]{:S(2)}, u32[]{:S(2)}) collective-permute-start(bf16[4,64,128]{2,1,0:T(8,128)(2,1)S(1)} %get-tuple-element.19), channel_id=1, source_target_pairs={{0,3},{1,0},{2,1},{3,2},{4,7},{5,4},{6,5},{7,6},{8,11},{9,8},{10,9... | collective-permute-start | bytes 196616 | tf_op jit(solution)/shard_map/update/ppermute | solution.py:249
  191.8 6.5 %collective-permute-done.21.refs_5_ = bf16[4,64,128]{2,1,0:T(8,128)(2,1)S(1)} collective-permute-done((bf16[4,64,128]{2,1,0:T(8,128)(2,1)S(1)}, bf16[4,64,128]{2,1,0:T(8,128)(2,1)S(1)}, u32[]{:S(2)}, u32[]{:S(2)}) %collective-permute-start.21) | collective-permute-done | bytes 65568 | tf_op jit(solution)/shard_map/update/ppermute | solution.py:249
  198.3 11.1 %collective-permute-start.23 = (bf16[4,64,128]{2,1,0:T(8,128)(2,1)S(1)}, bf16[4,64,128]{2,1,0:T(8,128)(2,1)S(1)}, u32[]{:S(2)}, u32[]{:S(2)}) collective-permute-start(bf16[4,64,128]{2,1,0:T(8,128)(2,1)S(1)} %get-tuple-element.17), channel_id=1, source_target_pairs={{0,1},{1,2},{2,3},{3,0},{4,5},{5,6},{6,7},{7,4},{8,9},{9,10},{10,1... | collective-permute-start | bytes 196616 | tf_op jit(solution)/shard_map/update/ppermute | solution.py:249
  209.3 1.1 collective-permute-done.22.refs_6_
  211.5 2.3 %assemble_update.1 = bf16[64,64,128]{2,1,0:T(8,128)(2,1)} custom-call(s32[4]{0:T(128)} %copy-done.3, bf16[12,64,128]{2,1,0:T(8,128)(2,1)} %get-tuple-element.16.refs_0_, bf16[12,64,128]{2,1,0:T(8,128)(2,1)} %copy-done.10, bf16[12,64,128]{2,1,0:T(8,128)(2,1)} %copy-done.11, bf16[12,64,128]{2,1,0:T(8,128)(2,1)} %copy-done.12, ...), custom_call_target="tpu_custom_call" | custom-call | tf_op jit(solution)/shard_map/assemble_update/pallas_call | solution.py:226
  (98 shorter events, 4.6 us)
Async XLA Ops:
  6.5 5.6 %copy-start = (f32[128,4]{0,1:T(4,128)S(1)}, f32[128,4]{0,1:T(4,128)}, u32[]{:S(2)}) copy-start(f32[128,4]{0,1:T(4,128)} %param.19) | copy-start | bytes 6148
  6.5 4.3 %copy-start.8 = (bf16[64,64,128]{2,1,0:T(8,128)(2,1)S(1)}, bf16[64,64,128]{2,1,0:T(8,128)(2,1)}, u32[]{:S(2)}) copy-start(bf16[64,64,128]{2,1,0:T(8,128)(2,1)} %param.11) | copy-start | bytes 3145732
  6.5 4.3 %copy-start.27 = (f32[128]{0:T(128)S(1)}, f32[128]{0:T(128)}, u32[]{:S(2)}) copy-start(f32[128]{0:T(128)} %param.12) | copy-start | bytes 1540
  6.5 4.3 %copy-start.26 = (f32[128]{0:T(128)S(1)}, f32[128]{0:T(128)}, u32[]{:S(2)}) copy-start(f32[128]{0:T(128)} %param.13) | copy-start | bytes 1540
  14.9 4.3 %collective-permute-start.3 = (f32[4,32,64]{1,0,2:T(4,128)S(1)}, f32[4,32,64]{1,0,2:T(4,128)S(1)}, u32[]{:S(2)}, u32[]{:S(2)}) collective-permute-start(f32[4,32,64]{1,0,2:T(4,128)S(1)} %get-tuple-element.22), channel_id=1, source_target_pairs={{0,16},{1,17},{2,18},{3,19},{4,20},{5,21},{6,22},{7,23},{8,24},{9,... | collective-permute-start | bytes 98312 | tf_op jit(solution)/shard_map/bias/ppermute | solution.py:249
  19.5 9.0 %collective-permute-start.4 = (f32[32,128]{1,0:T(8,128)S(1)}, f32[32,128]{1,0:T(8,128)S(1)}, u32[]{:S(2)}, u32[]{:S(2)}) collective-permute-start(f32[32,128]{1,0:T(8,128)S(1)} %get-tuple-element.26), channel_id=1, source_target_pairs={{0,0},{1,1},{2,2},{3,3},{4,64},{5,65},{6,66},{7,67},{8,128},{9,129... | collective-permute-start | bytes 49160 | tf_op jit(solution)/shard_map/bias/ppermute | solution.py:249
  20.2 8.3 %collective-permute-start.5 = (f32[32,128]{1,0:T(8,128)S(1)}, f32[32,128]{1,0:T(8,128)S(1)}, u32[]{:S(2)}, u32[]{:S(2)}) collective-permute-start(f32[32,128]{1,0:T(8,128)S(1)} %get-tuple-element.25), channel_id=1, source_target_pairs={{0,64},{1,65},{2,66},{3,67},{4,128},{5,129},{6,130},{7,131},{8,192... | collective-permute-start | bytes 49160 | tf_op jit(solution)/shard_map/bias/ppermute | solution.py:249
  22.1 6.5 %collective-permute-start.6 = (f32[32,128]{1,0:T(8,128)S(1)}, f32[32,128]{1,0:T(8,128)S(1)}, u32[]{:S(2)}, u32[]{:S(2)}) collective-permute-start(f32[32,128]{1,0:T(8,128)S(1)} %get-tuple-element.24), channel_id=1, source_target_pairs={{0,128},{1,129},{2,130},{3,131},{4,192},{5,193},{6,194},{7,195},{8... | collective-permute-start | bytes 49160 | tf_op jit(solution)/shard_map/bias/ppermute | solution.py:249
  26.6 4.4 %collective-permute-start.7 = (f32[32,128]{1,0:T(8,128)S(1)}, f32[32,128]{1,0:T(8,128)S(1)}, u32[]{:S(2)}, u32[]{:S(2)}) collective-permute-start(f32[32,128]{1,0:T(8,128)S(1)} %get-tuple-element.23), channel_id=1, source_target_pairs={{0,192},{1,193},{2,194},{3,195},{4,0},{5,1},{6,2},{7,3},{8,64},{9,... | collective-permute-start | bytes 49160 | tf_op jit(solution)/shard_map/bias/ppermute | solution.py:249
  31.0 27.6 %copy-start.9 = (f32[4,32,128]{2,1,0:T(8,128)}, f32[4,32,128]{2,1,0:T(8,128)S(1)}, u32[]{:S(2)}) copy-start(f32[4,32,128]{2,1,0:T(8,128)S(1)} %constant_dynamic-slice_fusion.4) | copy-start | bytes 196612
  31.9 23.3 %all-to-all-start = ((f32[8,128,128]{2,1,0:T(8,128)}), f32[8,128,128]{2,1,0:T(8,128)S(1)}, u32[]{:S(2)}, u32[]{:S(2)}) async-start(f32[8,128,128]{2,1,0:T(8,128)} %broadcast_in_dim.6), calls=%async_computation | async-start | bytes 1048576 | tf_op jit(solution)/shard_map/bias/all_to_all | solution.py:305
  40.0 71.1 %all-gather.7.cloned.1.call-start = ((), (), s32[]{:S(2)}) async-start(), calls=%async_computation.2 | async-start | bytes 1310720 | tf_op jit(solution)/shard_map/rows/all_gather | solution.py:287
  40.8 9.8 %collective-permute-start.18 = (bf16[4,64,128]{2,1,0:T(8,128)(2,1)S(1)}, bf16[4,64,128]{2,1,0:T(8,128)(2,1)S(1)}, u32[]{:S(2)}, u32[]{:S(2)}) collective-permute-start(bf16[4,64,128]{2,1,0:T(8,128)(2,1)S(1)} %get-tuple-element.7), channel_id=1, source_target_pairs={{0,1},{1,2},{2,3},{3,0},{4,5},{5,6},{6,7},{7,4},{8,9},{9,10},{10,1... | collective-permute-start | bytes 196616 | tf_op jit(solution)/shard_map/rows/ppermute | solution.py:249
  42.1 10.1 %collective-permute-start.19 = (bf16[4,64,128]{2,1,0:T(8,128)(2,1)S(1)}, bf16[4,64,128]{2,1,0:T(8,128)(2,1)S(1)}, u32[]{:S(2)}, u32[]{:S(2)}) collective-permute-start(bf16[4,64,128]{2,1,0:T(8,128)(2,1)S(1)} %get-tuple-element.6), channel_id=1, source_target_pairs={{0,2},{1,3},{2,0},{3,1},{4,6},{5,7},{6,4},{7,5},{8,10},{9,11},{10,... | collective-permute-start | bytes 196616 | tf_op jit(solution)/shard_map/rows/ppermute | solution.py:249
  44.2 8.7 %collective-permute-start.20 = (bf16[4,64,128]{2,1,0:T(8,128)(2,1)S(1)}, bf16[4,64,128]{2,1,0:T(8,128)(2,1)S(1)}, u32[]{:S(2)}, u32[]{:S(2)}) collective-permute-start(bf16[4,64,128]{2,1,0:T(8,128)(2,1)S(1)} %get-tuple-element.5), channel_id=1, source_target_pairs={{0,3},{1,0},{2,1},{3,2},{4,7},{5,4},{6,5},{7,6},{8,11},{9,8},{10,9... | collective-permute-start | bytes 196616 | tf_op jit(solution)/shard_map/rows/ppermute | solution.py:249
  50.6 4.6 %copy-start.19 = (bf16[4,64,128]{2,1,0:T(8,128)(2,1)}, bf16[4,64,128]{2,1,0:T(8,128)(2,1)S(1)}, u32[]{:S(2)}) copy-start(bf16[4,64,128]{2,1,0:T(8,128)(2,1)S(1)} %collective-permute-done.18.refs_1_) | copy-start | bytes 196612
  52.2 3.0 %copy-start.20 = (bf16[4,64,128]{2,1,0:T(8,128)(2,1)}, bf16[4,64,128]{2,1,0:T(8,128)(2,1)S(1)}, u32[]{:S(2)}) copy-start(bf16[4,64,128]{2,1,0:T(8,128)(2,1)S(1)} %collective-permute-done.19.refs_2_) | copy-start | bytes 196612
  52.9 2.3 %copy-start.21 = (bf16[4,64,128]{2,1,0:T(8,128)(2,1)}, bf16[4,64,128]{2,1,0:T(8,128)(2,1)S(1)}, u32[]{:S(2)}) copy-start(bf16[4,64,128]{2,1,0:T(8,128)(2,1)S(1)} %collective-permute-done.20.refs_3_) | copy-start | bytes 196612
  57.6 23.5 %copy-start.2 = (f32[8,128,128]{2,1,0:T(8,128)S(1)}, f32[8,128,128]{2,1,0:T(8,128)}, u32[]{:S(2)}) copy-start(f32[8,128,128]{2,1,0:T(8,128)} %copy-done.1) | copy-start | bytes 1572868
  57.6 51.1 %copy-start.25 = (f32[128]{0:T(128)S(1)}, f32[128]{0:T(128)}, u32[]{:S(2)}) copy-start(f32[128]{0:T(128)} %param.18) | copy-start | bytes 1540
  57.7 51.2 %copy-start.22 = (bf16[128,128]{1,0:T(8,128)(2,1)S(1)}, bf16[128,128]{1,0:T(8,128)(2,1)}, u32[]{:S(2)}) copy-start(bf16[128,128]{1,0:T(8,128)(2,1)} %param.16) | copy-start | bytes 98308
  57.7 51.3 %copy-start.23 = (bf16[128,128]{1,0:T(8,128)(2,1)S(1)}, bf16[128,128]{1,0:T(8,128)(2,1)}, u32[]{:S(2)}) copy-start(bf16[128,128]{1,0:T(8,128)(2,1)} %param.14) | copy-start | bytes 98308
  57.7 72.9 %all-gather.5.cloned.1.call-start = ((), (), s32[]{:S(2)}) async-start(), calls=%async_computation.1 | async-start | bytes 3932160 | tf_op jit(solution)/shard_map/rows/all_gather | solution.py:287
  57.8 51.3 %copy-start.24 = (bf16[128,128]{1,0:T(8,128)(2,1)S(1)}, bf16[128,128]{1,0:T(8,128)(2,1)}, u32[]{:S(2)}) copy-start(bf16[128,128]{1,0:T(8,128)(2,1)} %param.17) | copy-start | bytes 98308
  57.8 53.4 %copy-start.5 = (bf16[128,128]{1,0:T(8,128)(2,1)S(1)}, bf16[128,128]{1,0:T(8,128)(2,1)}, u32[]{:S(2)}) copy-start(bf16[128,128]{1,0:T(8,128)(2,1)} %w_key.3) | copy-start | bytes 98308
  57.8 53.4 %copy-start.6 = (bf16[128,128]{1,0:T(8,128)(2,1)S(1)}, bf16[128,128]{1,0:T(8,128)(2,1)}, u32[]{:S(2)}) copy-start(bf16[128,128]{1,0:T(8,128)(2,1)} %w_out.3) | copy-start | bytes 98308
  57.8 53.4 %copy-start.7 = (f32[128]{0:T(128)S(1)}, f32[128]{0:T(128)}, u32[]{:S(2)}) copy-start(f32[128]{0:T(128)} %param.21) | copy-start | bytes 1540
  58.6 8.9 %collective-permute-start = (bf16[12,64,128]{2,1,0:T(8,128)(2,1)S(1)}, bf16[12,64,128]{2,1,0:T(8,128)(2,1)S(1)}, u32[]{:S(2)}, u32[]{:S(2)}) collective-permute-start(bf16[12,64,128]{2,1,0:T(8,128)(2,1)S(1)} %get-tuple-element.11), channel_id=1, source_target_pairs={{0,1},{1,2},{2,3},{3,0},{4,5},{5,6},{6,7},{7,4},{8,9},{9,10},{10,1... | collective-permute-start | bytes 589832 | tf_op jit(solution)/shard_map/rows/ppermute | solution.py:249
  61.3 16.9 %collective-permute-start.1 = (bf16[12,64,128]{2,1,0:T(8,128)(2,1)S(1)}, bf16[12,64,128]{2,1,0:T(8,128)(2,1)S(1)}, u32[]{:S(2)}, u32[]{:S(2)}) collective-permute-start(bf16[12,64,128]{2,1,0:T(8,128)(2,1)S(1)} %get-tuple-element.10), channel_id=1, source_target_pairs={{0,2},{1,3},{2,0},{3,1},{4,6},{5,7},{6,4},{7,5},{8,10},{9,11},{10,... | collective-permute-start | bytes 589832 | tf_op jit(solution)/shard_map/rows/ppermute | solution.py:249
  64.5 13.7 %collective-permute-start.2 = (bf16[12,64,128]{2,1,0:T(8,128)(2,1)S(1)}, bf16[12,64,128]{2,1,0:T(8,128)(2,1)S(1)}, u32[]{:S(2)}, u32[]{:S(2)}) collective-permute-start(bf16[12,64,128]{2,1,0:T(8,128)(2,1)S(1)} %get-tuple-element.9), channel_id=1, source_target_pairs={{0,3},{1,0},{2,1},{3,2},{4,7},{5,4},{6,5},{7,6},{8,11},{9,8},{10,9... | collective-permute-start | bytes 589832 | tf_op jit(solution)/shard_map/rows/ppermute | solution.py:249
  67.4 10.7 %copy-start.13 = (bf16[12,64,128]{2,1,0:T(8,128)(2,1)}, bf16[12,64,128]{2,1,0:T(8,128)(2,1)S(1)}, u32[]{:S(2)}) copy-start(bf16[12,64,128]{2,1,0:T(8,128)(2,1)S(1)} %collective-permute-done.refs_1_) | copy-start | bytes 589828
  81.1 14.3 %collective-permute-start.9 = (f32[8,128,128]{2,1,0:T(8,128)S(1)}, f32[8,128,128]{2,1,0:T(8,128)S(1)}, u32[]{:S(2)}, u32[]{:S(2)}) collective-permute-start(f32[8,128,128]{2,1,0:T(8,128)S(1)} %copy-done.2), channel_id=1, source_target_pairs={{0,64},{1,65},{2,66},{3,67},{4,68},{5,69},{6,70},{7,71},{8,72},{9,... | collective-permute-start | bytes 1572872 | tf_op jit(solution)/shard_map/bias/ppermute | solution.py:249
  81.2 26.2 %collective-permute-start.11 = (f32[8,128,128]{2,1,0:T(8,128)S(1)}, f32[8,128,128]{2,1,0:T(8,128)S(1)}, u32[]{:S(2)}, u32[]{:S(2)}) collective-permute-start(f32[8,128,128]{2,1,0:T(8,128)S(1)} %copy-done.2), channel_id=1, source_target_pairs={{0,128},{1,129},{2,130},{3,131},{4,132},{5,133},{6,134},{7,135},{8... | collective-permute-start | bytes 1572872 | tf_op jit(solution)/shard_map/bias/ppermute | solution.py:249
  84.6 24.1 %collective-permute-start.13 = (f32[8,128,128]{2,1,0:T(8,128)S(1)}, f32[8,128,128]{2,1,0:T(8,128)S(1)}, u32[]{:S(2)}, u32[]{:S(2)}) collective-permute-start(f32[8,128,128]{2,1,0:T(8,128)S(1)} %copy-done.2), channel_id=1, source_target_pairs={{0,192},{1,193},{2,194},{3,195},{4,196},{5,197},{6,198},{7,199},{8... | collective-permute-start | bytes 1572872 | tf_op jit(solution)/shard_map/bias/ppermute | solution.py:249
  85.9 23.4 %collective-permute-start.8 = (f32[8,128,128]{2,1,0:T(8,128)S(1)}, f32[8,128,128]{2,1,0:T(8,128)S(1)}, u32[]{:S(2)}, u32[]{:S(2)}) collective-permute-start(f32[8,128,128]{2,1,0:T(8,128)S(1)} %copy-done.2), channel_id=1, source_target_pairs={{0,16},{1,17},{2,18},{3,19},{4,20},{5,21},{6,22},{7,23},{8,24},{9,... | collective-permute-start | bytes 1572872 | tf_op jit(solution)/shard_map/bias/ppermute | solution.py:249
  95.4 13.9 %collective-permute-start.10 = (f32[8,128,128]{2,1,0:T(8,128)S(1)}, f32[8,128,128]{2,1,0:T(8,128)}, u32[]{:S(2)}, u32[]{:S(2)}) collective-permute-start(f32[8,128,128]{2,1,0:T(8,128)S(1)} %collective-permute-done.9.b10), channel_id=1, source_target_pairs={{0,16},{1,17},{2,18},{3,19},{4,20},{5,21},{6,22},{7,23},{8,24},{9,... | collective-permute-start | bytes 1572872 | tf_op jit(solution)/shard_map/bias/ppermute | solution.py:249
  107.4 3.0 %collective-permute-start.12 = (f32[8,128,128]{2,1,0:T(8,128)S(1)}, f32[8,128,128]{2,1,0:T(8,128)}, u32[]{:S(2)}, u32[]{:S(2)}) collective-permute-start(f32[8,128,128]{2,1,0:T(8,128)S(1)} %collective-permute-done.11.b20), channel_id=1, source_target_pairs={{0,16},{1,17},{2,18},{3,19},{4,20},{5,21},{6,22},{7,23},{8,24},{9,... | collective-permute-start | bytes 1572872 | tf_op jit(solution)/shard_map/bias/ppermute | solution.py:249
  108.7 2.4 %collective-permute-start.14 = (f32[8,128,128]{2,1,0:T(8,128)S(1)}, f32[8,128,128]{2,1,0:T(8,128)}, u32[]{:S(2)}, u32[]{:S(2)}) collective-permute-start(f32[8,128,128]{2,1,0:T(8,128)S(1)} %collective-permute-done.13.b30), channel_id=1, source_target_pairs={{0,16},{1,17},{2,18},{3,19},{4,20},{5,21},{6,22},{7,23},{8,24},{9,... | collective-permute-start | bytes 1572872 | tf_op jit(solution)/shard_map/bias/ppermute | solution.py:249
  109.3 21.3 %copy-start.3 = (s32[4]{0:T(128)}, s32[4]{0:T(128)S(1)}, u32[]{:S(2)}) copy-start(s32[4]{0:T(128)S(1)} %pad_add_fusion.at) | copy-start | bytes 52
  111.1 1.2 copy-start.4
  182.3 28.3 %collective-permute-start.15 = (bf16[12,64,128]{2,1,0:T(8,128)(2,1)S(1)}, bf16[12,64,128]{2,1,0:T(8,128)(2,1)S(1)}, u32[]{:S(2)}, u32[]{:S(2)}) collective-permute-start(bf16[12,64,128]{2,1,0:T(8,128)(2,1)S(1)} %get-tuple-element.15), channel_id=1, source_target_pairs={{0,3},{1,0},{2,1},{3,2},{4,7},{5,4},{6,5},{7,6},{8,11},{9,8},{10,9... | collective-permute-start | bytes 589832 | tf_op jit(solution)/shard_map/update/ppermute | solution.py:249
  184.8 25.8 %collective-permute-start.16 = (bf16[12,64,128]{2,1,0:T(8,128)(2,1)S(1)}, bf16[12,64,128]{2,1,0:T(8,128)(2,1)S(1)}, u32[]{:S(2)}, u32[]{:S(2)}) collective-permute-start(bf16[12,64,128]{2,1,0:T(8,128)(2,1)S(1)} %get-tuple-element.14), channel_id=1, source_target_pairs={{0,2},{1,3},{2,0},{3,1},{4,6},{5,7},{6,4},{7,5},{8,10},{9,11},{10,... | collective-permute-start | bytes 589832 | tf_op jit(solution)/shard_map/update/ppermute | solution.py:249
  187.9 22.8 %collective-permute-start.17 = (bf16[12,64,128]{2,1,0:T(8,128)(2,1)S(1)}, bf16[12,64,128]{2,1,0:T(8,128)(2,1)S(1)}, u32[]{:S(2)}, u32[]{:S(2)}) collective-permute-start(bf16[12,64,128]{2,1,0:T(8,128)(2,1)S(1)} %get-tuple-element.13), channel_id=1, source_target_pairs={{0,1},{1,2},{2,3},{3,0},{4,5},{5,6},{6,7},{7,4},{8,9},{9,10},{10,1... | collective-permute-start | bytes 589832 | tf_op jit(solution)/shard_map/update/ppermute | solution.py:249
  188.5 9.7 %collective-permute-start.21 = (bf16[4,64,128]{2,1,0:T(8,128)(2,1)S(1)}, bf16[4,64,128]{2,1,0:T(8,128)(2,1)S(1)}, u32[]{:S(2)}, u32[]{:S(2)}) collective-permute-start(bf16[4,64,128]{2,1,0:T(8,128)(2,1)S(1)} %get-tuple-element.19), channel_id=1, source_target_pairs={{0,3},{1,0},{2,1},{3,2},{4,7},{5,4},{6,5},{7,6},{8,11},{9,8},{10,9... | collective-permute-start | bytes 196616 | tf_op jit(solution)/shard_map/update/ppermute | solution.py:249
  191.8 18.6 %collective-permute-start.22 = (bf16[4,64,128]{2,1,0:T(8,128)(2,1)S(1)}, bf16[4,64,128]{2,1,0:T(8,128)(2,1)S(1)}, u32[]{:S(2)}, u32[]{:S(2)}) collective-permute-start(bf16[4,64,128]{2,1,0:T(8,128)(2,1)S(1)} %get-tuple-element.18), channel_id=1, source_target_pairs={{0,2},{1,3},{2,0},{3,1},{4,6},{5,7},{6,4},{7,5},{8,10},{9,11},{10,... | collective-permute-start | bytes 196616 | tf_op jit(solution)/shard_map/update/ppermute | solution.py:249
  198.3 12.4 %copy-start.16 = (bf16[4,64,128]{2,1,0:T(8,128)(2,1)}, bf16[4,64,128]{2,1,0:T(8,128)(2,1)S(1)}, u32[]{:S(2)}) copy-start(bf16[4,64,128]{2,1,0:T(8,128)(2,1)S(1)} %collective-permute-done.21.refs_5_) | copy-start | bytes 196612
  198.3 12.4 %collective-permute-start.23 = (bf16[4,64,128]{2,1,0:T(8,128)(2,1)S(1)}, bf16[4,64,128]{2,1,0:T(8,128)(2,1)S(1)}, u32[]{:S(2)}, u32[]{:S(2)}) collective-permute-start(bf16[4,64,128]{2,1,0:T(8,128)(2,1)S(1)} %get-tuple-element.17), channel_id=1, source_target_pairs={{0,1},{1,2},{2,3},{3,0},{4,5},{5,6},{6,7},{7,4},{8,9},{9,10},{10,1... | collective-permute-start | bytes 196616 | tf_op jit(solution)/shard_map/update/ppermute | solution.py:249
  210.7 0.8 copy-start.12
  (7 other events, 5.0 us)
Sparse Core Ops, SparseCore 0:
  57.8 26.8 all-gather.6
  86.5 43.3 all-gather.4

commit v4 on v3

v4 whole, which is shorter than its diff:
```python
import functools
import math

import jax
import jax.numpy as jnp
from jax import lax
from jax.experimental import pallas as pl
from jax.experimental.pallas import tpu as pltpu
from jax.sharding import Mesh
from jax.sharding import PartitionSpec as P

F32 = jnp.float32
BF = jnp.bfloat16
TOGETHER = 2
DEPTH = 32


def dot(a, b):
    return jnp.dot(a, b, preferred_element_type=F32)


def dot_t(a, b):
    return lax.dot_general(a, b, (((1,), (1,)), ((), ())), preferred_element_type=F32)


def fold(function, so_far, value):
    return value if so_far is None else function(so_far, value)


def places(at):
    y, x, zl, core = at[0], at[1], at[2], at[3]
    slot = [lax.rem(zl + 4 - part, 4) for part in range(4)]
    halves = [pl.multiple_of(lax.rem(core + half, 2) * 32, 32) for half in range(2)]
    z_of = [[zh * 4 + lax.rem(zl + 4 - s, 4) for zh in range(2)] for s in range(4)]
    return y, slot, halves, z_of


def attend_heads(heads, bias, z_of, key, query, value, put, score_ref):
    work = [(r, a) for r in range(TOGETHER) for a in range(len(heads))]

    def masked(r, a):
        of_head = lax.broadcasted_iota(jnp.int32, (128, 256), 0) // DEPTH
        read = query(r)
        return jnp.where(of_head == heads[a], read, jnp.zeros_like(read))

    def score(r, a, c, own):
        half, s = divmod(c, 4)
        added = jnp.concatenate([bias(a, half, z) for z in z_of[s]], axis=1)
        return dot(key(r, c), own) + added

    def raise_plain(r, a):
        own, total = masked(r, a), None
        for c in range(8):
            raised = jnp.exp(score(r, a, c, own))
            score_ref[r, a, c] = raised
            total = fold(jnp.add, total, jnp.sum(raised.reshape(16, 8, 256), axis=0))
        return jnp.sum(total, axis=0, keepdims=True)

    def raise_shifted(r, a):
        own, largest, total = masked(r, a), None, None
        for c in range(8):
            scores = score(r, a, c, own)
            score_ref[r, a, c] = scores
            top = jnp.max(scores.reshape(16, 8, 256), axis=0)
            largest = fold(jnp.maximum, largest, top)
        largest = jnp.max(largest, axis=0, keepdims=True)
        for c in range(8):
            raised = jnp.exp(score_ref[r, a, c] - largest)
            score_ref[r, a, c] = raised
            total = fold(jnp.add, total, jnp.sum(raised.reshape(16, 8, 256), axis=0))
        return jnp.sum(total, axis=0, keepdims=True)

    def weigh(r, a, total):
        scale = 1.0 / total
        weights = jnp.concatenate(
            [(score_ref[r, a, c] * scale).astype(BF) for c in range(8)], axis=0
        )
        own = pl.ds(pl.multiple_of(heads[a] * DEPTH, DEPTH), DEPTH)
        put(r, own, dot(value(r, own), weights))

    totals = [raise_plain(r, a) for r, a in work]
    for (r, a), total in zip(work, totals):
        weigh(r, a, total)

    safe = None
    for total in totals:
        inside = jnp.logical_and(total > 2.0**-60, total < 2.0**120)
        safe = fold(jnp.minimum, safe, jnp.where(inside, 1.0, 0.0))

    def again():
        for r, a in work:
            weigh(r, a, raise_shifted(r, a))

    return jnp.min(safe) < 0.5, again


def first_kernel(
    at,
    x0,
    x1,
    x2,
    x3,
    bias_own,
    bias_other,
    w_key,
    w_value_t,
    w_query_t,
    w_gate_t,
    gate_shift,
    key_out,
    value_out,
    query_out,
    gate_out,
    attended_out,
    score_ref,
):
    rows, bias = (x0, x1, x2, x3), (bias_own, bias_other)
    y, slot, halves, z_of = places(at)
    for r in range(TOGETHER):
        tokens = jnp.concatenate(
            [
                rows[t][s, r, pl.ds(halves[half], 32), :]
                for half in range(2)
                for s in range(4)
                for t in range(4)
            ],
            axis=0,
        )
        key_out[r] = dot(tokens, w_key[...]).astype(BF)
        value_out[r] = dot_t(w_value_t[...], tokens).astype(BF)
        tokens = jnp.concatenate([x0[slot[part], r] for part in range(4)], axis=0)
        query = dot_t(w_query_t[...], tokens) * (1.0 / math.sqrt(DEPTH))
        query_out[r] = query.astype(BF)
        gate_out[r] = jax.nn.sigmoid(dot_t(w_gate_t[...], tokens) + gate_shift[...])

    def put(r, own, attended):
        attended_out[r] = attended

    unsafe, again = attend_heads(
        [y],
        lambda a, half, z: bias[half][z],
        z_of,
        lambda r, c: key_out[r, c * 128 : (c + 1) * 128, :],
        lambda r: query_out[r],
        lambda r, own: value_out[r, own, :],
        put,
        score_ref,
    )
    pl.when(unsafe)(again)


def second_kernel(
    at,
    key,
    value,
    query,
    gate,
    attended,
    bias_own,
    bias_other,
    w_out,
    out_shift,
    out,
    attended_ref,
    score_ref,
):
    bias = (bias_own, bias_other)
    y, slot, _, z_of = places(at)
    heads = [lax.rem(y + step, 4) for step in range(1, 4)]
    own = pl.ds(pl.multiple_of(y * DEPTH, DEPTH), DEPTH)
    for r in range(TOGETHER):
        attended_ref[r, own, :] = attended[r]

    def put(r, own, attended):
        attended_ref[r, own, :] = attended

    def finish():
        for r in range(TOGETHER):
            gated = (gate[r] * attended_ref[r]).astype(BF)
            update = lax.dot_general(
                gated, w_out[...], (((0,), (0,)), ((), ())), preferred_element_type=F32
            )
            update = (update + out_shift[...]).astype(BF)
            for part in range(4):
                out[slot[part], r] = update[part * 64 : (part + 1) * 64]

    unsafe, again = attend_heads(
        heads,
        lambda a, half, z: bias[half][heads[a], z],
        z_of,
        lambda r, c: key[r, c * 128 : (c + 1) * 128, :],
        lambda r: query[r],
        lambda r, own: value[r, own, :],
        put,
        score_ref,
    )
    finish()

    @pl.when(unsafe)
    def _():
        again()
        finish()


def call(kernel, name, count, at, operands, outs, scratch, work):
    def spec(shape, dim, first=0):
        if dim is None:
            return pl.BlockSpec(shape, lambda i, at: (0,) * len(shape))
        block = shape[:dim] + (TOGETHER,) + shape[dim + 1 :]
        where = (0,) * dim, (0,) * (len(shape) - dim - 1)
        return pl.BlockSpec(block, lambda i, at: where[0] + (i + first,) + where[1])

    return pl.pallas_call(
        kernel,
        out_shape=[jax.ShapeDtypeStruct(shape, dtype) for shape, dtype, _ in outs],
        grid_spec=pltpu.PrefetchScalarGridSpec(
            num_scalar_prefetch=1,
            grid=(count // TOGETHER,),
            in_specs=[spec(array.shape, *rest) for array, *rest in operands],
            out_specs=[spec(shape, dim) for shape, _, dim in outs],
            scratch_shapes=scratch,
        ),
        compiler_params=pltpu.CompilerParams(
            vmem_limit_bytes=48 << 20, dimension_semantics=("arbitrary",)
        ),
        cost_estimate=pl.CostEstimate(
            flops=count * 300_000_000,
            bytes_accessed=count << 20,
            transcendentals=count * work,
        ),
        name=name,
    )(at, *[array for array, *_ in operands])


def attend_first(at, rows, first, bias, weights):
    count = 8
    operands = [(array, 1, start // TOGETHER) for array, start in zip(rows, first)]
    operands += [(array, None) for array in (*bias, *weights)]
    outs = [
        ((count, 1024, 128), BF, 0),
        ((count, 128, 1024), BF, 0),
        ((count, 128, 256), BF, 0),
        ((count, 128, 256), F32, 0),
        ((count, 32, 256), F32, 0),
    ]
    scratch = [pltpu.VMEM((TOGETHER, 1, 8, 128, 256), F32)]
    return call(
        first_kernel, "project_own_head", count, at, operands, outs, scratch, 1 << 18
    )


def attend_second(at, held, bias, weights):
    count = 8
    operands = [(array, 0) for array in held]
    operands += [(array, None) for array in (*bias, *weights)]
    outs = [((4, count, 64, 128), BF, 1)]
    scratch = [
        pltpu.VMEM((TOGETHER, 128, 256), F32),
        pltpu.VMEM((TOGETHER, 3, 8, 128, 256), F32),
    ]
    return call(
        second_kernel, "other_heads", count, at, operands, outs, scratch, 3 << 18
    )[0]


def normalize(values, gain, shift):
    values = values.astype(F32)
    mean = jnp.mean(values, axis=-1, keepdims=True)
    centred = values - mean
    spread = jnp.mean(centred * centred, axis=-1, keepdims=True)
    return (centred * lax.rsqrt(spread + 1e-05) * gain + shift).astype(BF)


def assemble_kernel(at, *refs):
    *blocks, out = refs
    count = blocks[0].shape[0]
    for i, block in enumerate(blocks):
        chunk, step = divmod(i, 4)
        start = lax.rem(at[2] + step, 4) * 16 + chunk * count
        out[pl.ds(start, count)] = block[...]


def assemble(at, blocks):
    return pl.pallas_call(
        assemble_kernel,
        out_shape=jax.ShapeDtypeStruct((64, 64, 128), BF),
        in_specs=[pl.BlockSpec(memory_space=pltpu.SMEM)]
        + [pl.BlockSpec(memory_space=pltpu.VMEM)] * len(blocks),
        out_specs=pl.BlockSpec(memory_space=pltpu.VMEM),
        name="assemble_update",
    )(at, *blocks)


def tie_kernel(array, *rest):
    pass


def after(array, *earlier):
    return pl.pallas_call(
        tie_kernel,
        out_shape=jax.ShapeDtypeStruct(array.shape, array.dtype),
        in_specs=[pl.BlockSpec(memory_space=pl.ANY)] * (1 + len(earlier)),
        out_specs=pl.BlockSpec(memory_space=pl.ANY),
        input_output_aliases={0: 0},
        name="tie",
    )(array, *earlier)


AXES = ("y", "zh", "core", "x", "zl")


def move(array, to):
    pairs = []
    for source in range(256):
        row, col = divmod(source, 16)
        y, zh, core = row // 4, row // 2 % 2, row % 2
        x, zl = divmod(col, 4)
        y, z, core, x = to(y, zh * 4 + zl, core, x)
        y, z, x = y % 4, z % 8, x % 4
        target = ((y * 2 + z // 4) * 2 + core) * 16 + x * 4 + z % 4
        pairs.append((source, target))
    return lax.ppermute(array, AXES, pairs)


def swap_cores(array):
    return move(array, lambda y, z, core, x: (y, z, 1 - core, x))


def turn(z, step):
    return z // 4 * 4 + (z + step) % 4


def on_device(
    pair,
    norm_gain,
    norm_shift,
    w_query,
    w_key,
    w_value,
    w_gate,
    gate_shift,
    w_bias,
    w_out,
    out_shift,
):
    y, core, x, zl = (lax.axis_index(name) for name in ("y", "core", "x", "zl"))
    place = jnp.stack([y, x, zl, core]).astype(jnp.int32)
    normed = normalize(pair, norm_gain, norm_shift)
    with jax.named_scope("rows"):
        pieces = []
        for step in range(4):
            part = lax.dynamic_slice_in_dim(normed, (zl + step) % 4 * 16, 16, 0)
            if step:
                part = move(part, lambda y, z, core, x: (y, turn(z, step), core, x))
            pieces.append(part)
        here = jnp.stack(pieces)
        below = move(here, lambda y, z, core, x: (y, z, core, x + 1))
        above = move(here, lambda y, z, core, x: (y, z, core, x - 1))
        across = [
            move(below[:, :8], lambda y, z, core, x: (y, z, core, x + 1)),
            move(above[:, 8:], lambda y, z, core, x: (y, z, core, x - 1)),
        ]
        across[0] = after(across[0], across[1])
    with jax.named_scope("bias"):
        tile = jnp.einsum(
            "jkc,ch->hkj", normed.astype(F32), w_bias, precision=lax.Precision.HIGHEST
        )
        kept = lax.dynamic_slice_in_dim(tile, core * 32, 32, 1)
        got = swap_cores(lax.dynamic_slice_in_dim(tile, (1 - core) * 32, 32, 1))
        tile = jnp.where(
            core == 0, jnp.concatenate([kept, got], 2), jnp.concatenate([got, kept], 2)
        )
        rounds = []
        for step in range(4):
            part = lax.dynamic_index_in_dim(tile, (x + step) % 4, 0, keepdims=False)
            rounds.append(move(part, lambda y, z, core, x: (x + step, z, core, y)))
        rounds = jnp.stack(rounds + rounds[:3])
        block = lax.dynamic_slice_in_dim(rounds, (y - x) % 4, 4, 0).reshape(128, 128)
        block = after(block, here)
        along_z = lax.all_to_all(
            jnp.broadcast_to(block[None], (8, 128, 128)),
            ("zh", "zl"),
            split_axis=0,
            concat_axis=0,
            tiled=True,
        )
        own_bias = along_z, swap_cores(along_z)
        whole = lax.all_gather(along_z, "y", axis=0, tiled=False)
    params = (w_key, w_value.T, w_query.T, w_gate.T, gate_shift[:, None])
    blocks = []
    with jax.named_scope("attention"):
        held = [
            attend_first(
                place,
                (here, below, across[chunk], above),
                (8 * chunk, 8 * chunk, 0, 8 * chunk),
                own_bias,
                params,
            )
            for chunk in range(2)
        ]
    with jax.named_scope("bias"):
        whole = after(whole, held[0][4])
        biases = whole, swap_cores(whole)
    for chunk in range(2):
        with jax.named_scope("attention"):
            part = attend_second(place, held[chunk], biases, (w_out, out_shift[None]))
        with jax.named_scope("update"):
            for step in range(4):
                back = part[step]
                if step:
                    back = move(back, lambda y, z, core, x: (y, turn(z, -step), core, x))
                blocks.append(back)
    return assemble(place, blocks)


def solution(mesh):
    parts = Mesh(mesh.devices.reshape(4, 2, 2, 4, 4), AXES)
    tiles = P(("y", "zh", "core"), ("x", "zl"), None)
    return jax.shard_map(
        on_device,
        mesh=parts,
        in_specs=(tiles,) + (P(),) * 10,
        out_specs=tiles,
        check_vma=False,
    )
```

time: 223 us -> 230 us (1.031)
  the two profiles are of different devices: /device:TPU:1 before, /device:TPU:30 now
where the time goes in v4:
time: 230 us; the launch traced here: 229 us
  Pallas kernels  80.4 us (35%)
  waiting for transfers between devices  53.9 us (23%)
  starting transfers between devices  30.3 us (13%)
  blocking collectives  24.7 us (11%)
  local copies, waits for them, and re-layouts  16.7 us (7%)
  between operations  13.9 us (6%)
  other arithmetic  6.85 us (3%)
  matrix products  2.53 us (1%)
    pallas_call x4, Pallas kernels, call(): pl.pallas_call(kernel, out_shape=[jax.ShapeDtypeStruct(shape, dtype) for...  78.1 us
    ppermute x20, waiting for transfers between devices, move(): return lax.ppermute(array, AXES, pairs)  53.9 us
    ppermute x20, starting transfers between devices, move(): return lax.ppermute(array, AXES, pairs)  30.3 us
    all_to_all x1, blocking collectives, on_device(): lax.all_to_all(jnp.broadcast_to(block[None], (8, 128, 128)), ('zh', 'zl')...  24.7 us
    unnamed x87, local copies, waits for them, and re-layouts  11.3 us
  transfers between devices with their start and end apart: 21, of which 9 were waited for; matrix products, arithmetic and copies ran while one was open for 2% of the time, Pallas kernels for 23%

profile of v4, /device:TPU:30, one launch (start us, length us, event | category | flops | bytes accessed | tf_op | source)
XLA Modules:
  0.0 229.3 jit_solution(17297192792296423698)
XLA Ops:
  6.6 1.9 convert_reduce_fusion
  8.5 2.3 %fusion.2 = f32[64,64]{1,0:T(8,128)S(1)} fusion(bf16[64,64,128]{2,1,0:T(8,128)(2,1)} %param.11, f32[64,64]{1,0:T(8,128)S(1)} %broadcast_multiply_fusion), kind=kLoop, calls=%fused_computation.4 | loop fusion | flops 2093056 | bytes 1081344 | tf_op jit(solution)/shard_map/reduce_sum | solution.py:270
  10.9 1.3 fusion.5
  12.2 2.5 %fusion.6 = f32[64,64,4]{1,2,0:T(4,128)S(1)} fusion(bf16[64,64,128]{2,1,0:T(8,128)(2,1)S(1)} %fusion.5, f32[128,4]{0,1:T(4,128)S(1)} %copy-done), kind=kOutput, calls=%fused_computation.38 | convolution fusion | flops 25165824 | bytes 1116160 | tf_op jit(solution)/shard_map/bias/jkc,ch->hkj/dot_general | solution.py:365
  15.3 1.1 collective-permute-done.7
  16.6 0.7 collective-permute-start.8
  17.4 4.7 %collective-permute-start.2 = (bf16[16,64,128]{2,1,0:T(8,128)(2,1)S(1)}, bf16[16,64,128]{2,1,0:T(8,128)(2,1)S(1)}, u32[]{:S(2)}, u32[]{:S(2)}) collective-permute-start(bf16[16,64,128]{2,1,0:T(8,128)(2,1)S(1)} %get-tuple-element.26), channel_id=1, source_target_pairs={{0,3},{1,0},{2,1},{3,2},{4,7},{5,4},{6,5},{7,6},{8,11},{9,8},{10,9... | collective-permute-start | bytes 786440 | tf_op jit(solution)/shard_map/rows/ppermute | solution.py:322
  22.1 0.7 collective-permute-start
  22.8 4.4 %collective-permute-start.9 = (f32[32,128]{1,0:T(8,128)S(1)}, f32[32,128]{1,0:T(8,128)S(1)}, u32[]{:S(2)}, u32[]{:S(2)}) collective-permute-start(f32[32,128]{1,0:T(8,128)S(1)} %get-tuple-element.41), channel_id=1, source_target_pairs={{0,64},{1,65},{2,66},{3,67},{4,128},{5,129},{6,130},{7,131},{8,192... | collective-permute-start | bytes 49160 | tf_op jit(solution)/shard_map/bias/ppermute | solution.py:322
  27.2 1.2 collective-permute-start.10
  28.6 3.8 %collective-permute-start.11 = (f32[32,128]{1,0:T(8,128)S(1)}, f32[32,128]{1,0:T(8,128)S(1)}, u32[]{:S(2)}, u32[]{:S(2)}) collective-permute-start(f32[32,128]{1,0:T(8,128)S(1)} %get-tuple-element.39), channel_id=1, source_target_pairs={{0,192},{1,193},{2,194},{3,195},{4,0},{5,1},{6,2},{7,3},{8,64},{9,... | collective-permute-start | bytes 49160 | tf_op jit(solution)/shard_map/bias/ppermute | solution.py:322
  32.5 3.5 %collective-permute-done.11 = f32[32,128]{1,0:T(8,128)S(1)} collective-permute-done((f32[32,128]{1,0:T(8,128)S(1)}, f32[32,128]{1,0:T(8,128)S(1)}, u32[]{:S(2)}, u32[]{:S(2)}) %collective-permute-start.11) | collective-permute-done | bytes 16416 | tf_op jit(solution)/shard_map/bias/ppermute | solution.py:322
  36.0 0.6 constant_dynamic-slice_fusion
  36.6 7.6 %collective-permute-done.1 = bf16[16,64,128]{2,1,0:T(8,128)(2,1)S(1)} collective-permute-done((bf16[16,64,128]{2,1,0:T(8,128)(2,1)S(1)}, bf16[16,64,128]{2,1,0:T(8,128)(2,1)S(1)}, u32[]{:S(2)}, u32[]{:S(2)}) %collective-permute-start.1) | collective-permute-done | bytes 262176 | tf_op jit(solution)/shard_map/rows/ppermute | solution.py:322
  44.2 1.1 pad_maximum_fusion.rest_0_.x0
  45.4 1.0 broadcast_in_dim.6
  46.3 24.7 %all_to_all.5.bias_own = f32[8,128,128]{2,1,0:T(8,128)} all-to-all(f32[8,128,128]{2,1,0:T(8,128)S(1)} %broadcast_in_dim.6), channel_id=1, replica_groups=mesh['y'=4,'zh'=2,'core'=2,'x'=4,'zl'=4] {'zh','zl'}, dimensions={0} | all-to-all | bytes 1048576 | tf_op jit(solution)/shard_map/bias/all_to_all | solution.py:380
  71.0 3.9 %collective-permute-start.3 = (bf16[4,16,64,128]{3,2,1,0:T(8,128)(2,1)S(1)}, bf16[4,16,64,128]{3,2,1,0:T(8,128)(2,1)S(1)}, u32[]{:S(2)}, u32[]{:S(2)}) collective-permute-start(bf16[4,16,64,128]{3,2,1,0:T(8,128)(2,1)S(1)} %copy-done.1), channel_id=1, source_target_pairs={{0,4},{1,5},{2,6},{3,7},{4,8},{5,9},{6,10},{7,11},{8,12},{9,13},{1... | collective-permute-start | bytes 3145736 | tf_op jit(solution)/shard_map/rows/ppermute | solution.py:322
  75.0 20.5 %collective-permute-done.3.x1 = bf16[4,16,64,128]{3,2,1,0:T(8,128)(2,1)S(1)} collective-permute-done((bf16[4,16,64,128]{3,2,1,0:T(8,128)(2,1)S(1)}, bf16[4,16,64,128]{3,2,1,0:T(8,128)(2,1)S(1)}, u32[]{:S(2)}, u32[]{:S(2)}) %collective-permute-start.3) | collective-permute-done | bytes 1048608 | tf_op jit(solution)/shard_map/rows/ppermute | solution.py:322
  95.5 0.9 slice.40
  96.4 3.6 %collective-permute-start.4 = (bf16[4,8,64,128]{3,2,1,0:T(8,128)(2,1)}, bf16[4,8,64,128]{3,2,1,0:T(8,128)(2,1)S(1)}, u32[]{:S(2)}, u32[]{:S(2)}) collective-permute-start(bf16[4,8,64,128]{3,2,1,0:T(8,128)(2,1)} %slice.40), channel_id=1, source_target_pairs={{0,4},{1,5},{2,6},{3,7},{4,8},{5,9},{6,10},{7,11},{8,12},{9,13},{1... | collective-permute-start | bytes 1572872 | tf_op jit(solution)/shard_map/rows/ppermute | solution.py:322
  100.0 0.9 slice.41
  101.8 6.9 %collective-permute-done.4.array = bf16[4,8,64,128]{3,2,1,0:T(8,128)(2,1)S(1)} collective-permute-done((bf16[4,8,64,128]{3,2,1,0:T(8,128)(2,1)}, bf16[4,8,64,128]{3,2,1,0:T(8,128)(2,1)S(1)}, u32[]{:S(2)}, u32[]{:S(2)}) %collective-permute-start.4) | collective-permute-done | bytes 524320 | tf_op jit(solution)/shard_map/rows/ppermute | solution.py:322
  108.7 4.3 %collective-permute-done.6.rest_0_.x2 = bf16[4,8,64,128]{3,2,1,0:T(8,128)(2,1)S(1)} collective-permute-done((bf16[4,8,64,128]{3,2,1,0:T(8,128)(2,1)}, bf16[4,8,64,128]{3,2,1,0:T(8,128)(2,1)S(1)}, u32[]{:S(2)}, u32[]{:S(2)}) %collective-permute-start.6) | collective-permute-done | bytes 524320 | tf_op jit(solution)/shard_map/rows/ppermute | solution.py:322
  113.0 0.8 copy-done.3
  113.8 1.2 copy-done.6
  115.0 1.2 copy-done.10
  116.2 13.0 %project_own_head.2 = (bf16[8,1024,128]{2,1,0:T(8,128)(2,1)}, bf16[8,128,1024]{2,1,0:T(8,128)(2,1)}, bf16[8,128,256]{2,1,0:T(8,128)(2,1)S(1)}, f32[8,128,256]{2,1,0:T(8,128)S(1)}, f32[8,32,256]{2,1,0:T(8,128)S(1)}) custom-call(s32[4]{0:T(128)S(1)} %pad_add_fusion.at, bf16[4,16,64,128]{3,2,1,0:T(8,128)(2,1)S(1)} %copy-done.1, ...), custom_call_target="tpu_custom_call" | custom-call | flops 2400000000 | bytes 8388608 | tf_op jit(solution)/shard_map/attention/project_own_head/pallas_call | solution.py:213
  129.2 0.7 copy-done.7
  130.0 1.0 copy-done.20
  130.9 0.8 copy-done.22
  131.9 0.9 copy-done.4
  133.1 1.0 copy-done.14
  134.2 13.2 %project_own_head.3 = (bf16[8,1024,128]{2,1,0:T(8,128)(2,1)}, bf16[8,128,1024]{2,1,0:T(8,128)(2,1)}, bf16[8,128,256]{2,1,0:T(8,128)(2,1)S(1)}, f32[8,128,256]{2,1,0:T(8,128)S(1)}, f32[8,32,256]{2,1,0:T(8,128)S(1)}) custom-call(s32[4]{0:T(128)S(1)} %pad_add_fusion.at, bf16[4,16,64,128]{3,2,1,0:T(8,128)(2,1)S(1)} %copy-done.1, ...), custom_call_target="tpu_custom_call" | custom-call | flops 2400000000 | bytes 8388608 | tf_op jit(solution)/shard_map/attention/project_own_head/pallas_call | solution.py:213
  147.4 1.3 copy-done.38
  148.8 25.9 %other_heads.2 = bf16[4,8,64,128]{3,2,1,0:T(8,128)(2,1)S(1)} custom-call(s32[4]{0:T(128)S(1)} %pad_add_fusion.at, bf16[8,1024,128]{2,1,0:T(8,128)(2,1)S(1)} %copy-done.19, bf16[8,128,1024]{2,1,0:T(8,128)(2,1)} %get-tuple-element.16.value, bf16[8,128,256]{2,1,0:T(8,128)(2,1)S(1)} %copy-done.23, f32[8,128,256]{2,1,0:T(8,128)S(1)} %copy-done.21, ...), custom_call_target="tpu_custom_call" | custom-call | flops 2400000000 | bytes 8388608 | tf_op jit(solution)/shard_map/attention/other_heads/pallas_call | solution.py:213
  174.7 0.7 slice_bitcast_fusion.4
  175.4 1.7 collective-permute-start.14
  177.1 0.6 collective-permute-start.16
  177.7 26.0 %other_heads.3 = bf16[4,8,64,128]{3,2,1,0:T(8,128)(2,1)S(1)} custom-call(s32[4]{0:T(128)S(1)} %pad_add_fusion.at, bf16[8,1024,128]{2,1,0:T(8,128)(2,1)S(1)} %copy-done.18, bf16[8,128,1024]{2,1,0:T(8,128)(2,1)} %get-tuple-element.21.value, bf16[8,128,256]{2,1,0:T(8,128)(2,1)S(1)} %get-tuple-element.22.query, f32[8,128,256]{2,1,0:T(8,128)S(1)} %get-tuple-element.23.gate, ...), custom_call_target="tpu_custom_call" | custom-call | flops 2400000000 | bytes 8388608 | tf_op jit(solution)/shard_map/attention/other_heads/pallas_call | solution.py:213
  203.6 0.5 copy-done.12
  204.2 0.7 slice_bitcast_fusion
  204.9 3.3 %collective-permute-start.17 = (bf16[8,64,128]{2,1,0:T(8,128)(2,1)S(1)}, bf16[8,64,128]{2,1,0:T(8,128)(2,1)S(1)}, u32[]{:S(2)}, u32[]{:S(2)}) collective-permute-start(bf16[8,64,128]{2,1,0:T(8,128)(2,1)S(1)} %get-tuple-element.31), channel_id=1, source_target_pairs={{0,3},{1,0},{2,1},{3,2},{4,7},{5,4},{6,5},{7,6},{8,11},{9,8},{10,9... | collective-permute-start | bytes 393224 | tf_op jit(solution)/shard_map/update/ppermute | solution.py:322
  208.1 1.1 collective-permute-start.18
  209.6 2.5 %collective-permute-done.17.refs_5_ = bf16[8,64,128]{2,1,0:T(8,128)(2,1)S(1)} collective-permute-done((bf16[8,64,128]{2,1,0:T(8,128)(2,1)S(1)}, bf16[8,64,128]{2,1,0:T(8,128)(2,1)S(1)}, u32[]{:S(2)}, u32[]{:S(2)}) %collective-permute-start.17) | collective-permute-done | bytes 131104 | tf_op jit(solution)/shard_map/update/ppermute | solution.py:322
  212.1 7.3 %collective-permute-done.18.refs_6_ = bf16[8,64,128]{2,1,0:T(8,128)(2,1)S(1)} collective-permute-done((bf16[8,64,128]{2,1,0:T(8,128)(2,1)S(1)}, bf16[8,64,128]{2,1,0:T(8,128)(2,1)S(1)}, u32[]{:S(2)}, u32[]{:S(2)}) %collective-permute-start.18) | collective-permute-done | bytes 131104 | tf_op jit(solution)/shard_map/update/ppermute | solution.py:322
  219.4 0.6 copy-done.30
  220.1 2.3 %assemble_update.1 = bf16[64,64,128]{2,1,0:T(8,128)(2,1)} custom-call(s32[4]{0:T(128)} %copy-done.12, bf16[8,64,128]{2,1,0:T(8,128)(2,1)} %get-tuple-element.36.refs_0_, bf16[8,64,128]{2,1,0:T(8,128)(2,1)} %copy-done.26, bf16[8,64,128]{2,1,0:T(8,128)(2,1)} %copy-done.27, bf16[8,64,128]{2,1,0:T(8,128)(2,1)} %copy-done.28, ...), custom_call_target="tpu_custom_call" | custom-call | tf_op jit(solution)/shard_map/assemble_update/pallas_call | solution.py:284
  (113 shorter events, 2.8 us)
Async XLA Ops:
  6.5 5.7 %copy-start = (f32[128,4]{0,1:T(4,128)S(1)}, f32[128,4]{0,1:T(4,128)}, u32[]{:S(2)}) copy-start(f32[128,4]{0,1:T(4,128)} %param.19) | copy-start | bytes 6148
  6.5 4.4 %copy-start.24 = (bf16[64,64,128]{2,1,0:T(8,128)(2,1)S(1)}, bf16[64,64,128]{2,1,0:T(8,128)(2,1)}, u32[]{:S(2)}) copy-start(bf16[64,64,128]{2,1,0:T(8,128)(2,1)} %param.11) | copy-start | bytes 3145732
  6.5 4.4 %copy-start.36 = (f32[128]{0:T(128)S(1)}, f32[128]{0:T(128)}, u32[]{:S(2)}) copy-start(f32[128]{0:T(128)} %param.13) | copy-start | bytes 1540
  6.5 4.4 %copy-start.37 = (f32[128]{0:T(128)S(1)}, f32[128]{0:T(128)}, u32[]{:S(2)}) copy-start(f32[128]{0:T(128)} %param.12) | copy-start | bytes 1540
  6.5 125.2 %all-gather.3.cloned.1.call-start = ((), (), s32[]{:S(2)}) async-start(), calls=%async_computation.1 | async-start | bytes 2621440 | tf_op jit(solution)/shard_map/bias/all_gather | solution.py:388
  15.0 1.4 collective-permute-start.7
  16.6 10.5 %collective-permute-start.8 = (f32[32,128]{1,0:T(8,128)S(1)}, f32[32,128]{1,0:T(8,128)S(1)}, u32[]{:S(2)}, u32[]{:S(2)}) collective-permute-start(f32[32,128]{1,0:T(8,128)S(1)} %get-tuple-element.42), channel_id=1, source_target_pairs={{0,0},{1,1},{2,2},{3,3},{4,64},{5,65},{6,66},{7,67},{8,128},{9,129... | collective-permute-start | bytes 49160 | tf_op jit(solution)/shard_map/bias/ppermute | solution.py:322
  17.4 19.2 %collective-permute-start.2 = (bf16[16,64,128]{2,1,0:T(8,128)(2,1)S(1)}, bf16[16,64,128]{2,1,0:T(8,128)(2,1)S(1)}, u32[]{:S(2)}, u32[]{:S(2)}) collective-permute-start(bf16[16,64,128]{2,1,0:T(8,128)(2,1)S(1)} %get-tuple-element.26), channel_id=1, source_target_pairs={{0,3},{1,0},{2,1},{3,2},{4,7},{5,4},{6,5},{7,6},{8,11},{9,8},{10,9... | collective-permute-start | bytes 786440 | tf_op jit(solution)/shard_map/rows/ppermute | solution.py:322
  22.1 22.1 %collective-permute-start.1 = (bf16[16,64,128]{2,1,0:T(8,128)(2,1)S(1)}, bf16[16,64,128]{2,1,0:T(8,128)(2,1)S(1)}, u32[]{:S(2)}, u32[]{:S(2)}) collective-permute-start(bf16[16,64,128]{2,1,0:T(8,128)(2,1)S(1)} %get-tuple-element.27), channel_id=1, source_target_pairs={{0,2},{1,3},{2,0},{3,1},{4,6},{5,7},{6,4},{7,5},{8,10},{9,11},{10,... | collective-permute-start | bytes 786440 | tf_op jit(solution)/shard_map/rows/ppermute | solution.py:322
  22.1 22.1 %collective-permute-start = (bf16[16,64,128]{2,1,0:T(8,128)(2,1)S(1)}, bf16[16,64,128]{2,1,0:T(8,128)(2,1)S(1)}, u32[]{:S(2)}, u32[]{:S(2)}) collective-permute-start(bf16[16,64,128]{2,1,0:T(8,128)(2,1)S(1)} %get-tuple-element.28), channel_id=1, source_target_pairs={{0,1},{1,2},{2,3},{3,0},{4,5},{5,6},{6,7},{7,4},{8,9},{9,10},{10,1... | collective-permute-start | bytes 786440 | tf_op jit(solution)/shard_map/rows/ppermute | solution.py:322
  22.8 5.8 %collective-permute-start.9 = (f32[32,128]{1,0:T(8,128)S(1)}, f32[32,128]{1,0:T(8,128)S(1)}, u32[]{:S(2)}, u32[]{:S(2)}) collective-permute-start(f32[32,128]{1,0:T(8,128)S(1)} %get-tuple-element.41), channel_id=1, source_target_pairs={{0,64},{1,65},{2,66},{3,67},{4,128},{5,129},{6,130},{7,131},{8,192... | collective-permute-start | bytes 49160 | tf_op jit(solution)/shard_map/bias/ppermute | solution.py:322
  27.2 5.3 %collective-permute-start.10 = (f32[32,128]{1,0:T(8,128)S(1)}, f32[32,128]{1,0:T(8,128)S(1)}, u32[]{:S(2)}, u32[]{:S(2)}) collective-permute-start(f32[32,128]{1,0:T(8,128)S(1)} %get-tuple-element.40), channel_id=1, source_target_pairs={{0,128},{1,129},{2,130},{3,131},{4,192},{5,193},{6,194},{7,195},{8... | collective-permute-start | bytes 49160 | tf_op jit(solution)/shard_map/bias/ppermute | solution.py:322
  28.6 7.4 %collective-permute-start.11 = (f32[32,128]{1,0:T(8,128)S(1)}, f32[32,128]{1,0:T(8,128)S(1)}, u32[]{:S(2)}, u32[]{:S(2)}) collective-permute-start(f32[32,128]{1,0:T(8,128)S(1)} %get-tuple-element.39), channel_id=1, source_target_pairs={{0,192},{1,193},{2,194},{3,195},{4,0},{5,1},{6,2},{7,3},{8,64},{9,... | collective-permute-start | bytes 49160 | tf_op jit(solution)/shard_map/bias/ppermute | solution.py:322
  45.3 25.7 %copy-start.1 = (bf16[4,16,64,128]{3,2,1,0:T(8,128)(2,1)S(1)}, bf16[4,16,64,128]{3,2,1,0:T(8,128)(2,1)}, u32[]{:S(2)}) copy-start(bf16[4,16,64,128]{3,2,1,0:T(8,128)(2,1)} %pad_maximum_fusion.rest_0_.x0) | copy-start | bytes 3145732
  45.3 55.9 %copy-start.32 = (bf16[128,128]{1,0:T(8,128)(2,1)S(1)}, bf16[128,128]{1,0:T(8,128)(2,1)}, u32[]{:S(2)}) copy-start(bf16[128,128]{1,0:T(8,128)(2,1)} %param.16) | copy-start | bytes 98308
  45.3 56.1 %copy-start.33 = (bf16[128,128]{1,0:T(8,128)(2,1)S(1)}, bf16[128,128]{1,0:T(8,128)(2,1)}, u32[]{:S(2)}) copy-start(bf16[128,128]{1,0:T(8,128)(2,1)} %param.14) | copy-start | bytes 98308
  45.3 56.2 %copy-start.34 = (bf16[128,128]{1,0:T(8,128)(2,1)S(1)}, bf16[128,128]{1,0:T(8,128)(2,1)}, u32[]{:S(2)}) copy-start(bf16[128,128]{1,0:T(8,128)(2,1)} %param.17) | copy-start | bytes 98308
  45.3 56.3 %copy-start.35 = (f32[128]{0:T(128)S(1)}, f32[128]{0:T(128)}, u32[]{:S(2)}) copy-start(f32[128]{0:T(128)} %param.18) | copy-start | bytes 1540
  71.0 30.2 %copy-start.2 = (f32[8,128,128]{2,1,0:T(8,128)S(1)}, f32[8,128,128]{2,1,0:T(8,128)}, u32[]{:S(2)}) copy-start(f32[8,128,128]{2,1,0:T(8,128)} %all_to_all.5.bias_own) | copy-start | bytes 1572868
  71.0 42.8 %copy-start.15 = (bf16[128,128]{1,0:T(8,128)(2,1)S(1)}, bf16[128,128]{1,0:T(8,128)(2,1)}, u32[]{:S(2)}) copy-start(bf16[128,128]{1,0:T(8,128)(2,1)} %w_key.3) | copy-start | bytes 98308
  71.0 24.4 %collective-permute-start.3 = (bf16[4,16,64,128]{3,2,1,0:T(8,128)(2,1)S(1)}, bf16[4,16,64,128]{3,2,1,0:T(8,128)(2,1)S(1)}, u32[]{:S(2)}, u32[]{:S(2)}) collective-permute-start(bf16[4,16,64,128]{3,2,1,0:T(8,128)(2,1)S(1)} %copy-done.1), channel_id=1, source_target_pairs={{0,4},{1,5},{2,6},{3,7},{4,8},{5,9},{6,10},{7,11},{8,12},{9,13},{1... | collective-permute-start | bytes 3145736 | tf_op jit(solution)/shard_map/rows/ppermute | solution.py:322
  75.0 25.0 %collective-permute-start.5 = (bf16[4,16,64,128]{3,2,1,0:T(8,128)(2,1)S(1)}, bf16[4,16,64,128]{3,2,1,0:T(8,128)(2,1)S(1)}, u32[]{:S(2)}, u32[]{:S(2)}) collective-permute-start(bf16[4,16,64,128]{3,2,1,0:T(8,128)(2,1)S(1)} %copy-done.1), channel_id=1, source_target_pairs={{0,12},{1,13},{2,14},{3,15},{4,0},{5,1},{6,2},{7,3},{8,4},{9,5},{1... | collective-permute-start | bytes 3145736 | tf_op jit(solution)/shard_map/rows/ppermute | solution.py:322
  95.5 5.5 %copy-start.9 = (bf16[4,16,64,128]{3,2,1,0:T(8,128)(2,1)}, bf16[4,16,64,128]{3,2,1,0:T(8,128)(2,1)S(1)}, u32[]{:S(2)}) copy-start(bf16[4,16,64,128]{3,2,1,0:T(8,128)(2,1)S(1)} %collective-permute-done.3.x1) | copy-start | bytes 3145732
  96.4 12.3 %collective-permute-start.4 = (bf16[4,8,64,128]{3,2,1,0:T(8,128)(2,1)}, bf16[4,8,64,128]{3,2,1,0:T(8,128)(2,1)S(1)}, u32[]{:S(2)}, u32[]{:S(2)}) collective-permute-start(bf16[4,8,64,128]{3,2,1,0:T(8,128)(2,1)} %slice.40), channel_id=1, source_target_pairs={{0,4},{1,5},{2,6},{3,7},{4,8},{5,9},{6,10},{7,11},{8,12},{9,13},{1... | collective-permute-start | bytes 1572872 | tf_op jit(solution)/shard_map/rows/ppermute | solution.py:322
  101.0 12.0 %collective-permute-start.6 = (bf16[4,8,64,128]{3,2,1,0:T(8,128)(2,1)}, bf16[4,8,64,128]{3,2,1,0:T(8,128)(2,1)S(1)}, u32[]{:S(2)}, u32[]{:S(2)}) collective-permute-start(bf16[4,8,64,128]{3,2,1,0:T(8,128)(2,1)} %slice.41), channel_id=1, source_target_pairs={{0,12},{1,13},{2,14},{3,15},{4,0},{5,1},{6,2},{7,3},{8,4},{9,5},{1... | collective-permute-start | bytes 1572872 | tf_op jit(solution)/shard_map/rows/ppermute | solution.py:322
  101.2 12.6 %collective-permute-start.12 = (f32[8,128,128]{2,1,0:T(8,128)S(1)}, f32[8,128,128]{2,1,0:T(8,128)S(1)}, u32[]{:S(2)}, u32[]{:S(2)}) collective-permute-start(f32[8,128,128]{2,1,0:T(8,128)S(1)} %copy-done.2), channel_id=1, source_target_pairs={{0,16},{1,17},{2,18},{3,19},{4,20},{5,21},{6,22},{7,23},{8,24},{9,... | collective-permute-start | bytes 1572872 | tf_op jit(solution)/shard_map/bias/ppermute | solution.py:322
  108.7 4.3 %copy-start.5 = (bf16[4,8,64,128]{3,2,1,0:T(8,128)(2,1)}, bf16[4,8,64,128]{3,2,1,0:T(8,128)(2,1)S(1)}, u32[]{:S(2)}) copy-start(bf16[4,8,64,128]{3,2,1,0:T(8,128)(2,1)S(1)} %collective-permute-done.4.array) | copy-start | bytes 1572868
  113.8 15.5 %copy-start.13 = (f32[8,128,128]{2,1,0:T(8,128)}, f32[8,128,128]{2,1,0:T(8,128)S(1)}, u32[]{:S(2)}) copy-start(f32[8,128,128]{2,1,0:T(8,128)S(1)} %collective-permute-done.12.bias_other) | copy-start | bytes 1572868
  131.7 1.4 copy-start.11
  131.7 17.0 %copy-start.8 = (f32[8,32,256]{2,1,0:T(8,128)S(1)}, f32[8,32,256]{2,1,0:T(8,128)}, u32[]{:S(2)}) copy-start(f32[8,32,256]{2,1,0:T(8,128)} %copy-done.7) | copy-start | bytes 786436
  131.8 15.7 %collective-permute-start.13 = (f32[4,8,128,128]{3,2,1,0:T(8,128)}, f32[4,8,128,128]{3,2,1,0:T(8,128)S(1)}, u32[]{:S(2)}, u32[]{:S(2)}) collective-permute-start(f32[4,8,128,128]{3,2,1,0:T(8,128)} %tie.5.bias_own), channel_id=1, source_target_pairs={{0,16},{1,17},{2,18},{3,19},{4,20},{5,21},{6,22},{7,23},{8,24},{9,... | collective-permute-start | bytes 6291464 | tf_op jit(solution)/shard_map/bias/ppermute | solution.py:322
  134.2 14.6 %copy-start.16 = (bf16[128,128]{1,0:T(8,128)(2,1)S(1)}, bf16[128,128]{1,0:T(8,128)(2,1)}, u32[]{:S(2)}) copy-start(bf16[128,128]{1,0:T(8,128)(2,1)} %w_out.3) | copy-start | bytes 98308
  134.2 14.6 %copy-start.17 = (f32[128]{0:T(128)S(1)}, f32[128]{0:T(128)}, u32[]{:S(2)}) copy-start(f32[128]{0:T(128)} %param.21) | copy-start | bytes 1540
  134.2 14.6 %copy-start.19 = (bf16[8,1024,128]{2,1,0:T(8,128)(2,1)S(1)}, bf16[8,1024,128]{2,1,0:T(8,128)(2,1)}, u32[]{:S(2)}) copy-start(bf16[8,1024,128]{2,1,0:T(8,128)(2,1)} %get-tuple-element.15.key) | copy-start | bytes 6291460
  134.2 14.6 %copy-start.21 = (f32[8,128,256]{2,1,0:T(8,128)S(1)}, f32[8,128,256]{2,1,0:T(8,128)}, u32[]{:S(2)}) copy-start(f32[8,128,256]{2,1,0:T(8,128)} %copy-done.20) | copy-start | bytes 3145732
  134.2 14.6 %copy-start.23 = (bf16[8,128,256]{2,1,0:T(8,128)(2,1)S(1)}, bf16[8,128,256]{2,1,0:T(8,128)(2,1)}, u32[]{:S(2)}) copy-start(bf16[8,128,256]{2,1,0:T(8,128)(2,1)} %copy-done.22) | copy-start | bytes 1572868
  147.4 1.3 copy-start.38
  148.8 28.9 %copy-start.18 = (bf16[8,1024,128]{2,1,0:T(8,128)(2,1)S(1)}, bf16[8,1024,128]{2,1,0:T(8,128)(2,1)}, u32[]{:S(2)}) copy-start(bf16[8,1024,128]{2,1,0:T(8,128)(2,1)} %get-tuple-element.20.key) | copy-start | bytes 6291460
  175.4 33.9 %collective-permute-start.14 = (bf16[8,64,128]{2,1,0:T(8,128)(2,1)S(1)}, bf16[8,64,128]{2,1,0:T(8,128)(2,1)S(1)}, u32[]{:S(2)}, u32[]{:S(2)}) collective-permute-start(bf16[8,64,128]{2,1,0:T(8,128)(2,1)S(1)} %get-tuple-element.35), channel_id=1, source_target_pairs={{0,3},{1,0},{2,1},{3,2},{4,7},{5,4},{6,5},{7,6},{8,11},{9,8},{10,9... | collective-permute-start | bytes 393224 | tf_op jit(solution)/shard_map/update/ppermute | solution.py:322
  177.1 32.5 %collective-permute-start.15 = (bf16[8,64,128]{2,1,0:T(8,128)(2,1)S(1)}, bf16[8,64,128]{2,1,0:T(8,128)(2,1)S(1)}, u32[]{:S(2)}, u32[]{:S(2)}) collective-permute-start(bf16[8,64,128]{2,1,0:T(8,128)(2,1)S(1)} %get-tuple-element.34), channel_id=1, source_target_pairs={{0,2},{1,3},{2,0},{3,1},{4,6},{5,7},{6,4},{7,5},{8,10},{9,11},{10,... | collective-permute-start | bytes 393224 | tf_op jit(solution)/shard_map/update/ppermute | solution.py:322
  177.1 32.5 %collective-permute-start.16 = (bf16[8,64,128]{2,1,0:T(8,128)(2,1)S(1)}, bf16[8,64,128]{2,1,0:T(8,128)(2,1)S(1)}, u32[]{:S(2)}, u32[]{:S(2)}) collective-permute-start(bf16[8,64,128]{2,1,0:T(8,128)(2,1)S(1)} %get-tuple-element.33), channel_id=1, source_target_pairs={{0,1},{1,2},{2,3},{3,0},{4,5},{5,6},{6,7},{7,4},{8,9},{9,10},{10,1... | collective-permute-start | bytes 393224 | tf_op jit(solution)/shard_map/update/ppermute | solution.py:322
  204.9 7.2 %collective-permute-start.17 = (bf16[8,64,128]{2,1,0:T(8,128)(2,1)S(1)}, bf16[8,64,128]{2,1,0:T(8,128)(2,1)S(1)}, u32[]{:S(2)}, u32[]{:S(2)}) collective-permute-start(bf16[8,64,128]{2,1,0:T(8,128)(2,1)S(1)} %get-tuple-element.31), channel_id=1, source_target_pairs={{0,3},{1,0},{2,1},{3,2},{4,7},{5,4},{6,5},{7,6},{8,11},{9,8},{10,9... | collective-permute-start | bytes 393224 | tf_op jit(solution)/shard_map/update/ppermute | solution.py:322
  208.1 11.3 %collective-permute-start.18 = (bf16[8,64,128]{2,1,0:T(8,128)(2,1)S(1)}, bf16[8,64,128]{2,1,0:T(8,128)(2,1)S(1)}, u32[]{:S(2)}, u32[]{:S(2)}) collective-permute-start(bf16[8,64,128]{2,1,0:T(8,128)(2,1)S(1)} %get-tuple-element.30), channel_id=1, source_target_pairs={{0,2},{1,3},{2,0},{3,1},{4,6},{5,7},{6,4},{7,5},{8,10},{9,11},{10,... | collective-permute-start | bytes 393224 | tf_op jit(solution)/shard_map/update/ppermute | solution.py:322
  209.2 10.2 %copy-start.26 = (bf16[8,64,128]{2,1,0:T(8,128)(2,1)}, bf16[8,64,128]{2,1,0:T(8,128)(2,1)S(1)}, u32[]{:S(2)}) copy-start(bf16[8,64,128]{2,1,0:T(8,128)(2,1)S(1)} %collective-permute-done.14.refs_1_) | copy-start | bytes 393220
  209.2 10.2 %collective-permute-start.19 = (bf16[8,64,128]{2,1,0:T(8,128)(2,1)S(1)}, bf16[8,64,128]{2,1,0:T(8,128)(2,1)S(1)}, u32[]{:S(2)}, u32[]{:S(2)}) collective-permute-start(bf16[8,64,128]{2,1,0:T(8,128)(2,1)S(1)} %get-tuple-element.29), channel_id=1, source_target_pairs={{0,1},{1,2},{2,3},{3,0},{4,5},{5,6},{6,7},{7,4},{8,9},{9,10},{10,1... | collective-permute-start | bytes 393224 | tf_op jit(solution)/shard_map/update/ppermute | solution.py:322
  209.6 9.9 %copy-start.27 = (bf16[8,64,128]{2,1,0:T(8,128)(2,1)}, bf16[8,64,128]{2,1,0:T(8,128)(2,1)S(1)}, u32[]{:S(2)}) copy-start(bf16[8,64,128]{2,1,0:T(8,128)(2,1)S(1)} %collective-permute-done.15.refs_2_) | copy-start | bytes 393220
  209.6 9.9 %copy-start.28 = (bf16[8,64,128]{2,1,0:T(8,128)(2,1)}, bf16[8,64,128]{2,1,0:T(8,128)(2,1)S(1)}, u32[]{:S(2)}) copy-start(bf16[8,64,128]{2,1,0:T(8,128)(2,1)S(1)} %collective-permute-done.16.refs_3_) | copy-start | bytes 393220
  212.1 7.4 %copy-start.29 = (bf16[8,64,128]{2,1,0:T(8,128)(2,1)}, bf16[8,64,128]{2,1,0:T(8,128)(2,1)S(1)}, u32[]{:S(2)}) copy-start(bf16[8,64,128]{2,1,0:T(8,128)(2,1)S(1)} %collective-permute-done.17.refs_5_) | copy-start | bytes 393220
  (12 other events, 10.9 us)
Sparse Core Ops, SparseCore 0:
  71.1 29.7 all-gather.2
